TPU v7x, 32 devices: a whole 2x2x4 slice. The times are simulated.
32 devices in a mesh: dp: 4 (over z), expert: 8 (over y, x, core).
Axes of the slice: x: 2, y: 2, z: 4, core: 2. Of those that a mesh axis runs over, the one named last changes fastest.
Arguments:
- tokens: bfloat16 [512, 64, 512], P(('dp', 'expert')), may hold values from -8 to 8
- lengths: int32 [512], P(('dp', 'expert')), may hold values from 16 to 64
- tasks: int32 [512], P(('dp', 'expert')), may hold values from 0 to 29
- routes: int32 [30, 2], replicated, may hold values from 0 to 7, all different within a row
- gate_table: float32 [30, 8], replicated, may hold values from -4 to 4
- ln1_gain: float32 [512], replicated, may hold values from 0.1 to 1.9
- ln1_bias: float32 [512], replicated, may hold values from -1.5 to 1.5
- ln2_gain: float32 [512], replicated, may hold values from 0.1 to 1.9
- ln2_bias: float32 [512], replicated, may hold values from -1.5 to 1.5
- w_query: bfloat16 [512, 512], replicated, may hold values from -0.25 to 0.25
- w_key: bfloat16 [512, 512], replicated, may hold values from -0.25 to 0.25
- w_value: bfloat16 [512, 512], replicated, may hold values from -0.25 to 0.25
- w_out: bfloat16 [512, 512], replicated, may hold values from -1 to 1
- w_in: bfloat16 [8, 512, 2048], P('expert'), may hold values from -0.25 to 0.25
- w_back: bfloat16 [8, 2048, 512], P('expert'), may hold values from -0.1875 to 0.1875
- cotangent: bfloat16 [512, 64, 512], P(('dp', 'expert')), may hold values from -6 to 6
Outputs:
- output: bfloat16 [512, 64, 512], P(('dp', 'expert'))
- input_grad: bfloat16 [512, 64, 512], P(('dp', 'expert'))
- gate_grad: float32 [30, 8], replicated
- ln1_gain_grad: float32 [512], replicated
- ln1_bias_grad: float32 [512], replicated
- ln2_gain_grad: float32 [512], replicated
- ln2_bias_grad: float32 [512], replicated
- query_grad: float32 [512, 512], replicated
- key_grad: float32 [512, 512], replicated
- value_grad: float32 [512, 512], replicated
- out_grad: float32 [512, 512], replicated
- in_grad: float32 [8, 512, 2048], P('expert', 'dp')
- back_grad: float32 [8, 2048, 512], P('expert', 'dp')
- rms: float32 [3], replicated
Inputs may be any that keep to these rules, and one draw needn't show every extreme that they name: `routes`: each task names two different experts; every expert is named by some task.
All inputs are finite; a program needn't handle non-finite values.
Results may differ from a plain program's by a relative error of at most 0.012.
The roundings to bfloat16 on the way count: a program that leaves them out, or rounds other values in their place, can miss the bound.
Values may be sent and summed in bfloat16 or wider, within the bound.
A program may use at most 192 MiB of HBM per device.

v0:
```python
import jax
import jax.numpy as jnp
from jax import lax
from jax.sharding import PartitionSpec as P

HEADS = 8


def normalize(value):
    centered = value - jnp.mean(value, axis=-1, keepdims=True)
    variance = jnp.mean(centered * centered, axis=-1, keepdims=True)
    inverse = lax.rsqrt(variance + 1e-05)
    return (centered * inverse, inverse)


def norm_backward(grad, normed, inverse, gain):
    scaled = grad * gain
    inner = scaled - jnp.mean(scaled, axis=-1, keepdims=True)
    inner = inner - normed * jnp.mean(scaled * normed, axis=-1, keepdims=True)
    return (inverse * inner, jnp.sum(grad * normed, axis=(0, 1)), jnp.sum(grad, axis=(0, 1)))


def project(left, right):
    return jnp.dot(left, right, preferred_element_type=jnp.float32)


def expert_forward(incoming, first, second):
    pre_act = project(incoming, first)
    active = jax.nn.gelu(pre_act).astype(jnp.bfloat16)
    produced = project(active, second).astype(jnp.bfloat16)
    return (pre_act, active, produced)


def expert_backward(incoming, pre_act, active, grad_in, first, second):
    dactive = project(grad_in, second.T)
    back_local = project(active.T, grad_in)
    gelu_pull = jax.vjp(jax.nn.gelu, pre_act)[1]
    dpre = gelu_pull(dactive)[0].astype(jnp.bfloat16)
    in_local = project(incoming.T, dpre)
    dincoming = project(dpre, first.T).astype(jnp.bfloat16)
    return (in_local, back_local, dincoming)


def local(
    tokens,
    lengths,
    tasks,
    routes,
    gate_table,
    ln1_gain,
    ln1_bias,
    ln2_gain,
    ln2_bias,
    w_query,
    w_key,
    w_value,
    w_out,
    w_in,
    w_back,
    cotangent,
):
    sents, slot, width = tokens.shape
    heads = HEADS
    head = width // heads
    experts = gate_table.shape[1]
    ntasks = routes.shape[0]
    capacity = max(1, 4 * sents // experts)
    scale = 1.0 / jnp.sqrt(jnp.float32(head))
    task_hot = (tasks[:, None] == jnp.arange(ntasks)[None, :]).astype(jnp.int32)
    chosen = jnp.sum(task_hot[:, :, None] * routes[None, :, :], axis=1)
    flat = chosen.reshape(-1)
    order = jnp.arange(2 * sents)
    earlier = (flat[:, None] == flat[None, :]) & (order[None, :] < order[:, None])
    rank = jnp.sum(earlier.astype(jnp.int32), axis=1)
    slot_id = flat * capacity + rank
    placed = rank < capacity
    dispatch = (
        (jnp.arange(experts * capacity)[:, None] == slot_id[None, :]) & placed[None, :]
    ).astype(jnp.bfloat16)
    collect = dispatch.T
    expert_hot = (chosen[:, :, None] == jnp.arange(experts)[None, None, :]).astype(jnp.float32)
    valid = (jnp.arange(slot)[None, :] < lengths[:, None]).astype(jnp.float32)
    keymask = valid[:, None, None, :] > 0.5
    mask3 = valid[:, :, None]
    xfull = tokens.astype(jnp.float32)
    normed1, inverse1 = normalize(xfull)
    act = (normed1 * ln1_gain + ln1_bias).astype(jnp.bfloat16).reshape(-1, width)
    query = project(act, w_query).astype(jnp.bfloat16).reshape(sents, slot, heads, head)
    keyed = project(act, w_key).astype(jnp.bfloat16).reshape(sents, slot, heads, head)
    valued = project(act, w_value).astype(jnp.bfloat16).reshape(sents, slot, heads, head)

    def scores_of(qpart, kpart):
        raw = (
            jnp.einsum("sqhd,skhd->shqk", qpart, kpart, preferred_element_type=jnp.float32) * scale
        )
        return jnp.where(keymask, raw, -1000000000.0)

    scores = scores_of(query, keyed)
    peak = jnp.max(scores, axis=-1, keepdims=True)
    logsum = peak + jnp.log(jnp.sum(jnp.exp(scores - peak), axis=-1, keepdims=True))
    prob_low = jnp.exp(scores - logsum).astype(jnp.bfloat16)
    context = jnp.einsum("shqk,skhd->sqhd", prob_low, valued, preferred_element_type=jnp.float32)
    context = context.astype(jnp.bfloat16).reshape(-1, width)
    attention_block = project(context, w_out).reshape(sents, slot, width)
    hidden_res = xfull + attention_block
    normed2, inverse2 = normalize(hidden_res)
    mixed = (normed2 * ln2_gain + ln2_bias).astype(jnp.bfloat16)
    table_rows = jnp.dot(task_hot.astype(jnp.float32), gate_table, precision=lax.Precision.HIGHEST)
    picked = jnp.sum(expert_hot * table_rows[:, None, :], axis=-1)
    gate_values = jax.nn.softmax(picked, axis=-1)
    grad_total = cotangent.astype(jnp.float32) * mask3
    copies = jnp.broadcast_to(mixed[:, None], (sents, 2, slot, width)).reshape(
        2 * sents, slot * width
    )
    outgoing = (
        project(dispatch, copies).astype(jnp.bfloat16).reshape(experts, capacity, slot, width)
    )
    dycopy = (
        (gate_values[:, :, None, None] * grad_total[:, None])
        .astype(jnp.bfloat16)
        .reshape(2 * sents, slot * width)
    )
    grad_out = (
        project(dispatch, dycopy).astype(jnp.bfloat16).reshape(experts, capacity, slot, width)
    )
    incoming = lax.all_to_all(outgoing, "expert", split_axis=0, concat_axis=0, tiled=True).reshape(
        -1, width
    )
    pre_act, active, produced = expert_forward(incoming, w_in[0], w_back[0])
    returned = lax.all_to_all(
        produced.reshape(experts, capacity, slot, width),
        "expert",
        split_axis=0,
        concat_axis=0,
        tiled=True,
    )
    grad_in = lax.all_to_all(grad_out, "expert", split_axis=0, concat_axis=0, tiled=True).reshape(
        -1, width
    )
    in_local, back_local, dincoming = expert_backward(
        incoming, pre_act, active, grad_in, w_in[0], w_back[0]
    )
    grad_back = lax.all_to_all(
        dincoming.reshape(experts, capacity, slot, width),
        "expert",
        split_axis=0,
        concat_axis=0,
        tiled=True,
    )
    ycopy = project(collect, returned.reshape(experts * capacity, slot * width)).reshape(
        sents, 2, slot, width
    )
    expert_mixture = jnp.sum(gate_values[:, :, None, None] * ycopy, axis=1)
    total = mask3 * (hidden_res + expert_mixture)
    output = total.astype(jnp.bfloat16)
    stats_local = jnp.stack(
        [
            jnp.sum(total * total),
            jnp.sum(mask3 * attention_block * attention_block),
            jnp.sum(mask3 * expert_mixture * expert_mixture),
            jnp.sum(valid),
        ]
    )
    stat_totals = lax.psum(stats_local, ("dp", "expert"))
    gate_dot = jnp.sum(ycopy * grad_total[:, None], axis=(2, 3))
    dpicked = gate_values * (gate_dot - jnp.sum(gate_values * gate_dot, axis=-1, keepdims=True))
    dlogits = jnp.sum(expert_hot * dpicked[:, :, None], axis=1)
    table_grad = jnp.dot(task_hot.T.astype(jnp.float32), dlogits, precision=lax.Precision.HIGHEST)
    dmixed = project(collect, grad_back.reshape(experts * capacity, slot * width)).reshape(
        sents, 2, slot, width
    )
    dmixed = jnp.sum(dmixed, axis=1)
    dres2, gain2_grad, bias2_grad = norm_backward(dmixed, normed2, inverse2, ln2_gain)
    dhidden = grad_total + dres2
    dattn = dhidden.astype(jnp.bfloat16).reshape(-1, width)
    wout_grad = project(context.T, dattn)
    dcontext = project(dattn, w_out.T).astype(jnp.bfloat16).reshape(sents, slot, heads, head)
    again = jnp.exp(scores_of(query, keyed) - logsum)
    dprob = jnp.einsum("sqhd,skhd->shqk", dcontext, valued, preferred_element_type=jnp.float32)
    dscores = (again * (dprob - jnp.sum(dprob * again, axis=-1, keepdims=True))).astype(
        jnp.bfloat16
    )
    dquery = (
        jnp.einsum("shqk,skhd->sqhd", dscores, keyed, preferred_element_type=jnp.float32) * scale
    )
    dkeyed = (
        jnp.einsum("shqk,sqhd->skhd", dscores, query, preferred_element_type=jnp.float32) * scale
    )
    dvalued = jnp.einsum("shqk,sqhd->skhd", prob_low, dcontext, preferred_element_type=jnp.float32)
    dquery = dquery.astype(jnp.bfloat16).reshape(-1, width)
    dkeyed = dkeyed.astype(jnp.bfloat16).reshape(-1, width)
    dvalued = dvalued.astype(jnp.bfloat16).reshape(-1, width)
    wq_grad = project(act.T, dquery)
    wk_grad = project(act.T, dkeyed)
    wv_grad = project(act.T, dvalued)
    dact = project(dquery, w_query.T) + project(dkeyed, w_key.T) + project(dvalued, w_value.T)
    dres1, gain1_grad, bias1_grad = norm_backward(
        dact.reshape(sents, slot, width), normed1, inverse1, ln1_gain
    )
    input_grad = (dhidden + dres1).astype(jnp.bfloat16)
    members = (
        wq_grad,
        wk_grad,
        wv_grad,
        wout_grad,
        gain1_grad,
        bias1_grad,
        gain2_grad,
        bias2_grad,
        table_grad,
    )
    members = members + ()
    summed = lax.psum(members, ("dp", "expert"))
    rms = jnp.sqrt(stat_totals[0:3] / (stat_totals[3] * width))
    in_share, back_share = (
        lax.psum_scatter(
            in_local.astype(jnp.bfloat16), "dp", scatter_dimension=0, tiled=True
        ).astype(jnp.float32),
        lax.psum_scatter(
            back_local.astype(jnp.bfloat16), "dp", scatter_dimension=0, tiled=True
        ).astype(jnp.float32),
    )
    return (
        output,
        input_grad,
        summed[8],
        summed[4],
        summed[5],
        summed[6],
        summed[7],
        summed[0],
        summed[1],
        summed[2],
        summed[3],
        in_share[None],
        back_share[None],
        rms,
    )


def solution(mesh):
    in_specs = (
        P(("dp", "expert"), None, None),
        P(("dp", "expert")),
        P(("dp", "expert")),
        P(),
        P(),
        P(),
        P(),
        P(),
        P(),
        P(),
        P(),
        P(),
        P(),
        P("expert", None, None),
        P("expert", None, None),
        P(("dp", "expert"), None, None),
    )
    out_specs = (
        P(("dp", "expert"), None, None),
        P(("dp", "expert"), None, None),
        P(),
        P(),
        P(),
        P(),
        P(),
        P(),
        P(),
        P(),
        P(),
        P("expert", "dp", None),
        P("expert", "dp", None),
        P(),
    )
    return jax.shard_map(local, mesh=mesh, in_specs=in_specs, out_specs=out_specs, check_vma=False)
```

profile of v0, /device:TPU:0, one launch (start us, length us, event | category | flops | bytes accessed | tf_op | source)
XLA Modules:
  0.0 561.8 jit_solution(3173582061777527130)
XLA Ops:
  11.7 1.7 fusion.27
  15.1 1.7 convolution_convert_fusion.8
  16.7 3.9 reshape.369
  20.6 4.2 copy.136
  24.8 3.0 convolution_convert_fusion.9
  27.8 3.9 reshape.368
  31.7 4.1 copy.140
  35.8 3.0 convolution_convert_fusion.10
  38.9 3.9 reshape.367
  42.8 3.8 fusion.11
  49.7 2.2 convolution_convert_fusion.6
  52.0 2.1 fusion.83
  59.1 3.5 copy.125
  62.6 5.3 all-to-all-start
  70.9 2.4 copy.164
  74.7 3.6 copy.131
  78.3 38.8 %all-to-all-done = bf16[8,8,64,512]{3,2,1,0:T(8,128)(2,1)} async-done(((bf16[8,8,64,512]{3,2,1,0:T(8,128)(2,1)}), bf16[8,8,64,512]{3,2,1,0:T(8,128)(2,1)}, u32[]{:S(2)}, u32[]{:S(2)}) %all-to-all-start) | async-done | bytes 4194336 | tf_op jit(solution)/shard_map/all_to_all | solution.py:126
  117.1 4.8 all-to-all-start.2
  121.9 23.3 %multiply_convert_fusion = (bf16[4096,2048]{1,0:T(8,128)(2,1)}, f32[4096,2048]{1,0:T(8,128)}) fusion(bf16[4096,512]{1,0:T(8,128)(2,1)} %bitcast.8, bf16[1,512,2048]{2,1,0:T(8,128)(2,1)S(1)} %copy-done), kind=kOutput, calls=%fused_computation.11 | convolution fusion | flops 8665432064 | bytes 56623104 | tf_op jit(solution)/shard_map/dot_general | solution.py:24
  145.2 25.8 %all-to-all-done.2 = bf16[8,8,64,512]{3,2,1,0:T(8,128)(2,1)} async-done(((bf16[8,8,64,512]{3,2,1,0:T(8,128)(2,1)}), bf16[8,8,64,512]{3,2,1,0:T(8,128)(2,1)}, u32[]{:S(2)}, u32[]{:S(2)}) %all-to-all-start.2) | async-done | bytes 4194336 | tf_op jit(solution)/shard_map/all_to_all | solution.py:137
  171.0 31.9 %fusion.6 = bf16[4096,2048]{1,0:T(8,128)(2,1)} fusion(f32[4096,2048]{1,0:T(8,128)} %get-tuple-element.50, bf16[4096,512]{1,0:T(8,128)(2,1)} %bitcast.16, bf16[1,2048,512]{2,1,0:T(8,128)(2,1)} %param.30), kind=kOutput, calls=%fused_computation.10 | convolution fusion | flops 8757706752 | bytes 56623104 | tf_op jit(solution)/shard_map/dot_general | solution.py:24
  202.9 14.2 %convolution_convert_fusion.2 = bf16[4096,512]{1,0:T(8,128)(2,1)} fusion(bf16[4096,2048]{1,0:T(8,128)(2,1)} %fusion.6, bf16[1,512,2048]{2,1,0:T(8,128)(2,1)S(1)} %copy-done), kind=kOutput, calls=%fused_computation.12 | convolution fusion | flops 8592031744 | bytes 23068672 | tf_op jit(solution)/shard_map/dot_general | solution.py:24
  217.1 4.5 all-to-all-start.3
  221.7 14.6 %convolution_convert_fusion.4 = bf16[2048,512]{1,0:T(8,128)(2,1)} fusion(bf16[4096,2048]{1,0:T(8,128)(2,1)} %get-tuple-element.49, bf16[4096,512]{1,0:T(8,128)(2,1)} %bitcast.16), kind=kOutput, calls=%fused_computation.36 | convolution fusion | flops 8590983168 | bytes 23068672 | tf_op jit(solution)/shard_map/dot_general | solution.py:24
  236.4 1.6 copy-done.68
  237.9 13.8 %convolution_convert_fusion.3 = bf16[4096,512]{1,0:T(8,128)(2,1)} fusion(bf16[4096,2048]{1,0:T(8,128)(2,1)} %get-tuple-element.49, bf16[1,2048,512]{2,1,0:T(8,128)(2,1)S(1)} %copy-done.68), kind=kOutput, calls=%fused_computation.13 | convolution fusion | flops 8592031744 | bytes 23068672 | tf_op jit(solution)/shard_map/dot_general | solution.py:24
  251.7 19.1 %all-to-all-done.3 = bf16[8,8,64,512]{3,2,1,0:T(8,128)(2,1)} async-done(((bf16[8,8,64,512]{3,2,1,0:T(8,128)(2,1)}), bf16[8,8,64,512]{3,2,1,0:T(8,128)(2,1)}, u32[]{:S(2)}, u32[]{:S(2)}) %all-to-all-start.3) | async-done | bytes 4194336 | tf_op jit(solution)/shard_map/all_to_all | solution.py:143
  270.8 4.7 all-to-all-start.1
  275.8 2.6 copy.129
  278.4 3.2 copy.148
  281.7 2.0 reshape.386
  284.5 14.6 %convolution_convert_fusion.5 = bf16[512,2048]{1,0:T(8,128)(2,1)} fusion(bf16[4096,512]{1,0:T(8,128)(2,1)} %bitcast.8, bf16[4096,2048]{1,0:T(8,128)(2,1)} %fusion.6), kind=kOutput, calls=%fused_computation.37 | convolution fusion | flops 8590983168 | bytes 23068672 | tf_op jit(solution)/shard_map/dot_general | solution.py:24
  299.2 8.7 %fusion.81 = (f32[512]{0:T(512)S(1)}, f32[16,64,512]{2,0,1:T(8,128)}) fusion(s32[16,2]{0,1:T(2,128)S(1)} %multiply_add_fusion.1, pred[16,2]{0,1:T(4,128)(4,1)S(1)} %broadcast_compare_fusion, bf16[8,8,64,512]{3,2,1,0:T(8,128)(2,1)} %all-to-all-done.3), kind=kOutput, calls=%fused_computation.149 | convolution fusion | flops 135794176 | bytes 6293664 | tf_op jit(solution)/shard_map/dot_general | solution.py:24
  307.9 16.7 %all-to-all-done.1 = bf16[8,8,64,512]{3,2,1,0:T(8,128)(2,1)} async-done(((bf16[8,8,64,512]{3,2,1,0:T(8,128)(2,1)}), bf16[8,8,64,512]{3,2,1,0:T(8,128)(2,1)}, u32[]{:S(2)}, u32[]{:S(2)}) %all-to-all-start.1) | async-done | bytes 4194336 | tf_op jit(solution)/shard_map/all_to_all | solution.py:130
  324.6 8.6 %multiply_reduce_fusion = (f32[16,2]{0,1:T(2,128)S(1)}, f32[16,64,512]{2,0,1:T(8,128)S(1)}) fusion(f32[16,64,512]{2,0,1:T(8,128)} %copy.129, f32[16,2]{0,1:T(2,128)S(1)} %copy-done.59, s32[16,2]{0,1:T(2,128)S(1)} %multiply_add_fusion.1, pred[16,2]{0,1:T(4,128)(4,1)S(1)} %broadcast_compare_fusion, bf16[8,8,64,512]{3,2,1,0:T(8,128)(2,1)} %all-to-all-done.1), kind=kOutput, calls=%fused_computation.20 | convolution fusion | flops 137891808 | bytes 8389024 | tf_op jit(solution)/shard_map/dot_general | solution.py:24
  333.3 6.2 %multiply_reduce_fusion.3 = (f32[]{:T(128)}, f32[]{:T(128)}, f32[16,64]{1,0:T(8,128)S(1)}, f32[16,64]{1,0:T(8,128)S(1)}, f32[512]{0:T(512)S(1)}, /*index=5*/f32[]{:T(128)}, bf16[16,64,512]{2,1,0:T(8,128)(2,1)}) fusion(f32[16,64,512]{2,1,0:T(8,128)S(1)} %copy-done.5, f32[16,64,512]{2,0,1:T(8,128)S(1)} %get-tuple-element.19, f32[16,64]{1,0:T(8,128)S(1)} %copy-done.39, ...), kind=kLoop, calls=%fused_computation.61 | loop fusion | flops 9958909 | bytes 9461772 | tf_op jit(solution)/shard_map/reduce_sum | solution.py:158
  339.5 1.8 fusion.80
  343.0 2.1 reshape.381
  345.1 4.2 copy.144
  349.3 5.2 multiply_reduce_fusion.1
  354.6 2.6 multiply_convert_fusion.3
  357.2 2.6 convert_bitcast_fusion
  359.8 4.1 copy.146
  363.9 3.6 reshape.384
  367.5 3.5 fusion.39
  371.0 3.1 copy.139
  374.1 4.0 reshape.382
  378.2 3.4 fusion.40
  381.6 3.1 copy.143
  384.8 4.2 reshape.383
  389.0 2.2 fusion.85
  392.3 2.2 fusion.82
  394.6 2.6 pad_maximum_fusion
  397.4 3.4 fusion.87
  400.8 1.7 fusion.86
  402.5 1.7 fusion.88
  404.3 1.7 fusion.89
  407.2 3.0 fusion.26
  410.2 40.8 %all-reduce = (f32[30,8]{0,1:T(8,128)}, f32[512]{0:T(512)}, f32[512]{0:T(512)}, f32[512]{0:T(512)}, f32[512]{0:T(512)}, /*index=5*/f32[4]{0:T(128)S(1)}) all-reduce(f32[30,8]{0,1:T(8,128)S(1)} %fusion.50, f32[512]{0:T(512)S(1)} %get-tuple-element.28, ...), channel_id=1, replica_groups=mesh['dp'=4,'expert'=8] {'dp','expert'}, use_global_device_ids=true, to_apply=%region_21.22 | all-reduce | flops 2292 | bytes 18336 | tf_op jit(solution)/shard_map/psum | solution.py:213
  452.7 5.3 fusion.25
  458.0 2.1 bitcast_convert_fusion
  460.2 2.1 bitcast_convert_fusion.1
  462.3 86.6 %all-reduce.4.cloned.1.call-done = (f32[512,512]{1,0:T(8,128)}, f32[512,512]{1,0:T(8,128)}, f32[512,512]{1,0:T(8,128)}, f32[512,512]{1,0:T(8,128)}) async-done(((f32[512,512]{1,0:T(8,128)}, f32[512,512]{1,0:T(8,128)}, f32[512,512]{1,0:T(8,128)}, f32[512,512]{1,0:T(8,128)}), (f32[512,512]{1,0:T(8,128)}, f32[512,512]{1,0:T(8,128)}, f32[512,512]{1,0:T(8,128)}, ...) | async-done | bytes 4194320 | tf_op jit(solution)/shard_map/psum | solution.py:213
  548.9 2.4 copy.212
  (198 shorter events, 27.0 us)
Async XLA Ops:
  8.0 113.9 %copy-start = (bf16[1,512,2048]{2,1,0:T(8,128)(2,1)S(1)}, bf16[1,512,2048]{2,1,0:T(8,128)(2,1)}, u32[]{:S(2)}) copy-start(bf16[1,512,2048]{2,1,0:T(8,128)(2,1)} %param.29) | copy-start | bytes 6291460
  8.0 5.5 copy-start.6
  8.0 5.4 copy-start.66
  8.1 5.5 copy-start.48
  8.1 5.5 copy-start.63
  9.8 58.3 %copy-start.52 = (s32[16,2]{0,1:T(2,128)}, s32[16,2]{0,1:T(2,128)S(1)}, u32[]{:S(2)}) copy-start(s32[16,2]{0,1:T(2,128)S(1)} %multiply_reduce_fusion.8) | copy-start | bytes 388
  10.2 3.9 copy-start.64
  10.2 4.9 copy-start.31
  11.7 1.8 copy-start.36
  13.6 34.5 %copy-start.44 = (pred[16,64]{1,0:T(8,128)(4,1)}, pred[16,64]{1,0:T(8,128)(4,1)S(1)}, u32[]{:S(2)}) copy-start(pred[16,64]{1,0:T(8,128)(4,1)S(1)} %get-tuple-element.45) | copy-start | bytes 3076
  13.6 55.8 %copy-start.38 = (f32[16,64]{1,0:T(8,128)}, f32[16,64]{1,0:T(8,128)S(1)}, u32[]{:S(2)}) copy-start(f32[16,64]{1,0:T(8,128)S(1)} %get-tuple-element.44) | copy-start | bytes 12292
  46.6 2.1 copy-start.2
  46.6 3.1 copy-start.16
  49.7 2.2 copy-start.19
  49.7 2.2 copy-start.29
  51.9 2.1 copy-start.14
  54.1 1.3 copy-start.4
  54.1 1.9 copy-start.50
  54.1 1.9 copy-start.60
  62.6 5.3 copy-start.61
  62.6 5.3 copy-start.69
  62.6 6.8 %copy-start.12 = (bf16[16,64,512]{2,1,0:T(8,128)(2,1)S(1)}, bf16[16,64,512]{2,1,0:T(8,128)(2,1)}, u32[]{:S(2)}) copy-start(bf16[16,64,512]{2,1,0:T(8,128)(2,1)} %param.31) | copy-start | bytes 3145732
  62.6 54.5 %all-to-all-start = ((bf16[8,8,64,512]{3,2,1,0:T(8,128)(2,1)}), bf16[8,8,64,512]{3,2,1,0:T(8,128)(2,1)}, u32[]{:S(2)}, u32[]{:S(2)}) async-start(bf16[8,8,64,512]{3,2,1,0:T(8,128)(2,1)} %copy.125), calls=%async_computation | async-start | bytes 8388608 | tf_op jit(solution)/shard_map/all_to_all | solution.py:126
  68.1 2.0 copy-start.46
  69.6 1.3 copy-start.9
  117.1 53.9 %all-to-all-start.2 = ((bf16[8,8,64,512]{3,2,1,0:T(8,128)(2,1)}), bf16[8,8,64,512]{3,2,1,0:T(8,128)(2,1)}, u32[]{:S(2)}, u32[]{:S(2)}) async-start(bf16[8,8,64,512]{3,2,1,0:T(8,128)(2,1)} %copy.131), calls=%async_computation.2 | async-start | bytes 8388608 | tf_op jit(solution)/shard_map/all_to_all | solution.py:137
  217.1 53.7 %all-to-all-start.3 = ((bf16[8,8,64,512]{3,2,1,0:T(8,128)(2,1)}), bf16[8,8,64,512]{3,2,1,0:T(8,128)(2,1)}, u32[]{:S(2)}, u32[]{:S(2)}) async-start(bf16[8,8,64,512]{3,2,1,0:T(8,128)(2,1)} %bitcast.163), calls=%async_computation.3 | async-start | bytes 8388608 | tf_op jit(solution)/shard_map/all_to_all | solution.py:143
  221.7 236.4 %reduce-scatter.5.cloned.1.call-start = ((), (), s32[]{:S(2)}) async-start(), calls=%async_computation.7 | async-start | bytes 2621440 | tf_op jit(solution)/shard_map/reduce_scatter | solution.py:219
  236.3 1.6 copy-start.68
  270.8 4.9 copy-start.65
  270.8 5.0 copy-start.10
  270.8 53.8 %all-to-all-start.1 = ((bf16[8,8,64,512]{3,2,1,0:T(8,128)(2,1)}), bf16[8,8,64,512]{3,2,1,0:T(8,128)(2,1)}, u32[]{:S(2)}, u32[]{:S(2)}) async-start(bf16[8,8,64,512]{3,2,1,0:T(8,128)(2,1)} %bitcast.162), calls=%async_computation.1 | async-start | bytes 8388608 | tf_op jit(solution)/shard_map/all_to_all | solution.py:130
  275.5 184.7 %reduce-scatter.3.cloned.1.call-start = ((), (), s32[]{:S(2)}) async-start(), calls=%async_computation.6 | async-start | bytes 2621440 | tf_op jit(solution)/shard_map/reduce_scatter | solution.py:216
  281.7 2.1 copy-start.67
  281.7 2.8 copy-start.53
  299.2 25.4 %copy-start.59 = (f32[16,2]{0,1:T(2,128)S(1)}, f32[16,2]{0,1:T(2,128)}, u32[]{:S(2)}) copy-start(f32[16,2]{0,1:T(2,128)} %copy-done.58) | copy-start | bytes 388
  299.2 249.7 %all-reduce.4.cloned.1.call-start = ((), (), s32[]{:S(2)}) async-start(), calls=%async_computation.8 | async-start | bytes 8388608 | tf_op jit(solution)/shard_map/psum | solution.py:213
  307.9 25.3 %copy-start.5 = (f32[16,64,512]{2,1,0:T(8,128)S(1)}, f32[16,64,512]{2,1,0:T(8,128)}, u32[]{:S(2)}) copy-start(f32[16,64,512]{2,1,0:T(8,128)} %copy-done.4) | copy-start | bytes 6291460
  307.9 25.3 %copy-start.35 = (f32[16,64]{1,0:T(8,128)S(1)}, f32[16,64]{1,0:T(8,128)}, u32[]{:S(2)}) copy-start(f32[16,64]{1,0:T(8,128)} %copy-done.34) | copy-start | bytes 12292
  307.9 25.3 %copy-start.39 = (f32[16,64]{1,0:T(8,128)S(1)}, f32[16,64]{1,0:T(8,128)}, u32[]{:S(2)}) copy-start(f32[16,64]{1,0:T(8,128)} %copy-done.38) | copy-start | bytes 12292
  307.9 25.4 %copy-start.41 = (f32[16,64]{1,0:T(8,128)S(1)}, f32[16,64]{1,0:T(8,128)}, u32[]{:S(2)}) copy-start(f32[16,64]{1,0:T(8,128)} %copy-done.40) | copy-start | bytes 12292
  307.9 25.4 %copy-start.51 = (f32[512]{0:T(512)S(1)}, f32[512]{0:T(512)}, u32[]{:S(2)}) copy-start(f32[512]{0:T(512)} %param.23) | copy-start | bytes 6148
  324.6 8.7 %copy-start.8 = (f32[16,64,512]{2,0,1:T(8,128)S(1)}, f32[16,64,512]{2,0,1:T(8,128)}, u32[]{:S(2)}) copy-start(f32[16,64,512]{2,0,1:T(8,128)} %get-tuple-element.17) | copy-start | bytes 6291460
  324.6 8.7 %copy-start.15 = (f32[16,64,512]{2,1,0:T(8,128)S(1)}, f32[16,64,512]{2,1,0:T(8,128)}, u32[]{:S(2)}) copy-start(f32[16,64,512]{2,1,0:T(8,128)} %get-tuple-element.48) | copy-start | bytes 6291460
  333.3 6.2 %copy-start.13 = (bf16[16,64,512]{2,1,0:T(8,128)(2,1)S(1)}, bf16[16,64,512]{2,1,0:T(8,128)(2,1)}, u32[]{:S(2)}) copy-start(bf16[16,64,512]{2,1,0:T(8,128)(2,1)} %param.31) | copy-start | bytes 3145732
  339.5 2.8 copy-start.30
  345.1 4.2 copy-start.20
  345.1 4.2 copy-start.45
  349.3 5.2 copy-start.3
  354.6 2.6 copy-start.11
  389.0 2.2 copy-start.17
  389.0 2.2 copy-start.32
  392.3 4.9 copy-start.47
  392.3 4.9 copy-start.55
  392.3 4.9 copy-start.57
  392.3 5.0 copy-start.62
  397.4 3.4 copy-start.18
  397.4 3.4 copy-start.23
  402.5 1.7 copy-start.21
  402.5 1.7 copy-start.28
  548.9 2.4 copy-start.26
  548.9 3.4 copy-start.25
  551.3 1.9 copy-start.24
  551.3 2.9 copy-start.1
  (13 other events, 12.2 us)
Sparse Core Ops, SparseCore 0:
  236.5 46.1 reduce-scatter.4
  299.3 46.2 reduce-scatter.2
Sparse Core Ops, SparseCore 1:
  406.1 142.7 all-reduce.3
where the time goes:
time: 571 us; the launch traced here: 562 us
  waiting for transfers between devices  187 us (33%)
  matrix products  178 us (31%)
  local copies, waits for them, and re-layouts  84.3 us (15%)
  blocking collectives  40.8 us (7%)
  other arithmetic  35.4 us (6%)
  starting transfers between devices  19.6 us (3%)
  between operations  17.2 us (3%)
    dot_general x22, matrix products, project(): return jnp.dot(left, right, preferred_element_type=jnp.float32)  156 us
    psum x1, waiting for transfers between devices, local(): summed = lax.psum(members, ('dp', 'expert'))  86.6 us
    psum x1, blocking collectives, local(): summed = lax.psum(members, ('dp', 'expert'))  40.8 us
    all_to_all x1, waiting for transfers between devices, local(): lax.all_to_all(outgoing, 'expert', split_axis=0, concat_axis=0, tiled=True)  38.8 us
    all_to_all x1, waiting for transfers between devices, local(): lax.all_to_all(grad_out, 'expert', split_axis=0, concat_axis=0, tiled=True)  25.8 us
    all_to_all x1, waiting for transfers between devices, local(): lax.all_to_all(dincoming.reshape(experts, capacity, slot, width), 'expert...  19.1 us
    unnamed x146, local copies, waits for them, and re-layouts  19 us
    all_to_all x1, waiting for transfers between devices, local(): lax.all_to_all(produced.reshape(experts, capacity, slot, width), 'expert'...  16.7 us
  transfers between devices with their start and end apart: 7, of which 5 were waited for; matrix products, arithmetic and copies ran while one was open for 33% of the time, Pallas kernels for 0%

commit v1 on v0

--- a/solution.py
+++ b/solution.py
@@ -1,6 +1,10 @@
+import functools
+
 import jax
 import jax.numpy as jnp
 from jax import lax
+from jax.experimental import pallas as pl
+from jax.experimental.pallas import tpu as pltpu
 from jax.sharding import PartitionSpec as P
 
 HEADS = 8
@@ -11,13 +15,6 @@
     variance = jnp.mean(centered * centered, axis=-1, keepdims=True)
     inverse = lax.rsqrt(variance + 1e-05)
     return (centered * inverse, inverse)
-
-
-def norm_backward(grad, normed, inverse, gain):
-    scaled = grad * gain
-    inner = scaled - jnp.mean(scaled, axis=-1, keepdims=True)
-    inner = inner - normed * jnp.mean(scaled * normed, axis=-1, keepdims=True)
-    return (inverse * inner, jnp.sum(grad * normed, axis=(0, 1)), jnp.sum(grad, axis=(0, 1)))
 
 
 def project(left, right):
@@ -39,6 +36,251 @@
     in_local = project(incoming.T, dpre)
     dincoming = project(dpre, first.T).astype(jnp.bfloat16)
     return (in_local, back_local, dincoming)
+
+
+BF = jnp.bfloat16
+F32 = jnp.float32
+VM = pltpu.VMEM
+
+
+def mm(a, b, ca=1, cb=0):
+    return lax.dot_general(a, b, (((ca,), (cb,)), ((), ())), preferred_element_type=F32)
+
+
+def block_diagonal(group, slot, head):
+    shape = (group * slot, group * head)
+    rows = lax.broadcasted_iota(jnp.int32, shape, 0) // slot
+    cols = lax.broadcasted_iota(jnp.int32, shape, 1) // head
+    return rows == cols
+
+
+def spread(part, mask, group):
+    return jnp.where(mask, jnp.concatenate([part] * group, axis=0), jnp.zeros((), part.dtype))
+
+
+def fold(product, mask, slot, group):
+    kept = jnp.where(mask, product, 0.0)
+    total = kept[0:slot]
+    for one in range(1, group):
+        total = total + kept[one * slot : (one + 1) * slot]
+    return total
+
+
+def attend(query, keyed, valued, length, mask, slot, group, scale):
+    scores = mm(keyed, spread(query, mask, group), 1, 1) * scale
+    place = lax.broadcasted_iota(jnp.int32, scores.shape, 0)
+    scores = jnp.where(place < length, scores, -1000000000.0)
+    raised = jnp.exp(scores - jnp.max(scores, axis=0, keepdims=True))
+    prob = raised / jnp.sum(raised, axis=0, keepdims=True)
+    context = fold(mm(prob.astype(BF), valued, 0, 0), mask, slot, group)
+    return prob, context
+
+
+def attention_forward_kernel(
+    heads, len_ref, x_ref, wq, wk, wv, wo, g1, b1, g2, b2,
+    act_o, q_o, k_o, v_o, ctx_o, p_o, h_o, m_o, st_o,
+):
+    count, slot, width = x_ref.shape
+    head = width // heads
+    group = max(1, min(heads, 256 // head))
+    span = group * head
+    step = pl.program_id(0)
+    scale = head ** -0.5
+    mask = block_diagonal(group, slot, head)
+    x = x_ref[...].astype(F32).reshape(count * slot, width)
+    normed, _ = normalize(x)
+    act = (normed * g1[...] + b1[...]).astype(BF)
+    act_o[...] = act
+    q_o[...] = mm(act, wq[...]).astype(BF)
+    k_o[...] = mm(act, wk[...]).astype(BF)
+    v_o[...] = mm(act, wv[...]).astype(BF)
+    for s in range(count):
+        length = len_ref[step * count + s]
+        rows = slice(s * slot, (s + 1) * slot)
+        for part in range(heads // group):
+            cols = slice(part * span, (part + 1) * span)
+            prob, context = attend(
+                q_o[rows, cols], k_o[rows, cols], v_o[rows, cols], length, mask, slot, group, scale
+            )
+            p_o[s, part] = prob
+            ctx_o[rows, cols] = context.astype(BF)
+    attn = mm(ctx_o[...], wo[...])
+    hidden = x + attn
+    h_o[...] = hidden
+    normed2, _ = normalize(hidden)
+    m_o[...] = (normed2 * g2[...] + b2[...]).astype(BF).reshape(count, slot, width)
+    place = lax.broadcasted_iota(jnp.int32, (slot, width), 0)
+    total = jnp.zeros((1, width), F32)
+    for s in range(count):
+        length = len_ref[step * count + s]
+        part = attn[s * slot : (s + 1) * slot]
+        total = total + jnp.sum(jnp.where(place < length, part * part, 0.0), axis=0, keepdims=True)
+
+    @pl.when(step == 0)
+    def _():
+        st_o[...] = jnp.zeros_like(st_o)
+
+    st_o[...] += total
+
+
+def attention_forward(tokens, lengths, wq, wk, wv, wo, g1, b1, g2, b2, heads):
+    sents, slot, width = tokens.shape
+    count = 4 if sents % 4 == 0 else 1
+    rows = count * slot
+    head = width // heads
+    group = max(1, min(heads, 256 // head))
+    whole = lambda *shape: pl.BlockSpec(shape, lambda i: (0,) * len(shape))
+    flat = pl.BlockSpec((rows, width), lambda i: (i, 0))
+    cube = pl.BlockSpec((count, slot, width), lambda i: (i, 0, 0))
+    probs = pl.BlockSpec((count, heads // group, slot, group * slot), lambda i: (i, 0, 0, 0))
+    shape = jax.ShapeDtypeStruct
+    total = sents * slot
+    return pl.pallas_call(
+        functools.partial(attention_forward_kernel, heads),
+        grid=(sents // count,),
+        in_specs=[pl.BlockSpec(memory_space=pltpu.SMEM), cube]
+        + [whole(width, width)] * 4
+        + [whole(1, width)] * 4,
+        out_specs=[flat] * 5 + [probs, flat, cube, whole(1, width)],
+        out_shape=[shape((total, width), BF)] * 5
+        + [
+            shape((sents, heads // group, slot, group * slot), F32),
+            shape((total, width), F32),
+            shape((sents, slot, width), BF),
+            shape((1, width), F32),
+        ],
+        compiler_params=pltpu.CompilerParams(
+            dimension_semantics=("arbitrary",), vmem_limit_bytes=56 * 2**20
+        ),
+        cost_estimate=pl.CostEstimate(
+            flops=8 * total * width * width + 4 * total * slot * width,
+            bytes_accessed=16 * total * width,
+            transcendentals=total * slot * heads,
+        ),
+    )(lengths, tokens, wq, wk, wv, wo, g1[None], b1[None], g2[None], b2[None])
+
+
+def row_sum(value, width):
+    return jnp.sum(value, axis=0, keepdims=True)
+
+
+def layer_norm_pull(grad, normed, inverse, gain):
+    scaled = grad * gain
+    inner = scaled - jnp.mean(scaled, axis=-1, keepdims=True)
+    inner = inner - normed * jnp.mean(scaled * normed, axis=-1, keepdims=True)
+    return inverse * inner
+
+
+def attention_pull(dcontext, query, keyed, valued, prob, mask, slot, group, scale):
+    low = prob.astype(BF)
+    dspread = spread(dcontext, mask, group)
+    dprob = mm(valued, dspread, 1, 1)
+    inner = jnp.sum(dprob * prob, axis=0, keepdims=True)
+    dscores = (prob * (dprob - inner)).astype(BF)
+    dquery = fold(mm(dscores, keyed, 0, 0), mask, slot, group) * scale
+    dkeyed = mm(dscores, spread(query, mask, group)) * scale
+    dvalued = mm(low, dspread)
+    return dquery.astype(BF), dkeyed.astype(BF), dvalued.astype(BF)
+
+
+def attention_backward_chunk(
+    heads, length_of, x_ref, cot_ref, dm_ref, h_ref, act, q, k, v, ctx, p_ref,
+    wq, wk, wv, wo, g1, g2, ig_o, dq_s, dk_s, dv_s, dctx_s, gq, gk, gv, go, norms,
+):
+    count, slot, width = x_ref.shape
+    head = width // heads
+    group = max(1, min(heads, 256 // head))
+    span = group * head
+    scale = head ** -0.5
+    mask = block_diagonal(group, slot, head)
+    place = lax.broadcasted_iota(jnp.int32, (slot, width), 0)
+    flat = lambda value: value.astype(F32).reshape(count * slot, width)
+    normed2, inverse2 = normalize(h_ref[...])
+    dm = flat(dm_ref[...])
+    cot = cot_ref[...].astype(F32)
+    gt = jnp.concatenate(
+        [jnp.where(place < length_of(s), cot[s], 0.0) for s in range(count)], axis=0
+    )
+    dhidden = gt + layer_norm_pull(dm, normed2, inverse2, g2[...])
+    norms[2:3] += row_sum(dm * normed2, width)
+    norms[3:4] += row_sum(dm, width)
+    dattn = dhidden.astype(BF)
+    go[...] += mm(ctx[...], dattn, 0, 0)
+    dctx_s[...] = mm(dattn, wo[...], 1, 1).astype(BF)
+    for s in range(count):
+        rows = slice(s * slot, (s + 1) * slot)
+        for part in range(heads // group):
+            cols = slice(part * span, (part + 1) * span)
+            dq_s[rows, cols], dk_s[rows, cols], dv_s[rows, cols] = attention_pull(
+                dctx_s[rows, cols], q[rows, cols], k[rows, cols], v[rows, cols],
+                p_ref[s, part], mask, slot, group, scale,
+            )
+    dq, dk, dv = dq_s[...], dk_s[...], dv_s[...]
+    gq[...] += mm(act[...], dq, 0, 0)
+    gk[...] += mm(act[...], dk, 0, 0)
+    gv[...] += mm(act[...], dv, 0, 0)
+    dact = mm(dq, wq[...], 1, 1) + mm(dk, wk[...], 1, 1) + mm(dv, wv[...], 1, 1)
+    normed1, inverse1 = normalize(flat(x_ref[...]))
+    norms[0:1] += row_sum(dact * normed1, width)
+    norms[1:2] += row_sum(dact, width)
+    dx = dhidden + layer_norm_pull(dact, normed1, inverse1, g1[...])
+    ig_o[...] = dx.astype(BF).reshape(count, slot, width)
+
+
+def attention_backward_kernel(
+    heads, len_ref, x_ref, cot_ref, dm_ref, h_ref, act, q, k, v, ctx, p_ref,
+    wq, wk, wv, wo, g1, g2, ig_o, gq, gk, gv, go, norms, dq_s, dk_s, dv_s, dctx_s,
+):
+    step = pl.program_id(0)
+    count = x_ref.shape[0]
+
+    @pl.when(step == 0)
+    def _():
+        for total in (gq, gk, gv, go, norms):
+            total[...] = jnp.zeros_like(total)
+
+    attention_backward_chunk(
+        heads, lambda s: len_ref[step * count + s], x_ref, cot_ref, dm_ref, h_ref,
+        act, q, k, v, ctx, p_ref, wq, wk, wv, wo, g1, g2, ig_o,
+        dq_s, dk_s, dv_s, dctx_s, gq, gk, gv, go, norms,
+    )
+
+
+def attention_backward(
+    lengths, tokens, cot, dm, hidden, act, q, k, v, ctx, prob, wq, wk, wv, wo, g1, g2, heads
+):
+    sents, slot, width = tokens.shape
+    count = 4 if sents % 4 == 0 else 1
+    rows = count * slot
+    head = width // heads
+    group = max(1, min(heads, 256 // head))
+    whole = lambda *shape: pl.BlockSpec(shape, lambda i: (0,) * len(shape))
+    flat = pl.BlockSpec((rows, width), lambda i: (i, 0))
+    cube = pl.BlockSpec((count, slot, width), lambda i: (i, 0, 0))
+    probs = pl.BlockSpec((count, heads // group, slot, group * slot), lambda i: (i, 0, 0, 0))
+    shape = jax.ShapeDtypeStruct
+    total = sents * slot
+    return pl.pallas_call(
+        functools.partial(attention_backward_kernel, heads),
+        grid=(sents // count,),
+        in_specs=[pl.BlockSpec(memory_space=pltpu.SMEM), cube, cube, cube]
+        + [flat] * 6 + [probs]
+        + [whole(width, width)] * 4
+        + [whole(1, width)] * 2,
+        out_specs=[cube] + [whole(width, width)] * 4 + [whole(8, width)],
+        out_shape=[shape((sents, slot, width), BF)]
+        + [shape((width, width), F32)] * 4
+        + [shape((8, width), F32)],
+        scratch_shapes=[VM((rows, width), BF)] * 4,
+        compiler_params=pltpu.CompilerParams(
+            dimension_semantics=("arbitrary",), vmem_limit_bytes=56 * 2**20
+        ),
+        cost_estimate=pl.CostEstimate(
+            flops=16 * total * width * width + 10 * total * slot * width,
+            bytes_accessed=24 * total * width,
+            transcendentals=0,
+        ),
+    )(lengths, tokens, cot, dm, hidden, act, q, k, v, ctx, prob, wq, wk, wv, wo, g1[None], g2[None])
 
 
 def local(
@@ -61,11 +303,9 @@
 ):
     sents, slot, width = tokens.shape
     heads = HEADS
-    head = width // heads
     experts = gate_table.shape[1]
     ntasks = routes.shape[0]
     capacity = max(1, 4 * sents // experts)
-    scale = 1.0 / jnp.sqrt(jnp.float32(head))
     task_hot = (tasks[:, None] == jnp.arange(ntasks)[None, :]).astype(jnp.int32)
     chosen = jnp.sum(task_hot[:, :, None] * routes[None, :, :], axis=1)
     flat = chosen.reshape(-1)
@@ -80,31 +320,12 @@
     collect = dispatch.T
     expert_hot = (chosen[:, :, None] == jnp.arange(experts)[None, None, :]).astype(jnp.float32)
     valid = (jnp.arange(slot)[None, :] < lengths[:, None]).astype(jnp.float32)
-    keymask = valid[:, None, None, :] > 0.5
     mask3 = valid[:, :, None]
-    xfull = tokens.astype(jnp.float32)
-    normed1, inverse1 = normalize(xfull)
-    act = (normed1 * ln1_gain + ln1_bias).astype(jnp.bfloat16).reshape(-1, width)
-    query = project(act, w_query).astype(jnp.bfloat16).reshape(sents, slot, heads, head)
-    keyed = project(act, w_key).astype(jnp.bfloat16).reshape(sents, slot, heads, head)
-    valued = project(act, w_value).astype(jnp.bfloat16).reshape(sents, slot, heads, head)
-
-    def scores_of(qpart, kpart):
-        raw = (
-            jnp.einsum("sqhd,skhd->shqk", qpart, kpart, preferred_element_type=jnp.float32) * scale
-        )
-        return jnp.where(keymask, raw, -1000000000.0)
-
-    scores = scores_of(query, keyed)
-    peak = jnp.max(scores, axis=-1, keepdims=True)
-    logsum = peak + jnp.log(jnp.sum(jnp.exp(scores - peak), axis=-1, keepdims=True))
-    prob_low = jnp.exp(scores - logsum).astype(jnp.bfloat16)
-    context = jnp.einsum("shqk,skhd->sqhd", prob_low, valued, preferred_element_type=jnp.float32)
-    context = context.astype(jnp.bfloat16).reshape(-1, width)
-    attention_block = project(context, w_out).reshape(sents, slot, width)
-    hidden_res = xfull + attention_block
-    normed2, inverse2 = normalize(hidden_res)
-    mixed = (normed2 * ln2_gain + ln2_bias).astype(jnp.bfloat16)
+    act, query, keyed, valued, context, prob, hidden, mixed, attn_sum = attention_forward(
+        tokens, lengths, w_query, w_key, w_value, w_out,
+        ln1_gain, ln1_bias, ln2_gain, ln2_bias, heads,
+    )
+    hidden_res = hidden.reshape(sents, slot, width)
     table_rows = jnp.dot(task_hot.astype(jnp.float32), gate_table, precision=lax.Precision.HIGHEST)
     picked = jnp.sum(expert_hot * table_rows[:, None, :], axis=-1)
     gate_values = jax.nn.softmax(picked, axis=-1)
@@ -156,7 +377,7 @@
     stats_local = jnp.stack(
         [
             jnp.sum(total * total),
-            jnp.sum(mask3 * attention_block * attention_block),
+            jnp.sum(attn_sum),
             jnp.sum(mask3 * expert_mixture * expert_mixture),
             jnp.sum(valid),
         ]
@@ -170,34 +391,11 @@
         sents, 2, slot, width
     )
     dmixed = jnp.sum(dmixed, axis=1)
-    dres2, gain2_grad, bias2_grad = norm_backward(dmixed, normed2, inverse2, ln2_gain)
-    dhidden = grad_total + dres2
-    dattn = dhidden.astype(jnp.bfloat16).reshape(-1, width)
-    wout_grad = project(context.T, dattn)
-    dcontext = project(dattn, w_out.T).astype(jnp.bfloat16).reshape(sents, slot, heads, head)
-    again = jnp.exp(scores_of(query, keyed) - logsum)
-    dprob = jnp.einsum("sqhd,skhd->shqk", dcontext, valued, preferred_element_type=jnp.float32)
-    dscores = (again * (dprob - jnp.sum(dprob * again, axis=-1, keepdims=True))).astype(
-        jnp.bfloat16
-    )
-    dquery = (
-        jnp.einsum("shqk,skhd->sqhd", dscores, keyed, preferred_element_type=jnp.float32) * scale
-    )
-    dkeyed = (
-        jnp.einsum("shqk,sqhd->skhd", dscores, query, preferred_element_type=jnp.float32) * scale
-    )
-    dvalued = jnp.einsum("shqk,sqhd->skhd", prob_low, dcontext, preferred_element_type=jnp.float32)
-    dquery = dquery.astype(jnp.bfloat16).reshape(-1, width)
-    dkeyed = dkeyed.astype(jnp.bfloat16).reshape(-1, width)
-    dvalued = dvalued.astype(jnp.bfloat16).reshape(-1, width)
-    wq_grad = project(act.T, dquery)
-    wk_grad = project(act.T, dkeyed)
-    wv_grad = project(act.T, dvalued)
-    dact = project(dquery, w_query.T) + project(dkeyed, w_key.T) + project(dvalued, w_value.T)
-    dres1, gain1_grad, bias1_grad = norm_backward(
-        dact.reshape(sents, slot, width), normed1, inverse1, ln1_gain
-    )
-    input_grad = (dhidden + dres1).astype(jnp.bfloat16)
+    input_grad, wq_grad, wk_grad, wv_grad, wout_grad, norms = attention_backward(
+        lengths, tokens, cotangent, dmixed, hidden, act, query, keyed, valued, context, prob,
+        w_query, w_key, w_value, w_out, ln1_gain, ln2_gain, heads,
+    )
+    gain1_grad, bias1_grad, gain2_grad, bias2_grad = norms[0], norms[1], norms[2], norms[3]
     members = (
         wq_grad,
         wk_grad,

time: 571 us -> 456 us (0.80)
  local copies, waits for them, and re-layouts: 84.3 us -> 32.4 us
  matrix products: 178 us -> 132 us
  Pallas kernels: 0 us -> 34.3 us
  waiting for transfers between devices: 187 us -> 157 us
  other arithmetic: 35.4 us -> 17.2 us
    reshape x11 -> x0, local copies, waits for them, and re-layouts: 40.1 us -> none  [the longest x2 8.07 us: local(): project(act, w_key).astype(jnp.bfloat16).reshape(sents, slot, heads, head)]
    pallas_call x0 -> x2, Pallas kernels: none -> 34.3 us  [the longest x1 21.2 us: attention_backward(): pl.pallas_call(functools.partial(attention_backward_kernel, heads), grid=...]
    dot_general x22 -> x10, matrix products: 156 us -> 131 us  [project(): return jnp.dot(left, right, preferred_element_type=jnp.float32)]
    dot_general x6 -> x0, matrix products: 20.8 us -> none  [the longest x1 5.23 us: local(): jnp.einsum('sqhd,skhd->shqk', dcontext, valued, preferred_element_type=jn...]
    all_to_all x1, waiting for transfers between devices: 16.7 us -> 0.01 us  [local(): lax.all_to_all(produced.reshape(experts, capacity, slot, width), 'expert'...]
    all_to_all x1, waiting for transfers between devices: 25.8 us -> 11.7 us  [local(): lax.all_to_all(grad_out, 'expert', split_axis=0, concat_axis=0, tiled=True)]
    convert_element_type x4 -> x2, local copies, waits for them, and re-layouts: 13.6 us -> 0.15 us  [local(): valid = (jnp.arange(slot)[None, :] < lengths[:, None]).astype(jnp.float32)]
    convert_element_type x5 -> x0, other arithmetic: 10.6 us -> none  [the longest x1 5.33 us: local(): input_grad = (dhidden + dres1).astype(jnp.bfloat16)]
  transfers between devices with their start and end apart: 7 -> 7, of which waited for: 5 -> 4; matrix products, arithmetic and copies ran while one was open for 33% -> 36% of each run, Pallas kernels for 0% -> 5%
where the time goes in v1:
time: 456 us; the launch traced here: 450 us
  waiting for transfers between devices  157 us (34%)
  matrix products  132 us (29%)
  blocking collectives  40.8 us (9%)
  Pallas kernels  34.3 us (8%)
  local copies, waits for them, and re-layouts  32.4 us (7%)
  starting transfers between devices  20 us (4%)
  other arithmetic  17.2 us (4%)
  between operations  16.8 us (4%)
    dot_general x10, matrix products, project(): return jnp.dot(left, right, preferred_element_type=jnp.float32)  131 us
    psum x1, waiting for transfers between devices, local(): summed = lax.psum(members, ('dp', 'expert'))  88.8 us
    psum x1, blocking collectives, local(): summed = lax.psum(members, ('dp', 'expert'))  40.8 us
    all_to_all x1, waiting for transfers between devices, local(): lax.all_to_all(outgoing, 'expert', split_axis=0, concat_axis=0, tiled=True)  36.4 us
    pallas_call x1, Pallas kernels, attention_backward(): pl.pallas_call(functools.partial(attention_backward_kernel, heads), grid=...  21.2 us
    all_to_all x1, waiting for transfers between devices, local(): lax.all_to_all(dincoming.reshape(experts, capacity, slot, width), 'expert...  20.4 us
    unnamed x72, local copies, waits for them, and re-layouts  16.8 us
    pallas_call x1, Pallas kernels, attention_forward(): pl.pallas_call(functools.partial(attention_forward_kernel, heads), grid=(...  13.1 us
  transfers between devices with their start and end apart: 7, of which 4 were waited for; matrix products, arithmetic and copies ran while one was open for 36% of the time, Pallas kernels for 5%

profile of v1, /device:TPU:0, one launch (start us, length us, event | category | flops | bytes accessed | tf_op | source)
XLA Modules:
  0.0 450.4 jit_solution(581063295284209538)
XLA Ops:
  8.0 0.9 fusion.45
  8.9 0.8 multiply_reduce_fusion.2
  9.7 0.1 copy.81
  9.8 0.1 reshape.264
  9.9 0.2 convert_reduce_fusion
  10.1 13.1 %shard_map.263 = (bf16[1024,512]{1,0:T(8,128)(2,1)}, bf16[1024,512]{1,0:T(8,128)(2,1)}, bf16[1024,512]{1,0:T(8,128)(2,1)}, bf16[1024,512]{1,0:T(8,128)(2,1)}, bf...) custom-call(s32[16]{0:T(128)} %len_ref.3, ...), custom_call_target="tpu_custom_call" | custom-call | flops 2281701376 | bytes 8388608 | tf_op jit(solution)/shard_map/pallas_call | solution.py:138
  23.2 1.5 broadcast_in_dim.24
  24.6 1.2 copy.99
  25.8 1.2 convolution_convert_fusion.1
  27.0 3.5 copy.84
  30.6 5.5 %all-to-all-start = ((bf16[8,8,64,512]{3,2,1,0:T(8,128)(2,1)}), bf16[8,8,64,512]{3,2,1,0:T(8,128)(2,1)}, u32[]{:S(2)}, u32[]{:S(2)}) async-start(bf16[8,8,64,512]{3,2,1,0:T(8,128)(2,1)} %copy.84), calls=%async_computation | async-start | bytes 8388608 | tf_op jit(solution)/shard_map/all_to_all | solution.py:347
  36.1 0.1 fusion.44
  36.2 0.1 copy.80
  36.3 0.2 fusion.42
  36.6 0.5 copy-done.16
  37.2 0.5 copy-done.18
  37.7 0.1 copy.87
  37.8 0.1 div.28
  37.9 0.7 convert_multiply_fusion
  38.5 1.3 copy-done.2
  39.9 1.2 copy.96
  41.1 0.5 mul.181.clone
  41.6 2.4 copy.101
  44.1 1.3 convolution_convert_fusion
  45.4 3.5 copy.90
  48.9 36.4 %all-to-all-done = bf16[8,8,64,512]{3,2,1,0:T(8,128)(2,1)} async-done(((bf16[8,8,64,512]{3,2,1,0:T(8,128)(2,1)}), bf16[8,8,64,512]{3,2,1,0:T(8,128)(2,1)}, u32[]{:S(2)}, u32[]{:S(2)}) %all-to-all-start) | async-done | bytes 4194336 | tf_op jit(solution)/shard_map/all_to_all | solution.py:347
  85.3 4.8 %all-to-all-start.2 = ((bf16[8,8,64,512]{3,2,1,0:T(8,128)(2,1)}), bf16[8,8,64,512]{3,2,1,0:T(8,128)(2,1)}, u32[]{:S(2)}, u32[]{:S(2)}) async-start(bf16[8,8,64,512]{3,2,1,0:T(8,128)(2,1)} %copy.90), calls=%async_computation.2 | async-start | bytes 8388608 | tf_op jit(solution)/shard_map/all_to_all | solution.py:358
  90.1 23.7 %multiply_convert_fusion = (bf16[4096,2048]{1,0:T(8,128)(2,1)}, f32[4096,2048]{1,0:T(8,128)}) fusion(bf16[4096,512]{1,0:T(8,128)(2,1)} %bitcast.9, bf16[1,512,2048]{2,1,0:T(8,128)(2,1)S(1)} %copy-done), kind=kOutput, calls=%fused_computation.11 | convolution fusion | flops 8665432064 | bytes 56623104 | tf_op jit(solution)/shard_map/dot_general | solution.py:21
  113.8 13.8 %convolution_convert_fusion.3 = bf16[4096,512]{1,0:T(8,128)(2,1)} fusion(bf16[4096,2048]{1,0:T(8,128)(2,1)} %get-tuple-element.104, bf16[1,2048,512]{2,1,0:T(8,128)(2,1)S(1)} %copy-done.30), kind=kOutput, calls=%fused_computation.13 | convolution fusion | flops 8592031744 | bytes 23068672 | tf_op jit(solution)/shard_map/dot_general | solution.py:21
  127.5 11.7 %all-to-all-done.2 = bf16[8,8,64,512]{3,2,1,0:T(8,128)(2,1)} async-done(((bf16[8,8,64,512]{3,2,1,0:T(8,128)(2,1)}), bf16[8,8,64,512]{3,2,1,0:T(8,128)(2,1)}, u32[]{:S(2)}, u32[]{:S(2)}) %all-to-all-start.2) | async-done | bytes 4194336 | tf_op jit(solution)/shard_map/all_to_all | solution.py:358
  139.2 4.6 %all-to-all-start.1 = ((bf16[8,8,64,512]{3,2,1,0:T(8,128)(2,1)}), bf16[8,8,64,512]{3,2,1,0:T(8,128)(2,1)}, u32[]{:S(2)}, u32[]{:S(2)}) async-start(bf16[8,8,64,512]{3,2,1,0:T(8,128)(2,1)} %bitcast.118), calls=%async_computation.1 | async-start | bytes 8388608 | tf_op jit(solution)/shard_map/all_to_all | solution.py:351
  143.8 0.3 reduce-scatter.5.cloned.1.call-start
  144.1 14.7 %convolution_convert_fusion.4 = bf16[2048,512]{1,0:T(8,128)(2,1)} fusion(bf16[4096,2048]{1,0:T(8,128)(2,1)} %get-tuple-element.104, bf16[4096,512]{1,0:T(8,128)(2,1)} %bitcast.17), kind=kOutput, calls=%fused_computation.24 | convolution fusion | flops 8590983168 | bytes 23068672 | tf_op jit(solution)/shard_map/dot_general | solution.py:21
  158.8 31.9 %fusion.6 = bf16[4096,2048]{1,0:T(8,128)(2,1)} fusion(f32[4096,2048]{1,0:T(8,128)} %get-tuple-element.105, bf16[4096,512]{1,0:T(8,128)(2,1)} %bitcast.17, bf16[1,2048,512]{2,1,0:T(8,128)(2,1)} %param.30), kind=kOutput, calls=%fused_computation.10 | convolution fusion | flops 8757706752 | bytes 56623104 | tf_op jit(solution)/shard_map/dot_general | solution.py:21
  190.6 14.3 %convolution_convert_fusion.2 = bf16[4096,512]{1,0:T(8,128)(2,1)} fusion(bf16[4096,2048]{1,0:T(8,128)(2,1)} %fusion.6, bf16[1,512,2048]{2,1,0:T(8,128)(2,1)S(1)} %copy-done), kind=kOutput, calls=%fused_computation.12 | convolution fusion | flops 8592031744 | bytes 23068672 | tf_op jit(solution)/shard_map/dot_general | solution.py:21
  204.9 4.6 %all-to-all-start.3 = ((bf16[8,8,64,512]{3,2,1,0:T(8,128)(2,1)}), bf16[8,8,64,512]{3,2,1,0:T(8,128)(2,1)}, u32[]{:S(2)}, u32[]{:S(2)}) async-start(bf16[8,8,64,512]{3,2,1,0:T(8,128)(2,1)} %bitcast.117), calls=%async_computation.3 | async-start | bytes 8388608 | tf_op jit(solution)/shard_map/all_to_all | solution.py:364
  209.6 14.6 %convolution_convert_fusion.5 = bf16[512,2048]{1,0:T(8,128)(2,1)} fusion(bf16[4096,512]{1,0:T(8,128)(2,1)} %bitcast.9, bf16[4096,2048]{1,0:T(8,128)(2,1)} %fusion.6), kind=kOutput, calls=%fused_computation.25 | convolution fusion | flops 8590983168 | bytes 23068672 | tf_op jit(solution)/shard_map/dot_general | solution.py:21
  224.3 0.2 all-reduce.4.cloned.1.call-start
  224.5 0.1 reduce_sum.125
  224.6 0.1 copy.82
  224.7 0.6 reduce_sum.133
  225.3 0.7 fusion.49
  226.0 8.4 %multiply_reduce_fusion = (f32[16,2]{0,1:T(2,128)S(1)}, f32[16,64,512]{2,0,1:T(8,128)S(1)}) fusion(f32[16,64,512]{2,0,1:T(8,128)} %copy-done.2, f32[16,2]{0,1:T(2,128)S(1)} %copy-done.21, s32[16,2]{0,1:T(2,128)S(1)} %multiply_add_fusion, pred[16,2]{0,1:T(4,128)(4,1)S(1)} %broadcast_compare_fusion, bf16[8,8,64,512]{3,2,1,0:T(8,128)(2,1)} %all-to-all-done.1), kind=kOutput, calls=%fused_computation.20 | convolution fusion | flops 137891808 | bytes 8389024 | tf_op jit(solution)/shard_map/dot_general | solution.py:21
  234.4 1.3 copy-done.3
  235.7 2.5 copy.93
  238.3 20.4 %all-to-all-done.3 = bf16[8,8,64,512]{3,2,1,0:T(8,128)(2,1)} async-done(((bf16[8,8,64,512]{3,2,1,0:T(8,128)(2,1)}), bf16[8,8,64,512]{3,2,1,0:T(8,128)(2,1)}, u32[]{:S(2)}, u32[]{:S(2)}) %all-to-all-start.3) | async-done | bytes 4194336 | tf_op jit(solution)/shard_map/all_to_all | solution.py:364
  258.6 7.5 %fusion.23 = f32[16,64,512]{2,0,1:T(8,128)S(1)} fusion(s32[16,2]{0,1:T(2,128)S(1)} %multiply_add_fusion, pred[16,2]{0,1:T(4,128)(4,1)S(1)} %broadcast_compare_fusion, bf16[8,8,64,512]{3,2,1,0:T(8,128)(2,1)} %all-to-all-done.3), kind=kOutput, calls=%fused_computation.41 | convolution fusion | flops 134746112 | bytes 6291616 | tf_op jit(solution)/shard_map/dot_general | solution.py:21
  266.2 2.8 copy.92.dm_ref
  268.9 2.3 fusion.11
  271.3 21.2 %shard_map.264 = (bf16[16,64,512]{2,1,0:T(8,128)(2,1)}, f32[512,512]{1,0:T(8,128)}, f32[512,512]{1,0:T(8,128)}, f32[512,512]{1,0:T(8,128)}, f32[512,512]{1,0:T(8,128)}, /*index=5*/f32[8,512]{1,0:T(8,128)}) custom-call(s32[16]{0:T(128)} %len_ref.3, bf16[16,64,512]{2,1,0:T(8,128)(2,1)} %x_ref.3, bf16[16,64,512]{2,1,0:T(8,128)(2,1)} %cot_ref.1, ...), custom_call_target="tpu_custom_call" | custom-call | flops 4630511616 | bytes 12582912 | tf_op jit(solution)/shard_map/pallas_call | solution.py:263
  292.6 3.5 fusion.14
  296.1 2.6 pad_maximum_fusion
  298.7 0.1 fusion.27
  298.9 40.8 %all-reduce = (f32[30,8]{0,1:T(8,128)}, f32[512]{0:T(512)}, f32[512]{0:T(512)}, f32[512]{0:T(512)}, f32[512]{0:T(512)}, /*index=5*/f32[4]{0:T(128)S(1)}) all-reduce(f32[30,8]{0,1:T(8,128)S(1)} %fusion.27, f32[512]{0:T(512)S(1)} %bitcast.122, f32[512]{0:T(512)S(1)} %bitcast.121, ...), channel_id=1, replica_groups=mesh['dp'=4,'expert'=8] {'dp','expert'}, use_global_device_ids=true, to_apply=%region_10.0 | all-reduce | flops 2292 | bytes 18336 | tf_op jit(solution)/shard_map/psum | solution.py:411
  339.7 0.6 slice.23
  340.3 1.5 copy.94
  342.5 0.5 divide_sqrt_fusion
  343.0 2.1 bitcast_convert_fusion
  345.1 2.1 bitcast_convert_fusion.1
  347.3 88.8 %all-reduce.4.cloned.1.call-done = (f32[512,512]{1,0:T(8,128)}, f32[512,512]{1,0:T(8,128)}, f32[512,512]{1,0:T(8,128)}, f32[512,512]{1,0:T(8,128)}) async-done(((f32[512,512]{1,0:T(8,128)}, f32[512,512]{1,0:T(8,128)}, f32[512,512]{1,0:T(8,128)}, f32[512,512]{1,0:T(8,128)}), (f32[512,512]{1,0:T(8,128)}, f32[512,512]{1,0:T(8,128)}, f32[512,512]{1,0:T(8,128)}, ...) | async-done | bytes 4194320 | tf_op jit(solution)/shard_map/psum | solution.py:411
  436.1 2.4 copy.131
  438.5 2.3 copy.132
  440.8 1.0 copy.133
  441.7 1.0 copy.134
  (80 shorter events, 0.5 us)
Async XLA Ops:
  8.0 82.1 %copy-start = (bf16[1,512,2048]{2,1,0:T(8,128)(2,1)S(1)}, bf16[1,512,2048]{2,1,0:T(8,128)(2,1)}, u32[]{:S(2)}) copy-start(bf16[1,512,2048]{2,1,0:T(8,128)(2,1)} %param.29) | copy-start | bytes 6291460
  9.7 26.8 %copy-start.14 = (s32[16,2]{0,1:T(2,128)}, s32[16,2]{0,1:T(2,128)S(1)}, u32[]{:S(2)}) copy-start(s32[16,2]{0,1:T(2,128)S(1)} %multiply_reduce_fusion.2) | copy-start | bytes 388
  10.1 13.1 %copy-start.28 = (s32[32]{0:T(128)}, s32[32]{0:T(128)S(1)}, u32[]{:S(2)}) copy-start(s32[32]{0:T(128)S(1)} %convert_reduce_fusion) | copy-start | bytes 388
  30.6 5.6 %copy-start.26 = (s32[16]{0:T(128)S(1)}, s32[16]{0:T(128)}, u32[]{:S(2)}) copy-start(s32[16]{0:T(128)} %len_ref.3) | copy-start | bytes 196
  30.6 5.7 %copy-start.23 = (s32[16]{0:T(128)S(1)}, s32[16]{0:T(128)}, u32[]{:S(2)}) copy-start(s32[16]{0:T(128)} %param.18) | copy-start | bytes 196
  30.6 5.7 %copy-start.31 = (f32[30,8]{0,1:T(8,128)S(1)}, f32[30,8]{0,1:T(8,128)}, u32[]{:S(2)}) copy-start(f32[30,8]{0,1:T(8,128)} %param.20) | copy-start | bytes 2884
  30.6 7.3 %copy-start.5 = (bf16[16,64,512]{2,1,0:T(8,128)(2,1)S(1)}, bf16[16,64,512]{2,1,0:T(8,128)(2,1)}, u32[]{:S(2)}) copy-start(bf16[16,64,512]{2,1,0:T(8,128)(2,1)} %cot_ref.1) | copy-start | bytes 3145732
  30.6 54.7 %all-to-all-start = ((bf16[8,8,64,512]{3,2,1,0:T(8,128)(2,1)}), bf16[8,8,64,512]{3,2,1,0:T(8,128)(2,1)}, u32[]{:S(2)}, u32[]{:S(2)}) async-start(bf16[8,8,64,512]{3,2,1,0:T(8,128)(2,1)} %copy.84), calls=%async_computation | async-start | bytes 8388608 | tf_op jit(solution)/shard_map/all_to_all | solution.py:347
  36.2 5.4 %copy-start.10 = (f32[16,64]{1,0:T(8,128)}, f32[16,64]{1,0:T(8,128)S(1)}, u32[]{:S(2)}) copy-start(f32[16,64]{1,0:T(8,128)S(1)} %fusion.44) | copy-start | bytes 12292
  36.3 5.3 %copy-start.8 = (f32[16,64]{0,1:T(8,128)}, f32[16,64]{0,1:T(8,128)S(1)}, u32[]{:S(2)}) copy-start(f32[16,64]{0,1:T(8,128)S(1)} %copy.80) | copy-start | bytes 12292
  36.5 5.1 %copy-start.12 = (f32[16,2]{0,1:T(2,128)}, f32[16,2]{0,1:T(2,128)S(1)}, u32[]{:S(2)}) copy-start(f32[16,2]{0,1:T(2,128)S(1)} %select_reduce_fusion.1) | copy-start | bytes 388
  36.6 0.6 copy-start.16
  37.2 0.5 copy-start.18
  37.7 4.0 copy-start.20
  38.5 1.3 copy-start.2
  85.3 53.9 %all-to-all-start.2 = ((bf16[8,8,64,512]{3,2,1,0:T(8,128)(2,1)}), bf16[8,8,64,512]{3,2,1,0:T(8,128)(2,1)}, u32[]{:S(2)}, u32[]{:S(2)}) async-start(bf16[8,8,64,512]{3,2,1,0:T(8,128)(2,1)} %copy.90), calls=%async_computation.2 | async-start | bytes 8388608 | tf_op jit(solution)/shard_map/all_to_all | solution.py:358
  90.1 23.7 %copy-start.30 = (bf16[1,2048,512]{2,1,0:T(8,128)(2,1)S(1)}, bf16[1,2048,512]{2,1,0:T(8,128)(2,1)}, u32[]{:S(2)}) copy-start(bf16[1,2048,512]{2,1,0:T(8,128)(2,1)} %param.30) | copy-start | bytes 6291460
  139.2 65.7 %all-to-all-start.1 = ((bf16[8,8,64,512]{3,2,1,0:T(8,128)(2,1)}), bf16[8,8,64,512]{3,2,1,0:T(8,128)(2,1)}, u32[]{:S(2)}, u32[]{:S(2)}) async-start(bf16[8,8,64,512]{3,2,1,0:T(8,128)(2,1)} %bitcast.118), calls=%async_computation.1 | async-start | bytes 8388608 | tf_op jit(solution)/shard_map/all_to_all | solution.py:351
  143.8 199.2 %reduce-scatter.5.cloned.1.call-start = ((), (), s32[]{:S(2)}) async-start(), calls=%async_computation.7 | async-start | bytes 2621440 | tf_op jit(solution)/shard_map/reduce_scatter | solution.py:417
  204.9 53.7 %all-to-all-start.3 = ((bf16[8,8,64,512]{3,2,1,0:T(8,128)(2,1)}), bf16[8,8,64,512]{3,2,1,0:T(8,128)(2,1)}, u32[]{:S(2)}, u32[]{:S(2)}) async-start(bf16[8,8,64,512]{3,2,1,0:T(8,128)(2,1)} %bitcast.117), calls=%async_computation.3 | async-start | bytes 8388608 | tf_op jit(solution)/shard_map/all_to_all | solution.py:364
  209.5 15.0 %copy-start.29 = (s32[32]{0:T(128)S(1)}, s32[32]{0:T(128)}, u32[]{:S(2)}) copy-start(s32[32]{0:T(128)} %copy-done.28) | copy-start | bytes 388
  209.5 15.0 %copy-start.11 = (f32[16,64]{1,0:T(8,128)S(1)}, f32[16,64]{1,0:T(8,128)}, u32[]{:S(2)}) copy-start(f32[16,64]{1,0:T(8,128)} %copy-done.10) | copy-start | bytes 12292
  209.5 15.2 %copy-start.25 = (f32[1,512]{1,0:T(1,128)S(1)}, f32[1,512]{1,0:T(1,128)}, u32[]{:S(2)}) copy-start(f32[1,512]{1,0:T(1,128)} %get-tuple-element.43) | copy-start | bytes 6148
  209.5 15.8 %copy-start.27 = (s32[16]{0:T(128)S(1)}, s32[16]{0:T(128)}, u32[]{:S(2)}) copy-start(s32[16]{0:T(128)} %len_ref.3) | copy-start | bytes 196
  209.6 16.4 %copy-start.15 = (s32[16,2]{0,1:T(2,128)S(1)}, s32[16,2]{0,1:T(2,128)}, u32[]{:S(2)}) copy-start(s32[16,2]{0,1:T(2,128)} %copy-done.14) | copy-start | bytes 388
  209.6 16.4 %copy-start.21 = (f32[16,2]{0,1:T(2,128)S(1)}, f32[16,2]{0,1:T(2,128)}, u32[]{:S(2)}) copy-start(f32[16,2]{0,1:T(2,128)} %copy-done.20) | copy-start | bytes 388
  209.6 135.6 %reduce-scatter.3.cloned.1.call-start = ((), (), s32[]{:S(2)}) async-start(), calls=%async_computation.6 | async-start | bytes 2621440 | tf_op jit(solution)/shard_map/reduce_scatter | solution.py:414
  224.3 211.8 %all-reduce.4.cloned.1.call-start = ((), (), s32[]{:S(2)}) async-start(), calls=%async_computation.8 | async-start | bytes 8388608 | tf_op jit(solution)/shard_map/psum | solution.py:411
  234.4 1.3 copy-start.3
  238.3 30.7 %copy-start.9 = (f32[16,64]{0,1:T(8,128)S(1)}, f32[16,64]{0,1:T(8,128)}, u32[]{:S(2)}) copy-start(f32[16,64]{0,1:T(8,128)} %copy-done.8) | copy-start | bytes 12292
  258.6 10.3 %copy-start.1 = (f32[1024,512]{1,0:T(8,128)S(1)}, f32[1024,512]{1,0:T(8,128)}, u32[]{:S(2)}) copy-start(f32[1024,512]{1,0:T(8,128)} %get-tuple-element.29.h_ref) | copy-start | bytes 6291460
  258.6 10.3 %copy-start.4 = (f32[16,64,512]{2,0,1:T(8,128)S(1)}, f32[16,64,512]{2,0,1:T(8,128)}, u32[]{:S(2)}) copy-start(f32[16,64,512]{2,0,1:T(8,128)} %copy-done.3) | copy-start | bytes 6291460
  292.5 6.2 %copy-start.13 = (f32[16,2]{0,1:T(2,128)S(1)}, f32[16,2]{0,1:T(2,128)}, u32[]{:S(2)}) copy-start(f32[16,2]{0,1:T(2,128)} %copy-done.12) | copy-start | bytes 388
  292.5 6.2 %copy-start.17 = (f32[16]{0:T(128)S(1)}, f32[16]{0:T(128)}, u32[]{:S(2)}) copy-start(f32[16]{0:T(128)} %copy-done.16) | copy-start | bytes 196
  292.5 6.1 %copy-start.19 = (f32[16]{0:T(128)S(1)}, f32[16]{0:T(128)}, u32[]{:S(2)}) copy-start(f32[16]{0:T(128)} %copy-done.18) | copy-start | bytes 196
  292.5 6.2 %copy-start.24 = (s32[16]{0:T(128)S(1)}, s32[16]{0:T(128)}, u32[]{:S(2)}) copy-start(s32[16]{0:T(128)} %param.18) | copy-start | bytes 196
  292.6 6.3 %copy-start.22 = (f32[8,512]{1,0:T(8,128)S(1)}, f32[8,512]{1,0:T(8,128)}, u32[]{:S(2)}) copy-start(f32[8,512]{1,0:T(8,128)} %get-tuple-element.38) | copy-start | bytes 49156
  436.1 4.7 %copy-start.7 = (f32[512,512]{1,0:T(8,128)S(1)}, f32[512,512]{1,0:T(8,128)}, u32[]{:S(2)}) copy-start(f32[512,512]{1,0:T(8,128)} %get-tuple-element.115) | copy-start | bytes 3145732
  436.1 5.7 %copy-start.6 = (f32[512,512]{1,0:T(8,128)S(1)}, f32[512,512]{1,0:T(8,128)}, u32[]{:S(2)}) copy-start(f32[512,512]{1,0:T(8,128)} %get-tuple-element.116) | copy-start | bytes 3145732
Sparse Core Ops, SparseCore 0:
  158.9 46.1 reduce-scatter.4
  224.4 46.2 reduce-scatter.2
Sparse Core Ops, SparseCore 1:
  292.7 143.3 all-reduce.3

commit v2 on v1

--- a/solution.py
+++ b/solution.py
@@ -281,6 +281,372 @@
             transcendentals=0,
         ),
     )(lengths, tokens, cot, dm, hidden, act, q, k, v, ctx, prob, wq, wk, wv, wo, g1[None], g2[None])
+
+
+MESH_ID = pl.DeviceIdType.MESH
+CORE, NEAR, FAR = 1, 2, 4
+
+
+def plane_peer(relation):
+    me = lax.axis_index("expert")
+    bits = []
+    for bit in (CORE, NEAR, FAR):
+        value = (me // bit) % 2
+        bits.append((1 - value if relation & bit else value) * bit)
+    return bits[0] + bits[1] + bits[2]
+
+
+def remote(src, dst, sends, recvs, index, relation):
+    return pltpu.make_async_remote_copy(
+        src_ref=src,
+        dst_ref=dst,
+        send_sem=sends.at[index],
+        recv_sem=recvs.at[index],
+        device_id=(lax.axis_index("dp"), plane_peer(relation)),
+        device_id_type=MESH_ID,
+    )
+
+
+def plane_barrier():
+    barrier = pltpu.get_barrier_semaphore()
+    for relation in range(1, 8):
+        pl.semaphore_signal(
+            barrier,
+            inc=1,
+            device_id=(lax.axis_index("dp"), plane_peer(relation)),
+            device_id_type=MESH_ID,
+        )
+    pl.semaphore_wait(barrier, 7)
+
+
+def gather_copies(own, held, sends, recvs, base):
+    half = own.shape[0] // 2
+    low, high = pl.ds(0, half), pl.ds(half, half)
+    plan = [
+        (own.at[low], held[2].at[low], NEAR),
+        (own.at[high], held[4].at[high], FAR),
+        (own, held[1], CORE),
+        (own.at[high], held[2].at[high], NEAR),
+        (own.at[low], held[4].at[low], FAR),
+        (held[2].at[low], held[6].at[low], FAR),
+        (held[4].at[high], held[6].at[high], NEAR),
+        (held[2], held[3], CORE),
+        (held[4], held[5], CORE),
+        (held[6], held[7], CORE),
+    ]
+    return [
+        remote(src, dst, sends, recvs, base + place, relation)
+        for place, (src, dst, relation) in enumerate(plan)
+    ]
+
+
+def return_copies(parts, cores, sides, sends, recvs, base):
+    half = parts[0].shape[0] // 2
+    low, high = pl.ds(0, half), pl.ds(half, half)
+    plan = [
+        (parts[1], cores[0], CORE),
+        (parts[3], cores[2], CORE),
+        (parts[5], cores[4], CORE),
+        (parts[7], cores[6], CORE),
+        (parts[2].at[low], sides[0], NEAR),
+        (parts[6].at[low], sides[1], NEAR),
+        (parts[4].at[high], sides[2], FAR),
+        (parts[6].at[high], sides[3], FAR),
+        (parts[4].at[low], sides[4], FAR),
+        (parts[2].at[high], sides[5], NEAR),
+    ]
+    return [
+        remote(src, dst, sends, recvs, base + place, relation)
+        for place, (src, dst, relation) in enumerate(plan)
+    ]
+
+
+def add_into(target, start, other, count):
+    def one(i, carry):
+        total = target[start + i].astype(F32) + other[i].astype(F32)
+        target[start + i] = total.astype(BF)
+        return carry
+
+    lax.fori_loop(0, count, one, 0)
+
+
+def return_finish(parts, sides, back, out):
+    half = out.shape[0] // 2
+    back[4].wait_recv()
+    add_into(parts[0], 0, sides[0], half)
+    back[5].wait_recv()
+    add_into(parts[4], 0, sides[1], half)
+    back[8].start()
+    back[6].wait_recv()
+    add_into(parts[0], half, sides[2], half)
+    back[7].wait_recv()
+    add_into(parts[2], half, sides[3], half)
+    back[9].start()
+    back[8].wait_recv()
+    add_into(parts[0], 0, sides[4], half)
+    back[9].wait_recv()
+    add_into(parts[0], half, sides[5], half)
+
+    def one(i, carry):
+        out[i] = parts[0][i]
+        return carry
+
+    lax.fori_loop(0, out.shape[0], one, 0)
+    for copy in back:
+        copy.wait_send()
+
+
+GELU_A = 0.7978845608028654
+GELU_B = 0.044715
+
+
+def expert_kernel(
+    cap, tab, gates, m, cot, win, wback, dm_o, py_o, gin_o, gback_o, dg_o, *scratch
+):
+    sents, slot, width = m.shape
+    hidden = win.shape[1]
+    held_m = dict(zip(range(1, 8), scratch[0:7]))
+    held_c = dict(zip(range(1, 8), scratch[7:14]))
+    parts = dict(zip(range(8), scratch[14:22]))
+    cores = dict(zip((0, 2, 4, 6), scratch[22:26]))
+    sides = scratch[26:32]
+    xs, gs, dys, zs, dus, ys, dms, stage, dg_s, accb, acci, sends, recvs, local = scratch[32:]
+    me = lax.axis_index("expert")
+    tile = min(512, hidden)
+    entries = 2 * cap + sents
+
+    plane_barrier()
+    to_m = gather_copies(m, held_m, sends, recvs, 0)
+    to_c = gather_copies(cot, held_c, sends, recvs, 10)
+    back = return_copies(parts, cores, sides, sends, recvs, 20)
+    gates_back = {
+        r: remote(dg_s.at[r], dg_o.at[r], sends, recvs, 30 + r, r) for r in range(1, 8)
+    }
+    for place in (0, 1, 2):
+        to_m[place].start()
+        to_c[place].start()
+    for place in (3, 4):
+        to_m[place].start()
+        to_c[place].start()
+    accb[...] = jnp.zeros_like(accb)
+    acci[...] = jnp.zeros_like(acci)
+    place = lax.broadcasted_iota(jnp.int32, (slot, width), 0)
+    held_m[0], held_c[0] = m, cot
+
+    def arrive(*indices):
+        for index in indices:
+            to_m[index].wait_recv()
+            to_c[index].wait_recv()
+
+    def forward(*indices):
+        for index in indices:
+            to_m[index].start()
+            to_c[index].start()
+
+    def before(r):
+        if r == 1:
+            arrive(2)
+        if r == 2:
+            arrive(0, 1)
+            forward(5, 6)
+            arrive(3)
+            forward(7)
+            arrive(4)
+            forward(8)
+        if r == 3:
+            arrive(7)
+        if r == 5:
+            arrive(8)
+        if r == 6:
+            arrive(5, 6)
+            forward(9)
+        if r == 7:
+            arrive(9)
+        source = plane_peer(r)
+
+        def fetch(j, carry):
+            index = tab[source, me * entries + j]
+            length = tab[source, me * entries + cap + j]
+            gate = gates[source, me * cap + j]
+            xs[j] = held_m[r][index]
+            gt = jnp.where(place < length, held_c[r][index].astype(F32), 0.0)
+            gs[j] = gt.astype(BF)
+            dys[j] = (gt * gate).astype(BF)
+            return carry
+
+        lax.fori_loop(0, cap, fetch, 0)
+
+    def after(r):
+        source = plane_peer(r)
+        if r >= 2:
+            pltpu.make_async_copy(stage.at[r % 2], py_o.at[r - 2], local.at[r % 2]).wait()
+
+        def give(i, carry):
+            index = tab[source, me * entries + 2 * cap + i]
+            there = jnp.maximum(index, 0)
+            gate = gates[source, me * cap + there]
+            hit = (index >= 0).astype(F32)
+            parts[r][i] = (dms[there].astype(F32) * hit).astype(BF)
+            stage[r % 2, i] = (ys[there].astype(F32) * (hit * gate)).astype(BF)
+            return carry
+
+        lax.fori_loop(0, sents, give, 0)
+        pltpu.make_async_copy(stage.at[r % 2], py_o.at[r], local.at[r % 2]).start()
+
+        def dots(j, carry):
+            product = ys[j].astype(F32) * gs[j].astype(F32)
+            total = jnp.sum(jnp.sum(product, axis=0, keepdims=True), axis=1, keepdims=True)
+            if r == 0:
+                dg_o[0, pl.ds(j, 1)] = jnp.broadcast_to(total, (1, 128))
+            else:
+                dg_s[r, pl.ds(j, 1)] = jnp.broadcast_to(total, (1, 128))
+            return carry
+
+        lax.fori_loop(0, cap, dots, 0)
+        if r > 0:
+            gates_back[r].start()
+        if r % 2 == 1:
+            back[r // 2].start()
+        if r == 4:
+            back[1].wait_recv()
+            add_into(parts[2], 0, cores[2], sents)
+            back[4].start()
+        if r == 6:
+            back[2].wait_recv()
+            add_into(parts[4], 0, cores[4], sents)
+            back[6].start()
+        if r == 7:
+            back[3].wait_recv()
+            add_into(parts[6], 0, cores[6], sents)
+            back[5].start()
+            back[7].start()
+            back[0].wait_recv()
+            add_into(parts[0], 0, cores[0], sents)
+
+    def chunk(t, carry):
+        for r in range(8):
+            pl.when(t == r)(functools.partial(before, r))
+        x = xs[...].reshape(cap * slot, width)
+        dy = dys[...].reshape(cap * slot, width)
+
+        def inner(f, carry):
+            cols = pl.ds(pl.multiple_of(f * tile, tile), tile)
+            u = mm(x, win[:, cols])
+            square = u * u
+            th = jnp.tanh(u * (GELU_A + GELU_A * GELU_B * square))
+            cdf = 0.5 + 0.5 * th
+            slope = cdf + (0.5 * u) * (1.0 - th * th) * (GELU_A + 3 * GELU_A * GELU_B * square)
+            z = (u * cdf).astype(BF)
+            zs[:, cols] = z
+            dz = mm(dy, wback[cols, :], 1, 1)
+            du = (dz * slope).astype(BF)
+            dus[:, cols] = du
+            accb[cols, :] += mm(z, dy, 0, 0)
+            acci[:, cols] += mm(x, du, 0, 0)
+            return carry
+
+        lax.fori_loop(0, hidden // tile, inner, 0)
+        ys[...] = mm(zs[...], wback[...]).astype(BF).reshape(cap, slot, width)
+        dms[...] = mm(dus[...], win[...], 1, 1).astype(BF).reshape(cap, slot, width)
+        for r in range(8):
+            pl.when(t == r)(functools.partial(after, r))
+        return carry
+
+    lax.fori_loop(0, 8, chunk, 0)
+    gin_o[...] = acci[...].astype(BF)
+    gback_o[...] = accb[...].astype(BF)
+    return_finish(parts, sides, back, dm_o)
+    for r in range(1, 8):
+        gates_back[r].wait()
+    for index in range(10):
+        to_m[index].wait_send()
+        to_c[index].wait_send()
+    for r in (6, 7):
+        pltpu.make_async_copy(stage.at[r % 2], py_o.at[r], local.at[r % 2]).wait()
+
+
+def expert_exchange(tab, gates, m, cot, win, wback, cap):
+    sents, slot, width = m.shape
+    hidden = win.shape[1]
+    vm = pl.BlockSpec(memory_space=VM)
+    sm = pl.BlockSpec(memory_space=pltpu.SMEM)
+    shape = jax.ShapeDtypeStruct
+    cube = (sents, slot, width)
+    rows = cap * slot
+    return pl.pallas_call(
+        functools.partial(expert_kernel, cap),
+        in_specs=[sm, sm, vm, vm, vm, vm],
+        out_specs=[vm, pl.BlockSpec(memory_space=pl.ANY), vm, vm, vm],
+        out_shape=[
+            shape(cube, BF),
+            shape((8,) + cube, BF),
+            shape((width, hidden), BF),
+            shape((hidden, width), BF),
+            shape((8, cap, 128), F32),
+        ],
+        scratch_shapes=[VM(cube, BF)] * (14 + 8 + 4)
+        + [VM((sents // 2, slot, width), BF)] * 6
+        + [VM((cap, slot, width), BF)] * 3
+        + [VM((rows, hidden), BF)] * 2
+        + [VM((cap, slot, width), BF)] * 2
+        + [VM((2,) + cube, BF), VM((8, cap, 128), F32)]
+        + [VM((hidden, width), F32), VM((width, hidden), F32)]
+        + [
+            pltpu.SemaphoreType.DMA((38,)),
+            pltpu.SemaphoreType.DMA((38,)),
+            pltpu.SemaphoreType.DMA((2,)),
+        ],
+        compiler_params=pltpu.CompilerParams(
+            collective_id=1, has_side_effects=True, vmem_limit_bytes=63 * 2**20
+        ),
+        cost_estimate=pl.CostEstimate(
+            flops=12 * 8 * rows * width * hidden, bytes_accessed=40 * 2**20, transcendentals=0
+        ),
+    )(tab, gates, m, cot, win, wback)
+
+
+def combine_kernel(py, out, *scratch):
+    parts = dict(zip(range(8), scratch[0:8]))
+    cores = dict(zip((0, 2, 4, 6), scratch[8:12]))
+    sides = scratch[12:18]
+    sends, recvs, local = scratch[18:]
+    sents = out.shape[0]
+    loads = [pltpu.make_async_copy(py.at[r], parts[r], local.at[r]) for r in range(8)]
+    for load in loads:
+        load.start()
+    plane_barrier()
+    back = return_copies(parts, cores, sides, sends, recvs, 0)
+    for r in (1, 3, 5, 7):
+        loads[r].wait()
+        back[r // 2].start()
+    for r, starts in ((6, (5, 7)), (2, (4,)), (4, (6,)), (0, ())):
+        loads[r].wait()
+        back[r // 2].wait_recv()
+        add_into(parts[r], 0, cores[r], sents)
+        for index in starts:
+            back[index].start()
+    return_finish(parts, sides, back, out)
+
+
+def combine_exchange(py):
+    cube = py.shape[1:]
+    return pl.pallas_call(
+        combine_kernel,
+        in_specs=[pl.BlockSpec(memory_space=pl.ANY)],
+        out_specs=pl.BlockSpec(memory_space=VM),
+        out_shape=jax.ShapeDtypeStruct(cube, BF),
+        scratch_shapes=[VM(cube, BF)] * 12
+        + [VM((cube[0] // 2,) + cube[1:], BF)] * 6
+        + [
+            pltpu.SemaphoreType.DMA((10,)),
+            pltpu.SemaphoreType.DMA((10,)),
+            pltpu.SemaphoreType.DMA((8,)),
+        ],
+        compiler_params=pltpu.CompilerParams(
+            collective_id=2, has_side_effects=True, vmem_limit_bytes=40 * 2**20
+        ),
+        cost_estimate=pl.CostEstimate(flops=0, bytes_accessed=16 * 2**20, transcendentals=0),
+    )(py)
 
 
 def local(
@@ -436,6 +802,134 @@
     )
 
 
+def local_plane(
+    tokens,
+    lengths,
+    tasks,
+    routes,
+    gate_table,
+    ln1_gain,
+    ln1_bias,
+    ln2_gain,
+    ln2_bias,
+    w_query,
+    w_key,
+    w_value,
+    w_out,
+    w_in,
+    w_back,
+    cotangent,
+):
+    sents, slot, width = tokens.shape
+    heads = HEADS
+    experts = gate_table.shape[1]
+    ntasks = routes.shape[0]
+    capacity = max(1, 4 * sents // experts)
+    task_hot = (tasks[:, None] == jnp.arange(ntasks)[None, :]).astype(jnp.int32)
+    chosen = jnp.sum(task_hot[:, :, None] * routes[None, :, :], axis=1)
+    flat = chosen.reshape(-1)
+    order = jnp.arange(2 * sents)
+    earlier = (flat[:, None] == flat[None, :]) & (order[None, :] < order[:, None])
+    rank = jnp.sum(earlier.astype(jnp.int32), axis=1)
+    slot_id = flat * capacity + rank
+    placed = rank < capacity
+    expert_hot = (chosen[:, :, None] == jnp.arange(experts)[None, None, :]).astype(jnp.float32)
+    valid = (jnp.arange(slot)[None, :] < lengths[:, None]).astype(jnp.float32)
+    mask3 = valid[:, :, None]
+    act, query, keyed, valued, context, prob, hidden, mixed, attn_sum = attention_forward(
+        tokens, lengths, w_query, w_key, w_value, w_out,
+        ln1_gain, ln1_bias, ln2_gain, ln2_bias, heads,
+    )
+    hidden_res = hidden.reshape(sents, slot, width)
+    table_rows = jnp.dot(task_hot.astype(jnp.float32), gate_table, precision=lax.Precision.HIGHEST)
+    picked = jnp.sum(expert_hot * table_rows[:, None, :], axis=-1)
+    gate_values = jax.nn.softmax(picked, axis=-1)
+    hits = (
+        (jnp.arange(experts * capacity)[:, None] == slot_id[None, :]) & placed[None, :]
+    ).astype(jnp.float32)
+    per_copy = jnp.stack(
+        [
+            (order // 2).astype(jnp.float32),
+            jnp.repeat(lengths, 2).astype(jnp.float32),
+            gate_values.reshape(-1),
+        ]
+    )
+    per_slot = jnp.sum(hits[None] * per_copy[:, None, :], axis=-1).reshape(3, experts, capacity)
+    taken = (flat[None, :] == jnp.arange(experts)[:, None]) & placed[None, :]
+    ranks = jnp.sum(
+        (taken * (rank + 1)[None, :]).reshape(experts, sents, 2), axis=-1
+    ).astype(jnp.float32)
+    sent_table = jnp.concatenate([per_slot[0], per_slot[1], ranks - 1.0, per_slot[2]], axis=1)
+    table = lax.all_gather(sent_table, "expert")
+    entries = 2 * capacity + sents
+    places = table[:, :, :entries].astype(jnp.int32).reshape(experts, -1)
+    gate_slots = table[:, :, entries:].reshape(experts, -1)
+    dmixed, parts_back, in_local, back_local, slot_dots = expert_exchange(
+        places, gate_slots, mixed, cotangent, w_in[0], w_back[0], capacity
+    )
+    expert_mixture = combine_exchange(parts_back).astype(jnp.float32)
+    total = mask3 * (hidden_res + expert_mixture)
+    output = total.astype(jnp.bfloat16)
+    stats_local = jnp.stack(
+        [
+            jnp.sum(total * total),
+            jnp.sum(attn_sum),
+            jnp.sum(mask3 * expert_mixture * expert_mixture),
+            jnp.sum(valid),
+        ]
+    )
+    stat_totals = lax.psum(stats_local, ("dp", "expert"))
+    me = lax.axis_index("expert")
+    dots_here = jnp.take(slot_dots[:, :, 0], me ^ jnp.arange(experts), axis=0).reshape(-1)
+    gate_dot = jnp.sum(hits * dots_here[:, None], axis=0).reshape(sents, 2)
+    dpicked = gate_values * (gate_dot - jnp.sum(gate_values * gate_dot, axis=-1, keepdims=True))
+    dlogits = jnp.sum(expert_hot * dpicked[:, :, None], axis=1)
+    table_grad = jnp.dot(task_hot.T.astype(jnp.float32), dlogits, precision=lax.Precision.HIGHEST)
+    input_grad, wq_grad, wk_grad, wv_grad, wout_grad, norms = attention_backward(
+        lengths, tokens, cotangent, dmixed, hidden, act, query, keyed, valued, context, prob,
+        w_query, w_key, w_value, w_out, ln1_gain, ln2_gain, heads,
+    )
+    gain1_grad, bias1_grad, gain2_grad, bias2_grad = norms[0], norms[1], norms[2], norms[3]
+    members = (
+        wq_grad,
+        wk_grad,
+        wv_grad,
+        wout_grad,
+        gain1_grad,
+        bias1_grad,
+        gain2_grad,
+        bias2_grad,
+        table_grad,
+    )
+    members = members + ()
+    summed = lax.psum(members, ("dp", "expert"))
+    rms = jnp.sqrt(stat_totals[0:3] / (stat_totals[3] * width))
+    in_share, back_share = (
+        lax.psum_scatter(
+            in_local, "dp", scatter_dimension=0, tiled=True
+        ).astype(jnp.float32),
+        lax.psum_scatter(
+            back_local, "dp", scatter_dimension=0, tiled=True
+        ).astype(jnp.float32),
+    )
+    return (
+        output,
+        input_grad,
+        summed[8],
+        summed[4],
+        summed[5],
+        summed[6],
+        summed[7],
+        summed[0],
+        summed[1],
+        summed[2],
+        summed[3],
+        in_share[None],
+        back_share[None],
+        rms,
+    )
+
+
 def solution(mesh):
     in_specs = (
         P(("dp", "expert"), None, None),
@@ -471,4 +965,6 @@
         P("expert", "dp", None),
         P(),
     )
-    return jax.shard_map(local, mesh=mesh, in_specs=in_specs, out_specs=out_specs, check_vma=False)
+    plane = dict(mesh.shape)["expert"]
+    body = local_plane if plane == 2 * 2 * 2 else local
+    return jax.shard_map(body, mesh=mesh, in_specs=in_specs, out_specs=out_specs, check_vma=False)

time: 456 us -> 405 us (0.89); the launches traced: 450 us -> 405 us
  Pallas kernels: 34.3 us -> 235 us
  matrix products: 132 us -> 0.99 us
  waiting for transfers between devices: 157 us -> 74.6 us
  starting transfers between devices: 20 us -> 0.3 us
  local copies, waits for them, and re-layouts: 32.4 us -> 13.5 us
  blocking collectives: 40.8 us -> 50.3 us
    pallas_call x0 -> x2, Pallas kernels: none -> 201 us  [the longest x1 147 us: expert_exchange(): pl.pallas_call(functools.partial(expert_kernel, cap), in_specs=[sm, sm, v...]
    dot_general x12 -> x2, matrix products: 132 us -> 0.99 us  [the longest x1 0.85 us: local_plane(): jnp.dot(task_hot.astype(jnp.float32), gate_table, precision=lax.Precision...]
    all_to_all x4 -> x0, waiting for transfers between devices: 68.4 us -> none  [the longest x1 36.4 us: local(): lax.all_to_all(outgoing, 'expert', split_axis=0, concat_axis=0, tiled=True)]
    all_to_all x4 -> x0, starting transfers between devices: 19.5 us -> none  [the longest x1 5.55 us: local(): lax.all_to_all(outgoing, 'expert', split_axis=0, concat_axis=0, tiled=True)]
    psum x1, waiting for transfers between devices: 88.8 us -> 73.8 us  [local_plane(): summed = lax.psum(members, ('dp', 'expert'))]
    all_gather x0 -> x1, blocking collectives: none -> 10.5 us  [local_plane(): table = lax.all_gather(sent_table, 'expert')]
    unnamed x72 -> x26, local copies, waits for them, and re-layouts: 16.8 us -> 9.42 us
    reshape x3 -> x5, local copies, waits for them, and re-layouts: 7.15 us -> 1.61 us  [the longest x1 0.68 us: local_plane(): places = table[:, :, :entries].astype(jnp.int32).reshape(experts, -1)]
  transfers between devices with their start and end apart: 7 -> 3, of which waited for: 4 -> 1; matrix products, arithmetic and copies ran while one was open for 36% -> 3% of each run, Pallas kernels for 5% -> 19%
where the time goes in v2:
time: 405 us
  Pallas kernels  235 us (58%)
  waiting for transfers between devices  74.6 us (18%)
  blocking collectives  50.3 us (12%)
  between operations  16.3 us (4%)
  other arithmetic  14.1 us (3%)
  local copies, waits for them, and re-layouts  13.5 us (3%)
    pallas_call x1, Pallas kernels, expert_exchange(): pl.pallas_call(functools.partial(expert_kernel, cap), in_specs=[sm, sm, v...  147 us
    psum x1, waiting for transfers between devices, local_plane(): summed = lax.psum(members, ('dp', 'expert'))  73.8 us
    pallas_call x1, Pallas kernels, combine_exchange(): pl.pallas_call(combine_kernel, in_specs=[pl.BlockSpec(memory_space=pl.ANY...  54 us
    psum x1, blocking collectives, local_plane(): summed = lax.psum(members, ('dp', 'expert'))  39.8 us
    pallas_call x1, Pallas kernels, attention_backward(): pl.pallas_call(functools.partial(attention_backward_kernel, heads), grid=...  21.1 us
    pallas_call x1, Pallas kernels, attention_forward(): pl.pallas_call(functools.partial(attention_forward_kernel, heads), grid=(...  13 us
    all_gather x1, blocking collectives, local_plane(): table = lax.all_gather(sent_table, 'expert')  10.5 us
    unnamed x26, local copies, waits for them, and re-layouts  9.42 us
  transfers between devices with their start and end apart: 3, of which 1 were waited for; matrix products, arithmetic and copies ran while one was open for 3% of the time, Pallas kernels for 19%

profile of v2, /device:TPU:0, one launch (start us, length us, event | category | flops | bytes accessed | tf_op | source)
XLA Modules:
  0.0 405.0 jit_solution(14574568093796205168)
XLA Ops:
  8.0 0.0 copy-start
  8.0 0.0 reduce-scatter.5.cloned.1.call-start
  8.1 0.7 fusion.13
  8.8 0.8 multiply_reduce_fusion.2
  9.6 0.1 copy.34
  9.7 0.1 reshape.352
  9.8 0.2 convert_reduce_fusion
  10.0 0.9 fusion.10
  10.9 0.1 copy.35
  11.0 0.1 div.37
  11.1 0.7 convert_element_type.78
  11.8 0.1 broadcast_in_dim.34
  11.9 0.1 convert_element_type.79
  12.0 0.1 lt.63
  12.1 0.1 fusion.7
  12.2 0.1 multiply_reduce_fusion.1
  12.3 0.1 squeeze.31
  12.3 0.1 squeeze.32
  12.4 0.1 squeeze.33
  12.5 0.1 add.71
  12.6 0.1 copy.37
  12.7 0.1 copy.36
  12.8 0.1 pad_maximum_fusion
  12.9 10.5 %all-gather = f32[64,40]{1,0:T(8,128)S(1)} all-gather(f32[8,40]{1,0:T(8,128)S(1)} %pad_maximum_fusion), channel_id=2, replica_groups=mesh['dp'=4,'expert'=8] {'expert'}, dimensions={0}, use_global_device_ids=true | all-gather | bytes 11520 | tf_op jit(solution)/shard_map/all_gather | solution.py:863
  23.4 0.1 slice.54
  23.5 0.7 reshape.353.tab
  24.2 0.7 reshape.354.gates
  24.8 13.0 %shard_map.263 = (bf16[1024,512]{1,0:T(8,128)(2,1)}, bf16[1024,512]{1,0:T(8,128)(2,1)}, bf16[1024,512]{1,0:T(8,128)(2,1)}, bf16[1024,512]{1,0:T(8,128)(2,1)}, bf...) custom-call(s32[16]{0:T(128)} %len_ref.3, ...), custom_call_target="tpu_custom_call" | custom-call | flops 2281701376 | bytes 8388608 | tf_op jit(solution)/shard_map/pallas_call | solution.py:138
  37.9 146.7 %shard_map.264 = (bf16[16,64,512]{2,1,0:T(8,128)(2,1)}, bf16[8,16,64,512]{3,2,1,0:T(8,128)(2,1)}, bf16[512,2048]{1,0:T(8,128)(2,1)}, bf16[2048,512]{1,0:T(8,128)(2,1)}, f32[8,8,128]{2,1,0:T(8,128)}) custom-call(s32[8,256]{1,0:T(8,128)} %reshape.353.tab, f32[8,64]{1,0:T(8,128)} %reshape.354.gates, bf16[16,64,512]{2,1,0:T(8,128)(2,1)} %get-tuple-element.35.m, ...), custom_call_target="tpu_custom_call" | custom-call | flops 51539607552 | bytes 41943040 | tf_op jit(solution)/shard_map/pallas_call | solution.py:576
  184.5 0.0 reduce-scatter.5.cloned.1.call-update
  184.6 0.0 reduce-scatter.3.cloned.1.call-start
  184.6 0.7 reduce-scatter.3.cloned.1.call-update
  185.3 0.2 all-reduce.4.cloned.1.call-start
  185.5 21.1 %shard_map.266 = (bf16[16,64,512]{2,1,0:T(8,128)(2,1)}, f32[512,512]{1,0:T(8,128)}, f32[512,512]{1,0:T(8,128)}, f32[512,512]{1,0:T(8,128)}, f32[512,512]{1,0:T(8,128)}, /*index=5*/f32[8,512]{1,0:T(8,128)}) custom-call(s32[16]{0:T(128)} %len_ref.3, bf16[16,64,512]{2,1,0:T(8,128)(2,1)} %x_ref.3, bf16[16,64,512]{2,1,0:T(8,128)(2,1)} %cot_ref.1, ...), custom_call_target="tpu_custom_call" | custom-call | flops 4630511616 | bytes 12582912 | tf_op jit(solution)/shard_map/pallas_call | solution.py:263
  206.7 0.0 copy-start.10
  206.7 0.0 all-reduce.4.cloned.1.call-update
  206.7 0.6 copy-done.10
  207.3 0.1 fusion.12
  207.4 3.4 copy-done.1
  210.9 54.0 %shard_map.265 = bf16[16,64,512]{2,1,0:T(8,128)(2,1)S(1)} custom-call(bf16[8,16,64,512]{3,2,1,0:T(8,128)(2,1)S(1)} %copy-done.1), custom_call_target="tpu_custom_call" | custom-call | bytes 16777216 | tf_op jit(solution)/shard_map/pallas_call | solution.py:633
  264.9 0.1 slice_reduce_fusion
  265.0 0.6 gather_fusion
  265.5 0.1 broadcast_select_fusion
  265.6 0.1 select_n.43
  265.7 0.2 select_reduce_fusion
  265.9 0.1 reshape.355
  266.0 0.1 copy.39
  266.0 0.6 reduce_sum.127
  266.7 2.3 multiply_reduce_fusion
  268.9 0.7 fusion.16
  269.6 2.7 pad_maximum_fusion.2
  272.3 0.1 fusion.3
  272.5 0.0 copy-done.7
  272.5 39.8 %all-reduce = (f32[30,8]{0,1:T(8,128)}, f32[512]{0:T(512)}, f32[512]{0:T(512)}, f32[512]{0:T(512)}, f32[512]{0:T(512)}, /*index=5*/f32[4]{0:T(128)S(1)}) all-reduce(f32[30,8]{0,1:T(8,128)S(1)} %fusion.3, f32[512]{0:T(512)S(1)} %bitcast.34, f32[512]{0:T(512)S(1)} %bitcast.33, ...), channel_id=1, replica_groups=mesh['dp'=4,'expert'=8] {'dp','expert'}, use_global_device_ids=true, to_apply=%region_10.11 | all-reduce | flops 2292 | bytes 18336 | tf_op jit(solution)/shard_map/psum | solution.py:905
  312.3 0.6 slice.50
  313.5 0.5 divide_sqrt_fusion
  314.1 2.1 bitcast_convert_fusion
  316.2 2.1 bitcast_convert_fusion.1
  318.3 73.8 %all-reduce.4.cloned.1.call-done = (f32[512,512]{1,0:T(8,128)}, f32[512,512]{1,0:T(8,128)}, f32[512,512]{1,0:T(8,128)}, f32[512,512]{1,0:T(8,128)}) async-done(((f32[512,512]{1,0:T(8,128)}, f32[512,512]{1,0:T(8,128)}, f32[512,512]{1,0:T(8,128)}, f32[512,512]{1,0:T(8,128)}), (f32[512,512]{1,0:T(8,128)}, f32[512,512]{1,0:T(8,128)}, f32[512,512]{1,0:T(8,128)}, ...) | async-done | bytes 4194320 | tf_op jit(solution)/shard_map/psum | solution.py:905
  392.2 2.4 copy.44
  394.6 0.0 copy-done.5
  394.6 1.0 copy.45
  395.6 1.0 copy.46
  396.6 1.0 copy.47
  (37 shorter events, 0.3 us)
Async XLA Ops:
  8.0 2.0 copy-start
  8.0 306.0 %reduce-scatter.5.cloned.1.call-start = ((), (), s32[]{:S(2)}) async-start(), calls=%async_computation.3 | async-start | bytes 2621440 | tf_op jit(solution)/shard_map/reduce_scatter | solution.py:911
  184.6 131.7 %reduce-scatter.3.cloned.1.call-start = ((), (), s32[]{:S(2)}) async-start(), calls=%async_computation.2 | async-start | bytes 2621440 | tf_op jit(solution)/shard_map/reduce_scatter | solution.py:908
  185.3 206.9 %all-reduce.4.cloned.1.call-start = ((), (), s32[]{:S(2)}) async-start(), calls=%async_computation.4 | async-start | bytes 8388608 | tf_op jit(solution)/shard_map/psum | solution.py:905
  206.7 0.7 copy-start.10
  207.4 3.4 copy-start.1
  210.8 54.0 %copy-start.6 = (f32[8,8,128]{2,1,0:T(8,128)S(1)}, f32[8,8,128]{2,1,0:T(8,128)}, u32[]{:S(2)}) copy-start(f32[8,8,128]{2,1,0:T(8,128)} %get-tuple-element.45) | copy-start | bytes 98308
  210.8 55.2 %copy-start.9 = (f32[1,512]{1,0:T(1,128)S(1)}, f32[1,512]{1,0:T(1,128)}, u32[]{:S(2)}) copy-start(f32[1,512]{1,0:T(1,128)} %get-tuple-element.53) | copy-start | bytes 6148
  210.9 55.8 %copy-start.2 = (f32[1024,512]{1,0:T(8,128)S(1)}, f32[1024,512]{1,0:T(8,128)}, u32[]{:S(2)}) copy-start(f32[1024,512]{1,0:T(8,128)} %get-tuple-element.34.h_ref) | copy-start | bytes 6291460
  266.7 5.7 %copy-start.8 = (s32[16]{0:T(128)S(1)}, s32[16]{0:T(128)}, u32[]{:S(2)}) copy-start(s32[16]{0:T(128)} %param.18) | copy-start | bytes 196
  266.7 5.8 %copy-start.7 = (f32[8,512]{1,0:T(8,128)S(1)}, f32[8,512]{1,0:T(8,128)}, u32[]{:S(2)}) copy-start(f32[8,512]{1,0:T(8,128)} %get-tuple-element.46) | copy-start | bytes 49156
  392.2 2.4 copy-start.5
  392.2 3.4 copy-start.4
  394.6 1.9 copy-start.3
Sparse Core Ops, SparseCore 0:
  184.7 47.0 reduce-scatter.4
  234.2 48.9 reduce-scatter.2
Sparse Core Ops, SparseCore 1:
  206.8 185.3 all-reduce.3

commit v3 on v2

--- a/solution.py
+++ b/solution.py
@@ -605,48 +605,530 @@
     )(tab, gates, m, cot, win, wback)
 
 
-def combine_kernel(py, out, *scratch):
-    parts = dict(zip(range(8), scratch[0:8]))
-    cores = dict(zip((0, 2, 4, 6), scratch[8:12]))
-    sides = scratch[12:18]
-    sends, recvs, local = scratch[18:]
-    sents = out.shape[0]
-    loads = [pltpu.make_async_copy(py.at[r], parts[r], local.at[r]) for r in range(8)]
-    for load in loads:
+def line_peer(offset, depth):
+    return lax.rem(lax.axis_index("dp") + offset, depth)
+
+
+def along(src, dst, sends, recvs, index, offset, depth):
+    return pltpu.make_async_remote_copy(
+        src_ref=src,
+        dst_ref=dst,
+        send_sem=sends.at[index],
+        recv_sem=recvs.at[index],
+        device_id=(line_peer(offset, depth), lax.axis_index("expert")),
+        device_id_type=MESH_ID,
+    )
+
+
+class Reduction:
+    def __init__(self, depth, value, wide, core_r, plane_r, line_s, line_r, final, sems, base):
+        self.depth, self.value, self.wide, self.final = depth, value, wide, final
+        self.core_r, self.plane_r, self.line_s, self.line_r = core_r, plane_r, line_s, line_r
+        sends, recvs = sems
+        me = lax.axis_index("expert")
+        z = lax.axis_index("dp")
+        core = me % 2
+        self.half = value.shape[0] // 2
+        self.quarter = self.half // 4
+        self.share = self.quarter // depth
+        self.mine = core * self.half
+        self.other = (1 - core) * self.half
+        self.block = self.mine + (me // 2) * self.quarter
+        self.own = self.block + z * self.share
+        self.to_core = remote(wide, core_r, sends, recvs, base, CORE)
+        self.to_plane = []
+        self.from_plane = []
+        for place, relation in enumerate((2, 4, 6)):
+            rows = pl.ds((plane_peer(relation) // 2) * self.quarter, self.quarter)
+            self.to_plane.append(
+                remote(wide.at[rows], plane_r.at[place], sends, recvs, base + 1 + place, relation)
+            )
+        self.to_line = []
+        for offset in range(1, depth):
+            rows = pl.ds(line_peer(offset, depth) * self.share, self.share)
+            self.to_line.append(
+                along(
+                    line_s.at[rows], line_r.at[offset - 1], sends, recvs, base + 3 + offset,
+                    offset, depth,
+                )
+            )
+        after = base + 3 + depth
+        rows = final.at[pl.ds(self.own, self.share)]
+        self.back_line = [
+            along(rows, rows, sends, recvs, after + offset - 1, offset, depth)
+            for offset in range(1, depth)
+        ]
+        after = after + depth - 1
+        rows = final.at[pl.ds(self.block, self.quarter)]
+        self.back_plane = [
+            remote(rows, rows, sends, recvs, after + place, relation)
+            for place, relation in enumerate((2, 4, 6))
+        ]
+        rows = final.at[pl.ds(self.mine, self.half)]
+        self.back_core = remote(rows, rows, sends, recvs, after + 3, CORE)
+
+    @staticmethod
+    def semaphores(depth):
+        return 2 * depth + 6
+
+    def send_core(self):
+        self.wide[...] = self.value[pl.ds(self.other, self.half), :].astype(BF)
+        self.to_core.start()
+
+    def send_plane(self):
+        self.to_core.wait()
+        rows = pl.ds(self.mine, self.half)
+        total = self.value[rows, :] + self.core_r[...].astype(F32)
+        self.value[rows, :] = total
+        self.wide[...] = total.astype(BF)
+        for copy in self.to_plane:
+            copy.start()
+
+    def send_line(self):
+        for copy in self.to_plane:
+            copy.wait()
+        rows = pl.ds(self.block, self.quarter)
+        total = self.value[rows, :]
+        for place in range(3):
+            total = total + self.plane_r[place].astype(F32)
+        self.value[rows, :] = total
+        self.line_s[...] = total.astype(BF)
+        for copy in self.to_line:
+            copy.start()
+
+    def send_back_line(self):
+        for copy in self.to_line:
+            copy.wait()
+        rows = pl.ds(self.own, self.share)
+        total = self.value[rows, :]
+        for offset in range(1, self.depth):
+            total = total + self.line_r[offset - 1].astype(F32)
+        self.final[rows, :] = total.astype(BF)
+        for copy in self.back_line:
+            copy.start()
+
+    def send_back_plane(self):
+        for copy in self.back_line:
+            copy.wait()
+        for copy in self.back_plane:
+            copy.start()
+
+    def send_back_core(self):
+        for copy in self.back_plane:
+            copy.wait()
+        self.back_core.start()
+
+    def finish(self):
+        self.back_core.wait()
+
+
+def backward_kernel(
+    heads, depth, len_ref, x_ref, cot_ref, dm_ref, h_ref, act, q, k, v, ctx, p_ref,
+    wq, wk, wv, wo, g1, g2, small_in, py, gin, gback,
+    ig_o, out_o, fin_o, fin_0, fin_1, gin_o, gback_o, small_o, *scratch
+):
+    sents, slot, width = x_ref.shape
+    total_rows = sents * slot
+    head = width // heads
+    group = max(1, min(heads, 256 // head))
+    span = group * head
+    scale = head ** -0.5
+    count = 4 if sents % 4 == 0 else 1
+    rows_per = count * slot
+    z = lax.axis_index("dp")
+    parts = {0: scratch[0], 2: scratch[1], 4: scratch[2], 6: scratch[3]}
+    cores = dict(zip((0, 2, 4, 6), scratch[4:8]))
+    sides = scratch[8:14]
+    dh_s, da_s, dctx_s, dq_s, dk_s, dv_s = scratch[14:20]
+    red = scratch[20:38]
+    line_in, line_back, extra_in, extra_back = scratch[38:42]
+    small, small_core, small_plane, small_line = scratch[42:46]
+    gin_s, gback_s = scratch[46:48]
+    sends, recvs, local = scratch[48:]
+    sems = (sends, recvs)
+    grad_loads = [
+        pltpu.make_async_copy(gin, gin_s, local.at[4]),
+        pltpu.make_async_copy(gback, gback_s, local.at[5]),
+    ]
+    for load in grad_loads:
         load.start()
-    plane_barrier()
-    back = return_copies(parts, cores, sides, sends, recvs, 0)
+
+    loads = {
+        r: pltpu.make_async_copy(py.at[r], parts[r], local.at[r // 2]) for r in (0, 2, 4, 6)
+    }
+    for r in (6, 2, 4, 0):
+        loads[r].start()
+    barrier = pltpu.get_barrier_semaphore()
+    for relation in range(1, 8):
+        pl.semaphore_signal(
+            barrier, inc=1, device_id=(z, plane_peer(relation)), device_id_type=MESH_ID
+        )
+    for offset in range(1, depth):
+        pl.semaphore_signal(
+            barrier,
+            inc=1,
+            device_id=(line_peer(offset, depth), lax.axis_index("expert")),
+            device_id_type=MESH_ID,
+        )
+    pl.semaphore_wait(barrier, 6 + depth)
+
+    all_parts = dict(parts)
     for r in (1, 3, 5, 7):
-        loads[r].wait()
+        all_parts[r] = py.at[r]
+    back = return_copies(all_parts, cores, sides, sends, recvs, 0)
+    for r in (7, 3, 5, 1):
         back[r // 2].start()
-    for r, starts in ((6, (5, 7)), (2, (4,)), (4, (6,)), (0, ())):
+
+    base = 10
+    in_rows = gin.shape[0] // depth
+    back_rows = gback.shape[0] // depth
+
+    def line_piece(s, array, right, last):
+        offset = 1 if right else depth - 1
+        index = base + (0 if right else 2 * depth) + 2 * s + array
+        share, source = ((in_rows, gin_s), (back_rows, gback_s))[array]
+        into = (line_in, line_back)[array].at[s]
+        if last and not right:
+            into = (extra_in, extra_back)[array]
+        here = source.at[pl.ds(s * share, share)]
+        return along(here, into, sends, recvs, index, offset, depth)
+
+    def add_piece(s, array):
+        share, source = ((in_rows, gin_s), (back_rows, gback_s))[array]
+        other = (line_in, line_back)[array]
+        here = pl.ds(s * share, share)
+        source[here, :] = (source[here, :].astype(F32) + other[s].astype(F32)).astype(BF)
+
+    def pieces(right):
+        order = range(depth - 1, 0, -1) if right else range(depth - 1)
+        return [(s, array) for s in order for array in (0, 1)]
+
+    def start_piece(s, array, right):
+        if right:
+            line_piece(s, array, True, False).start()
+            return
+        near = z == s + 1
+
+        @pl.when(near)
+        def _():
+            line_piece(s, array, False, True).start()
+
+        @pl.when(jnp.logical_not(near))
+        def _():
+            line_piece(s, array, False, False).start()
+
+    def line_service(t, ahead=1):
+        for right in (True, False):
+            every = pieces(right)
+            edge = 0 if right else depth - 1
+            opening = range(0, 1 + ahead) if t == 0 else range(t + ahead, t + ahead + 1)
+
+            @pl.when(z == edge)
+            def _():
+                for number in opening:
+                    if number < len(every):
+                        start_piece(*every[number], right)
+
+            for number, (s, array) in enumerate(every):
+                hops = t - number
+                away = s if right else depth - 1 - s
+                if 0 < hops < away:
+
+                    @pl.when(z == (hops if right else depth - 1 - hops))
+                    def _():
+                        line_piece(s, array, right, False).wait_recv()
+                        add_piece(s, array)
+                        start_piece(s, array, right)
+
+    def line_end():
+        for s in range(depth):
+
+            @pl.when(z == s)
+            def _():
+                here = pl.ds(s * in_rows, in_rows)
+                there = pl.ds(s * back_rows, back_rows)
+                gin_o[...] = gin_s[here, :].astype(F32)
+                gback_o[...] = gback_s[there, :].astype(F32)
+                if s > 0:
+                    for array in (0, 1):
+                        line_piece(s, array, True, True).wait_recv()
+                    gin_o[...] += line_in[s].astype(F32)
+                    gback_o[...] += line_back[s].astype(F32)
+                if s < depth - 1:
+                    for array in (0, 1):
+                        line_piece(s, array, False, True).wait_recv()
+                    gin_o[...] += extra_in[...].astype(F32)
+                    gback_o[...] += extra_back[...].astype(F32)
+
+        for s in range(depth):
+            for array in (0, 1):
+
+                @pl.when(z < s)
+                def _():
+                    line_piece(s, array, True, False).wait_send()
+
+                @pl.when(z > s)
+                def _():
+                    line_piece(s, array, False, False).wait_send()
+
+    for load in grad_loads:
+        load.wait()
+    line_service(0)
+
+    base_red = base + 4 * depth
+    per = Reduction.semaphores(depth)
+    reds = []
+    for place, final in enumerate((fin_o, fin_0, fin_1)):
+        value, wide, core_r, plane_r, line_s, line_r = red[6 * place : 6 * place + 6]
+        reds.append(
+            Reduction(
+                depth, value, wide, core_r, plane_r, line_s, line_r, final, sems,
+                base_red + place * per,
+            )
+        )
+    red_o, red_0, red_1 = reds
+
+    small[...] = small_in[...]
+    chunk_place = lax.broadcasted_iota(jnp.int32, (slot, width), 0)
+
+    def masked(ref, c):
+        return jnp.concatenate(
+            [
+                jnp.where(
+                    chunk_place < len_ref[c * count + s], ref[c * count + s].astype(F32), 0.0
+                )
+                for s in range(count)
+            ],
+            axis=0,
+        )
+
+    def flat(ref, c):
+        block = ref[pl.ds(c * count, count)]
+        return block.astype(F32).reshape(rows_per, width)
+
+    def first(c, carry):
+        rows = pl.ds(pl.multiple_of(c * rows_per, rows_per), rows_per)
+        normed2, inverse2 = normalize(h_ref[rows, :])
+        dm = flat(dm_ref, c)
+        dhidden = masked(cot_ref, c) + layer_norm_pull(dm, normed2, inverse2, g2[...])
+        small[2:3] += row_sum(dm * normed2, width)
+        small[3:4] += row_sum(dm, width)
+        dh_s[rows, :] = dhidden
+        dattn = dhidden.astype(BF)
+        da_s[rows, :] = dattn
+        dctx_s[rows, :] = mm(dattn, wo[...], 1, 1).astype(BF)
+        return carry
+
+    lax.fori_loop(0, sents // count, first, 0)
+    red_o.value[...] = mm(ctx[...], da_s[...], 0, 0)
+    red_o.send_core()
+    mask = block_diagonal(group, slot, head)
+
+    def pull(part, into):
+        cols = slice(part * span, (part + 1) * span)
+
+        def one(c, carry):
+            for s in range(count):
+                at = c * count + s
+                rows = pl.ds(pl.multiple_of(at * slot, slot), slot)
+                dq_s[rows, cols], dk_s[rows, cols], dv_s[rows, cols] = attention_pull(
+                    dctx_s[rows, cols], q[rows, cols], k[rows, cols], v[rows, cols],
+                    p_ref[at, part], mask, slot, group, scale,
+                )
+            return carry
+
+        lax.fori_loop(0, sents // count, one, 0)
+        into.value[0:width, :] = mm(act[...], dq_s[:, cols], 0, 0)
+        into.value[width : 2 * width, :] = mm(act[...], dk_s[:, cols], 0, 0)
+        into.value[2 * width : 3 * width, :] = mm(act[...], dv_s[:, cols], 0, 0)
+        into.send_core()
+
+    def returned(r, starts):
         loads[r].wait()
         back[r // 2].wait_recv()
         add_into(parts[r], 0, cores[r], sents)
         for index in starts:
             back[index].start()
-    return_finish(parts, sides, back, out)
-
-
-def combine_exchange(py):
-    cube = py.shape[1:]
+
+    pull(0, red_0)
+    red_o.send_plane()
+    line_service(1)
+    returned(6, (5, 7))
+    pull(1, red_1)
+    red_0.send_plane()
+    red_o.send_line()
+    line_service(2)
+    returned(2, ())
+    returned(4, ())
+    returned(0, ())
+
+    def last(c, carry):
+        rows = pl.ds(pl.multiple_of(c * rows_per, rows_per), rows_per)
+        dact = (
+            mm(dq_s[rows, :], wq[...], 1, 1)
+            + mm(dk_s[rows, :], wk[...], 1, 1)
+            + mm(dv_s[rows, :], wv[...], 1, 1)
+        )
+        normed1, inverse1 = normalize(flat(x_ref, c))
+        small[0:1] += row_sum(dact * normed1, width)
+        small[1:2] += row_sum(dact, width)
+        dx = dh_s[rows, :] + layer_norm_pull(dact, normed1, inverse1, g1[...])
+        ig_o[pl.ds(c * count, count)] = dx.astype(BF).reshape(count, slot, width)
+        return carry
+
+    lax.fori_loop(0, sents // count, last, 0)
+    red_1.send_plane()
+    back[4].start()
+    back[6].start()
+    red_o.send_back_line()
+    red_0.send_line()
+    line_service(3)
+    red_o.send_back_plane()
+    red_0.send_back_line()
+    red_1.send_line()
+    half = sents // 2
+    back[5].wait_recv()
+    add_into(parts[4], 0, sides[1], half)
+    back[7].wait_recv()
+    add_into(parts[2], half, sides[3], half)
+    line_service(4)
+    red_o.send_back_core()
+    red_0.send_back_plane()
+    red_1.send_back_line()
+    back[8].start()
+    back[9].start()
+    red_1.send_back_plane()
+    red_0.send_back_core()
+    back[4].wait_recv()
+    add_into(parts[0], 0, sides[0], half)
+    back[6].wait_recv()
+    add_into(parts[0], half, sides[2], half)
+    line_service(5)
+    red_1.send_back_core()
+    back[8].wait_recv()
+    back[9].wait_recv()
+
+    def outcome(low, side):
+        def one(i, carry):
+            at = low + i
+            valid = chunk_place < len_ref[at]
+            moe = jnp.where(valid, parts[0][at].astype(F32) + side[i].astype(F32), 0.0)
+            rows = pl.ds(pl.multiple_of(at * slot, slot), slot)
+            total = jnp.where(valid, h_ref[rows, :], 0.0) + moe
+            out_o[at] = total.astype(BF)
+            small[5:6] += row_sum(total * total, width)
+            small[6:7] += row_sum(moe * moe, width)
+            return carry
+
+        lax.fori_loop(0, half, one, 0)
+
+    outcome(0, sides[4])
+    outcome(half, sides[5])
+
+    base_small = base_red + 3 * per
+    me = lax.axis_index("expert")
+    to_core = remote(small, small_core, sends, recvs, base_small, CORE)
+    to_core.start()
+    to_core.wait()
+    spot = me // 2
+    small_plane[spot] = small[...] + small_core[...]
+    to_plane = [
+        remote(
+            small_plane.at[spot], small_plane.at[spot], sends, recvs, base_small + 1 + place,
+            relation,
+        )
+        for place, relation in enumerate((2, 4, 6))
+    ]
+    for copy in to_plane:
+        copy.start()
+    for copy in to_plane:
+        copy.wait()
+    total = small_plane[0]
+    for place in range(1, 4):
+        total = total + small_plane[place]
+    small_line[z] = total
+    to_line = [
+        along(
+            small_line.at[z], small_line.at[z], sends, recvs, base_small + 3 + offset, offset,
+            depth,
+        )
+        for offset in range(1, depth)
+    ]
+    for copy in to_line:
+        copy.start()
+    for copy in to_line:
+        copy.wait()
+    total = small_line[0]
+    for place in range(1, depth):
+        total = total + small_line[place]
+    small_o[...] = total
+    for one in reds:
+        one.finish()
+    line_end()
+    for copy in back:
+        copy.wait_send()
+
+
+def backward_exchange(
+    depth, lengths, tokens, cot, dm, hidden, act, q, k, v, ctx, prob, wq, wk, wv, wo, g1, g2,
+    small, py, gin, gback, heads,
+):
+    sents, slot, width = tokens.shape
+    total = sents * slot
+    vm = pl.BlockSpec(memory_space=VM)
+    shape = jax.ShapeDtypeStruct
+    cube = (sents, slot, width)
+    head = width // heads
+    span = max(1, min(heads, 256 // head)) * head
+    pieces = [(width, width), (3 * width, span), (3 * width, width - span)]
+    red = []
+    for rows, cols in pieces:
+        red += [
+            VM((rows, cols), F32),
+            VM((rows // 2, cols), BF),
+            VM((rows // 2, cols), BF),
+            VM((3, rows // 8, cols), BF),
+            VM((rows // 8, cols), BF),
+            VM((depth - 1, rows // 8 // depth, cols), BF),
+        ]
+    in_share = (gin.shape[0] // depth, gin.shape[1])
+    back_share = (gback.shape[0] // depth, gback.shape[1])
+    semaphores = 10 + 4 * depth + 3 * Reduction.semaphores(depth) + 4 + depth
     return pl.pallas_call(
-        combine_kernel,
-        in_specs=[pl.BlockSpec(memory_space=pl.ANY)],
-        out_specs=pl.BlockSpec(memory_space=VM),
-        out_shape=jax.ShapeDtypeStruct(cube, BF),
-        scratch_shapes=[VM(cube, BF)] * 12
-        + [VM((cube[0] // 2,) + cube[1:], BF)] * 6
+        functools.partial(backward_kernel, heads, depth),
+        in_specs=[pl.BlockSpec(memory_space=pltpu.SMEM)]
+        + [vm] * 17
+        + [pl.BlockSpec(memory_space=pl.ANY), pl.BlockSpec(memory_space=pl.ANY)]
+        + [pl.BlockSpec(memory_space=pl.ANY)],
+        out_specs=[vm] * 8,
+        out_shape=[shape(cube, BF), shape(cube, BF)]
+        + [shape(piece, BF) for piece in pieces]
+        + [shape(in_share, F32), shape(back_share, F32), shape(small.shape, F32)],
+        scratch_shapes=[VM(cube, BF)] * 8
+        + [VM((sents // 2, slot, width), BF)] * 6
+        + [VM((total, width), F32)]
+        + [VM((total, width), BF)] * 5
+        + red
+        + [VM((depth,) + in_share, BF), VM((depth,) + back_share, BF)]
+        + [VM(in_share, BF), VM(back_share, BF)]
+        + [VM(small.shape, F32)] * 2
+        + [VM((4,) + small.shape, F32), VM((depth,) + small.shape, F32)]
+        + [VM(gin.shape, BF), VM(gback.shape, BF)]
         + [
-            pltpu.SemaphoreType.DMA((10,)),
-            pltpu.SemaphoreType.DMA((10,)),
-            pltpu.SemaphoreType.DMA((8,)),
+            pltpu.SemaphoreType.DMA((semaphores,)),
+            pltpu.SemaphoreType.DMA((semaphores,)),
+            pltpu.SemaphoreType.DMA((6,)),
         ],
         compiler_params=pltpu.CompilerParams(
-            collective_id=2, has_side_effects=True, vmem_limit_bytes=40 * 2**20
+            collective_id=2, has_side_effects=True, vmem_limit_bytes=63 * 2**20
         ),
-        cost_estimate=pl.CostEstimate(flops=0, bytes_accessed=16 * 2**20, transcendentals=0),
-    )(py)
+        cost_estimate=pl.CostEstimate(
+            flops=16 * total * width * width, bytes_accessed=40 * 2**20, transcendentals=0
+        ),
+    )(
+        lengths, tokens, cot, dm, hidden, act, q, k, v, ctx, prob, wq, wk, wv, wo,
+        g1[None], g2[None], small, py, gin, gback,
+    )
 
 
 def local(
@@ -803,6 +1285,7 @@
 
 
 def local_plane(
+    depth,
     tokens,
     lengths,
     tasks,
@@ -835,12 +1318,10 @@
     placed = rank < capacity
     expert_hot = (chosen[:, :, None] == jnp.arange(experts)[None, None, :]).astype(jnp.float32)
     valid = (jnp.arange(slot)[None, :] < lengths[:, None]).astype(jnp.float32)
-    mask3 = valid[:, :, None]
     act, query, keyed, valued, context, prob, hidden, mixed, attn_sum = attention_forward(
         tokens, lengths, w_query, w_key, w_value, w_out,
         ln1_gain, ln1_bias, ln2_gain, ln2_bias, heads,
     )
-    hidden_res = hidden.reshape(sents, slot, width)
     table_rows = jnp.dot(task_hot.astype(jnp.float32), gate_table, precision=lax.Precision.HIGHEST)
     picked = jnp.sum(expert_hot * table_rows[:, None, :], axis=-1)
     gate_values = jax.nn.softmax(picked, axis=-1)
@@ -867,63 +1348,38 @@
     dmixed, parts_back, in_local, back_local, slot_dots = expert_exchange(
         places, gate_slots, mixed, cotangent, w_in[0], w_back[0], capacity
     )
-    expert_mixture = combine_exchange(parts_back).astype(jnp.float32)
-    total = mask3 * (hidden_res + expert_mixture)
-    output = total.astype(jnp.bfloat16)
-    stats_local = jnp.stack(
-        [
-            jnp.sum(total * total),
-            jnp.sum(attn_sum),
-            jnp.sum(mask3 * expert_mixture * expert_mixture),
-            jnp.sum(valid),
-        ]
-    )
-    stat_totals = lax.psum(stats_local, ("dp", "expert"))
     me = lax.axis_index("expert")
     dots_here = jnp.take(slot_dots[:, :, 0], me ^ jnp.arange(experts), axis=0).reshape(-1)
     gate_dot = jnp.sum(hits * dots_here[:, None], axis=0).reshape(sents, 2)
     dpicked = gate_values * (gate_dot - jnp.sum(gate_values * gate_dot, axis=-1, keepdims=True))
     dlogits = jnp.sum(expert_hot * dpicked[:, :, None], axis=1)
     table_grad = jnp.dot(task_hot.T.astype(jnp.float32), dlogits, precision=lax.Precision.HIGHEST)
-    input_grad, wq_grad, wk_grad, wv_grad, wout_grad, norms = attention_backward(
-        lengths, tokens, cotangent, dmixed, hidden, act, query, keyed, valued, context, prob,
-        w_query, w_key, w_value, w_out, ln1_gain, ln2_gain, heads,
-    )
-    gain1_grad, bias1_grad, gain2_grad, bias2_grad = norms[0], norms[1], norms[2], norms[3]
-    members = (
-        wq_grad,
-        wk_grad,
-        wv_grad,
-        wout_grad,
-        gain1_grad,
-        bias1_grad,
-        gain2_grad,
-        bias2_grad,
-        table_grad,
-    )
-    members = members + ()
-    summed = lax.psum(members, ("dp", "expert"))
-    rms = jnp.sqrt(stat_totals[0:3] / (stat_totals[3] * width))
-    in_share, back_share = (
-        lax.psum_scatter(
-            in_local, "dp", scatter_dimension=0, tiled=True
-        ).astype(jnp.float32),
-        lax.psum_scatter(
-            back_local, "dp", scatter_dimension=0, tiled=True
-        ).astype(jnp.float32),
-    )
+    row = lambda value: jnp.pad(value.reshape(-1), (0, width - value.size))[None]
+    empty = jnp.zeros((4, width), jnp.float32)
+    small = jnp.concatenate(
+        [empty, attn_sum, empty[:2], row(jnp.sum(valid)), row(table_grad), empty, empty[:3]]
+    )
+    input_grad, output, sum_o, sum_0, sum_1, in_share, back_share, small = backward_exchange(
+        depth, lengths, tokens, cotangent, dmixed, hidden, act, query, keyed, valued, context,
+        prob, w_query, w_key, w_value, w_out, ln1_gain, ln2_gain,
+        small, parts_back, in_local, back_local, heads,
+    )
+    sides = jnp.concatenate([sum_0, sum_1], axis=1).astype(jnp.float32)
+    wide = lambda place: sides[place * width : (place + 1) * width]
+    sums = jnp.sum(small[4:8], axis=1)
+    rms = jnp.sqrt(jnp.stack([sums[1], sums[0], sums[2]]) / (sums[3] * width))
     return (
         output,
         input_grad,
-        summed[8],
-        summed[4],
-        summed[5],
-        summed[6],
-        summed[7],
-        summed[0],
-        summed[1],
-        summed[2],
-        summed[3],
+        small[8, : table_grad.size].reshape(table_grad.shape),
+        small[0],
+        small[1],
+        small[2],
+        small[3],
+        wide(0),
+        wide(1),
+        wide(2),
+        sum_o.astype(jnp.float32),
         in_share[None],
         back_share[None],
         rms,
@@ -966,5 +1422,6 @@
         P(),
     )
     plane = dict(mesh.shape)["expert"]
-    body = local_plane if plane == 2 * 2 * 2 else local
+    depth = dict(mesh.shape)["dp"]
+    body = functools.partial(local_plane, depth) if plane == 2 * 2 * 2 else local
     return jax.shard_map(body, mesh=mesh, in_specs=in_specs, out_specs=out_specs, check_vma=False)

time: 405 us -> 308 us (0.76)
  waiting for transfers between devices: 74.6 us -> 0 us
  blocking collectives: 50.3 us -> 10.5 us
  Pallas kernels: 235 us -> 268 us
  between operations: 16.3 us -> 1.56 us
    psum x1 -> x0, waiting for transfers between devices: 73.8 us -> none  [local_plane(): summed = lax.psum(members, ('dp', 'expert'))]
    psum x1 -> x0, blocking collectives: 39.8 us -> none  [local_plane(): summed = lax.psum(members, ('dp', 'expert'))]
    pallas_call x2 -> x1, Pallas kernels: 75.1 us -> 109 us  [backward_exchange(): pl.pallas_call(functools.partial(backward_kernel, heads, depth), in_specs...]
    broadcast_in_dim x2 -> x0, other arithmetic: 4.27 us -> none  [the longest x1 2.14 us: local_plane(): back_share[None]]
    unnamed x26 -> x23, local copies, waits for them, and re-layouts: 9.42 us -> 5.24 us
  transfers between devices with their start and end apart: 3 -> 0, of which waited for: 1 -> 0; matrix products, arithmetic and copies ran while one was open for 3% -> 0% of each run, Pallas kernels for 19% -> 0%
where the time goes in v3:
time: 308 us; the launch traced here: 307 us
  Pallas kernels  268 us (87%)
  local copies, waits for them, and re-layouts  16 us (5%)
  other arithmetic  10.5 us (3%)
  blocking collectives  10.5 us (3%)
    pallas_call x1, Pallas kernels, expert_exchange(): pl.pallas_call(functools.partial(expert_kernel, cap), in_specs=[sm, sm, v...  146 us
    pallas_call x1, Pallas kernels, backward_exchange(): pl.pallas_call(functools.partial(backward_kernel, heads, depth), in_specs...  109 us
    pallas_call x1, Pallas kernels, attention_forward(): pl.pallas_call(functools.partial(attention_forward_kernel, heads), grid=(...  13 us
    all_gather x1, blocking collectives, local_plane(): table = lax.all_gather(sent_table, 'expert')  10.5 us

profile of v3, /device:TPU:0, one launch (start us, length us, event | category | flops | bytes accessed | tf_op | source)
XLA Modules:
  0.0 307.2 jit_solution(7273616239382379812)
XLA Ops:
  0.6 0.0 copy-start
  0.7 1.3 convert_reduce_fusion.1
  2.0 0.7 convert_element_type.75
  2.7 0.7 pad.8
  3.4 0.0 copy-done
  3.4 0.9 fusion.7
  4.2 0.1 broadcast_in_dim.27
  4.3 0.1 convert_element_type.76
  4.4 0.7 fusion.9
  5.1 0.8 multiply_reduce_fusion.1
  6.0 0.1 copy.38
  6.1 0.1 div.37
  6.2 0.1 copy.37
  6.3 0.1 reshape.333
  6.4 0.2 convert_reduce_fusion
  6.6 0.1 lt.56
  6.7 0.1 copy.39
  6.8 0.1 add.48
  6.8 0.1 copy.40
  7.0 0.1 fusion.4
  7.0 0.1 multiply_reduce_fusion
  7.2 0.1 squeeze.31
  7.2 0.1 squeeze.33
  7.3 0.1 squeeze.32
  7.4 0.1 pad_maximum_fusion
  7.5 10.5 %all-gather = f32[64,40]{1,0:T(8,128)S(1)} all-gather(f32[8,40]{1,0:T(8,128)S(1)} %pad_maximum_fusion), channel_id=2, replica_groups=mesh['dp'=4,'expert'=8] {'expert'}, dimensions={0}, use_global_device_ids=true | all-gather | bytes 11520 | tf_op jit(solution)/shard_map/all_gather | solution.py:1344
  18.0 0.1 slice.90
  18.1 0.7 reshape.335.gates
  18.8 0.7 reshape.334.tab
  19.4 13.0 %shard_map.263 = (bf16[1024,512]{1,0:T(8,128)(2,1)}, bf16[1024,512]{1,0:T(8,128)(2,1)}, bf16[1024,512]{1,0:T(8,128)(2,1)}, bf16[1024,512]{1,0:T(8,128)(2,1)}, bf...) custom-call(s32[16]{0:T(128)} %len_ref.3, ...), custom_call_target="tpu_custom_call" | custom-call | flops 2281701376 | bytes 8388608 | tf_op jit(solution)/shard_map/pallas_call | solution.py:138
  32.5 0.0 copy-start.8
  32.5 0.0 copy-start.7
  32.5 146.1 %shard_map.264 = (bf16[16,64,512]{2,1,0:T(8,128)(2,1)}, bf16[8,16,64,512]{3,2,1,0:T(8,128)(2,1)}, bf16[512,2048]{1,0:T(8,128)(2,1)}, bf16[2048,512]{1,0:T(8,128)(2,1)}, f32[8,8,128]{2,1,0:T(8,128)}) custom-call(s32[8,256]{1,0:T(8,128)} %reshape.334.tab, f32[8,64]{1,0:T(8,128)} %reshape.335.gates, bf16[16,64,512]{2,1,0:T(8,128)(2,1)} %get-tuple-element.36.m, ...), custom_call_target="tpu_custom_call" | custom-call | flops 51539607552 | bytes 41943040 | tf_op jit(solution)/shard_map/pallas_call | solution.py:576
  178.6 0.8 slice_reduce_fusion
  179.5 0.6 gather_fusion
  180.0 0.1 broadcast_select_fusion
  180.1 0.1 select_n.43
  180.2 0.2 select_reduce_fusion
  180.4 0.1 reshape.337
  180.5 0.1 copy.42
  180.6 0.0 copy-done.8
  180.6 0.1 fusion
  180.8 0.1 reshape.338
  180.9 0.0 copy-done.7
  180.9 1.3 concatenate.10.small_in
  182.2 108.5 %shard_map.265 = (bf16[16,64,512]{2,1,0:T(8,128)(2,1)}, bf16[16,64,512]{2,1,0:T(8,128)(2,1)}, bf16[512,512]{1,0:T(8,128)(2,1)}, bf16[1536,256]{1,0:T(8,128)(2,1)...) custom-call(s32[16]{0:T(128)} %len_ref.3, ...), custom_call_target="tpu_custom_call" | custom-call | flops 4294967296 | bytes 41943040 | tf_op jit(solution)/shard_map/pallas_call | solution.py:1097
  290.7 0.0 copy-start.5
  290.7 0.0 copy-start.6
  290.7 1.0 slice_reduce_fusion.1
  291.7 0.7 slice_reduce_fusion.2
  292.4 1.5 fusion.18
  293.8 0.6 fusion.19
  295.1 2.5 fusion.16
  297.6 0.1 reshape_squeeze.3
  297.7 0.7 copy.44
  298.4 2.1 convert_element_type.84
  300.5 0.4 maximum_convert_fusion
  301.0 1.7 fusion.17
  302.7 0.1 copy-done.4
  302.8 1.0 copy.50
  303.7 0.6 copy-done.3
  304.3 1.0 copy.51
  305.3 1.0 copy.52
  306.3 1.0 copy.53
  (30 shorter events, 0.3 us)
Async XLA Ops:
  0.6 2.7 copy-start
  32.5 148.1 %copy-start.8 = (s32[16]{0:T(128)S(1)}, s32[16]{0:T(128)}, u32[]{:S(2)}) copy-start(s32[16]{0:T(128)} %param.18) | copy-start | bytes 196
  32.5 148.4 %copy-start.7 = (f32[1,512]{1,0:T(1,128)S(1)}, f32[1,512]{1,0:T(1,128)}, u32[]{:S(2)}) copy-start(f32[1,512]{1,0:T(1,128)} %get-tuple-element.45) | copy-start | bytes 6148
  290.7 9.8 %copy-start.5 = (bf16[1536,256]{1,0:T(8,128)(2,1)S(1)}, bf16[1536,256]{1,0:T(8,128)(2,1)}, u32[]{:S(2)}) copy-start(bf16[1536,256]{1,0:T(8,128)(2,1)} %get-tuple-element.53) | copy-start | bytes 2359300
  290.7 9.8 %copy-start.6 = (bf16[1536,256]{1,0:T(8,128)(2,1)S(1)}, bf16[1536,256]{1,0:T(8,128)(2,1)}, u32[]{:S(2)}) copy-start(bf16[1536,256]{1,0:T(8,128)(2,1)} %get-tuple-element.54) | copy-start | bytes 2359300
  301.0 1.8 copy-start.4
  302.7 1.6 copy-start.3
  302.8 2.5 copy-start.2
  304.3 1.9 copy-start.1

commit v4 on v3

--- a/solution.py
+++ b/solution.py
@@ -15,6 +15,13 @@
     variance = jnp.mean(centered * centered, axis=-1, keepdims=True)
     inverse = lax.rsqrt(variance + 1e-05)
     return (centered * inverse, inverse)
+
+
+def norm_backward(grad, normed, inverse, gain):
+    scaled = grad * gain
+    inner = scaled - jnp.mean(scaled, axis=-1, keepdims=True)
+    inner = inner - normed * jnp.mean(scaled * normed, axis=-1, keepdims=True)
+    return (inverse * inner, jnp.sum(grad * normed, axis=(0, 1)), jnp.sum(grad, axis=(0, 1)))
 
 
 def project(left, right):
@@ -76,9 +83,51 @@
     return prob, context
 
 
+def route_tables(cap, tasks, lengths, routes, gate_table):
+    sents = tasks.shape[1]
+    ntasks, experts = gate_table.shape
+    iota = lambda rows, cols, axis: lax.broadcasted_iota(jnp.int32, (rows, cols), axis)
+    hot = (iota(ntasks, sents, 0) == tasks).astype(F32)
+    first = jnp.sum(hot * routes[:, 0:1].astype(F32), axis=0, keepdims=True)
+    second = jnp.sum(hot * routes[:, 1:2].astype(F32), axis=0, keepdims=True)
+    expert = iota(experts, sents, 0).astype(F32)
+    is_first, is_second = expert == first, expert == second
+    hit = jnp.logical_or(is_first, is_second)
+    before = (iota(sents, sents, 0) < iota(sents, sents, 1)).astype(BF)
+    rank = mm(hit.astype(F32).astype(BF), before)
+    place = jnp.where(hit, jnp.where(rank < cap, rank, -1.0), -1.0)
+    logits = lax.dot_general(
+        gate_table, hot, (((0,), (0,)), ((), ())), precision=lax.Precision.HIGHEST,
+        preferred_element_type=F32,
+    )
+    one = jnp.sum(jnp.where(is_first, logits, 0.0), axis=0, keepdims=True)
+    two = jnp.sum(jnp.where(is_second, logits, 0.0), axis=0, keepdims=True)
+    peak = jnp.maximum(one, two)
+    one, two = jnp.exp(one - peak), jnp.exp(two - peak)
+    gate = jnp.where(is_first, one / (one + two), 0.0)
+    gate = gate + jnp.where(is_second, two / (one + two), 0.0)
+    lane = iota(experts, 128, 1)
+    index = iota(experts, sents, 1).astype(F32)
+    table = jnp.zeros((experts, 128), F32)
+    gates = jnp.zeros((experts, 128), F32)
+    for j in range(cap):
+        here = place == float(j)
+        pick = lambda value: jnp.sum(jnp.where(here, value, 0.0), axis=1, keepdims=True)
+        table = jnp.where(lane == j, pick(index), table)
+        table = jnp.where(lane == cap + j, pick(lengths.astype(F32)), table)
+        gates = jnp.where(lane == j, pick(gate), gates)
+    shift = (iota(sents, 128, 1) == iota(sents, 128, 0) + 2 * cap).astype(BF)
+    spots = mm((place + 1.0).astype(BF), shift)
+    inside = jnp.logical_and(lane >= 2 * cap, lane < 2 * cap + sents)
+    table = jnp.where(inside, spots - 1.0, table)
+    return table.astype(jnp.int32), gates, hit.astype(F32), place, gate
+
+
 def attention_forward_kernel(
-    heads, len_ref, x_ref, wq, wk, wv, wo, g1, b1, g2, b2,
-    act_o, q_o, k_o, v_o, ctx_o, p_o, h_o, m_o, st_o,
+    heads, cap, len_ref, x_ref, wq, wk, wv, wo, g1, b1, g2, b2, tasks, lengths, routes,
+    gate_table, cot,
+    act_o, q_o, k_o, v_o, ctx_o, p_o, h_o, m_o, st_o, plan_o, tab_o, gates_o, near_o, far_o,
+    core_o, tab_s, gates_s, sends, recvs, local,
 ):
     count, slot, width = x_ref.shape
     head = width // heads
@@ -87,6 +136,45 @@
     step = pl.program_id(0)
     scale = head ** -0.5
     mask = block_diagonal(group, slot, head)
+    experts = gate_table.shape[1]
+    me = lax.axis_index("expert")
+    half = cot.shape[0] // 2
+    copies = [
+        remote(cot.at[pl.ds(0, half)], near_o, sends, recvs, 0, NEAR),
+        remote(cot.at[pl.ds(half, half)], far_o, sends, recvs, 1, FAR),
+        remote(cot, core_o, sends, recvs, 2, CORE),
+    ]
+    for relation in range(1, 8):
+        there = plane_peer(relation)
+        copies += [
+            remote(tab_s.at[there], tab_o.at[me], sends, recvs, 1 + 2 * relation, relation),
+            remote(gates_s.at[there], gates_o.at[me], sends, recvs, 2 + 2 * relation, relation),
+        ]
+    own = [
+        pltpu.make_async_copy(tab_s.at[me], tab_o.at[me], local.at[0]),
+        pltpu.make_async_copy(gates_s.at[me], gates_o.at[me], local.at[1]),
+    ]
+
+    @pl.when(step == 0)
+    def _():
+        plane_barrier()
+        for copy in copies[0:3]:
+            copy.start()
+        table, gates, hit, place, gate = route_tables(
+            cap, tasks[...], lengths[...], routes[...], gate_table[...]
+        )
+        for e in range(experts):
+            tab_s[e] = jnp.broadcast_to(table[e : e + 1], (8, 128))
+            gates_s[e] = jnp.broadcast_to(gates[e : e + 1], (8, 128))
+        for copy in copies[3:]:
+            copy.start()
+        for copy in own:
+            copy.start()
+        plan_o[0:experts] = hit
+        plan_o[experts : 2 * experts] = place
+        plan_o[2 * experts : 3 * experts] = gate
+        st_o[...] = jnp.zeros_like(st_o)
+
     x = x_ref[...].astype(F32).reshape(count * slot, width)
     normed, _ = normalize(x)
     act = (normed * g1[...] + b1[...]).astype(BF)
@@ -115,16 +203,19 @@
         length = len_ref[step * count + s]
         part = attn[s * slot : (s + 1) * slot]
         total = total + jnp.sum(jnp.where(place < length, part * part, 0.0), axis=0, keepdims=True)
-
-    @pl.when(step == 0)
+    st_o[...] += total
+
+    @pl.when(step == pl.num_programs(0) - 1)
     def _():
-        st_o[...] = jnp.zeros_like(st_o)
-
-    st_o[...] += total
-
-
-def attention_forward(tokens, lengths, wq, wk, wv, wo, g1, b1, g2, b2, heads):
+        for copy in copies + own:
+            copy.wait()
+
+
+def attention_forward(
+    tokens, lengths, wq, wk, wv, wo, g1, b1, g2, b2, tasks, routes, gate_table, cot, heads, cap
+):
     sents, slot, width = tokens.shape
+    experts = gate_table.shape[1]
     count = 4 if sents % 4 == 0 else 1
     rows = count * slot
     head = width // heads
@@ -133,31 +224,54 @@
     flat = pl.BlockSpec((rows, width), lambda i: (i, 0))
     cube = pl.BlockSpec((count, slot, width), lambda i: (i, 0, 0))
     probs = pl.BlockSpec((count, heads // group, slot, group * slot), lambda i: (i, 0, 0, 0))
+    anywhere = pl.BlockSpec(memory_space=pl.ANY)
     shape = jax.ShapeDtypeStruct
     total = sents * slot
+    half = (sents // 2, slot, width)
     return pl.pallas_call(
-        functools.partial(attention_forward_kernel, heads),
+        functools.partial(attention_forward_kernel, heads, cap),
         grid=(sents // count,),
         in_specs=[pl.BlockSpec(memory_space=pltpu.SMEM), cube]
         + [whole(width, width)] * 4
-        + [whole(1, width)] * 4,
-        out_specs=[flat] * 5 + [probs, flat, cube, whole(1, width)],
+        + [whole(1, width)] * 4
+        + [whole(1, sents)] * 2
+        + [whole(*routes.shape), whole(*gate_table.shape), anywhere],
+        out_specs=[flat] * 5
+        + [probs, flat, cube, whole(1, width), whole(3 * experts, sents)]
+        + [anywhere] * 5,
         out_shape=[shape((total, width), BF)] * 5
         + [
             shape((sents, heads // group, slot, group * slot), F32),
             shape((total, width), F32),
             shape((sents, slot, width), BF),
             shape((1, width), F32),
+            shape((3 * experts, sents), F32),
+            shape((experts, 8, 128), jnp.int32),
+            shape((experts, 8, 128), F32),
+            shape(half, BF),
+            shape(half, BF),
+            shape(tokens.shape, BF),
+        ],
+        scratch_shapes=[
+            VM((experts, 8, 128), jnp.int32),
+            VM((experts, 8, 128), F32),
+            pltpu.SemaphoreType.DMA((17,)),
+            pltpu.SemaphoreType.DMA((17,)),
+            pltpu.SemaphoreType.DMA((2,)),
         ],
         compiler_params=pltpu.CompilerParams(
-            dimension_semantics=("arbitrary",), vmem_limit_bytes=56 * 2**20
+            dimension_semantics=("arbitrary",), vmem_limit_bytes=56 * 2**20,
+            collective_id=0, has_side_effects=True,
         ),
         cost_estimate=pl.CostEstimate(
             flops=8 * total * width * width + 4 * total * slot * width,
             bytes_accessed=16 * total * width,
             transcendentals=total * slot * heads,
         ),
-    )(lengths, tokens, wq, wk, wv, wo, g1[None], b1[None], g2[None], b2[None])
+    )(
+        lengths, tokens, wq, wk, wv, wo, g1[None], b1[None], g2[None], b2[None],
+        tasks[None], lengths[None], routes, gate_table, cot,
+    )
 
 
 def row_sum(value, width):
@@ -181,106 +295,6 @@
     dkeyed = mm(dscores, spread(query, mask, group)) * scale
     dvalued = mm(low, dspread)
     return dquery.astype(BF), dkeyed.astype(BF), dvalued.astype(BF)
-
-
-def attention_backward_chunk(
-    heads, length_of, x_ref, cot_ref, dm_ref, h_ref, act, q, k, v, ctx, p_ref,
-    wq, wk, wv, wo, g1, g2, ig_o, dq_s, dk_s, dv_s, dctx_s, gq, gk, gv, go, norms,
-):
-    count, slot, width = x_ref.shape
-    head = width // heads
-    group = max(1, min(heads, 256 // head))
-    span = group * head
-    scale = head ** -0.5
-    mask = block_diagonal(group, slot, head)
-    place = lax.broadcasted_iota(jnp.int32, (slot, width), 0)
-    flat = lambda value: value.astype(F32).reshape(count * slot, width)
-    normed2, inverse2 = normalize(h_ref[...])
-    dm = flat(dm_ref[...])
-    cot = cot_ref[...].astype(F32)
-    gt = jnp.concatenate(
-        [jnp.where(place < length_of(s), cot[s], 0.0) for s in range(count)], axis=0
-    )
-    dhidden = gt + layer_norm_pull(dm, normed2, inverse2, g2[...])
-    norms[2:3] += row_sum(dm * normed2, width)
-    norms[3:4] += row_sum(dm, width)
-    dattn = dhidden.astype(BF)
-    go[...] += mm(ctx[...], dattn, 0, 0)
-    dctx_s[...] = mm(dattn, wo[...], 1, 1).astype(BF)
-    for s in range(count):
-        rows = slice(s * slot, (s + 1) * slot)
-        for part in range(heads // group):
-            cols = slice(part * span, (part + 1) * span)
-            dq_s[rows, cols], dk_s[rows, cols], dv_s[rows, cols] = attention_pull(
-                dctx_s[rows, cols], q[rows, cols], k[rows, cols], v[rows, cols],
-                p_ref[s, part], mask, slot, group, scale,
-            )
-    dq, dk, dv = dq_s[...], dk_s[...], dv_s[...]
-    gq[...] += mm(act[...], dq, 0, 0)
-    gk[...] += mm(act[...], dk, 0, 0)
-    gv[...] += mm(act[...], dv, 0, 0)
-    dact = mm(dq, wq[...], 1, 1) + mm(dk, wk[...], 1, 1) + mm(dv, wv[...], 1, 1)
-    normed1, inverse1 = normalize(flat(x_ref[...]))
-    norms[0:1] += row_sum(dact * normed1, width)
-    norms[1:2] += row_sum(dact, width)
-    dx = dhidden + layer_norm_pull(dact, normed1, inverse1, g1[...])
-    ig_o[...] = dx.astype(BF).reshape(count, slot, width)
-
-
-def attention_backward_kernel(
-    heads, len_ref, x_ref, cot_ref, dm_ref, h_ref, act, q, k, v, ctx, p_ref,
-    wq, wk, wv, wo, g1, g2, ig_o, gq, gk, gv, go, norms, dq_s, dk_s, dv_s, dctx_s,
-):
-    step = pl.program_id(0)
-    count = x_ref.shape[0]
-
-    @pl.when(step == 0)
-    def _():
-        for total in (gq, gk, gv, go, norms):
-            total[...] = jnp.zeros_like(total)
-
-    attention_backward_chunk(
-        heads, lambda s: len_ref[step * count + s], x_ref, cot_ref, dm_ref, h_ref,
-        act, q, k, v, ctx, p_ref, wq, wk, wv, wo, g1, g2, ig_o,
-        dq_s, dk_s, dv_s, dctx_s, gq, gk, gv, go, norms,
-    )
-
-
-def attention_backward(
-    lengths, tokens, cot, dm, hidden, act, q, k, v, ctx, prob, wq, wk, wv, wo, g1, g2, heads
-):
-    sents, slot, width = tokens.shape
-    count = 4 if sents % 4 == 0 else 1
-    rows = count * slot
-    head = width // heads
-    group = max(1, min(heads, 256 // head))
-    whole = lambda *shape: pl.BlockSpec(shape, lambda i: (0,) * len(shape))
-    flat = pl.BlockSpec((rows, width), lambda i: (i, 0))
-    cube = pl.BlockSpec((count, slot, width), lambda i: (i, 0, 0))
-    probs = pl.BlockSpec((count, heads // group, slot, group * slot), lambda i: (i, 0, 0, 0))
-    shape = jax.ShapeDtypeStruct
-    total = sents * slot
-    return pl.pallas_call(
-        functools.partial(attention_backward_kernel, heads),
-        grid=(sents // count,),
-        in_specs=[pl.BlockSpec(memory_space=pltpu.SMEM), cube, cube, cube]
-        + [flat] * 6 + [probs]
-        + [whole(width, width)] * 4
-        + [whole(1, width)] * 2,
-        out_specs=[cube] + [whole(width, width)] * 4 + [whole(8, width)],
-        out_shape=[shape((sents, slot, width), BF)]
-        + [shape((width, width), F32)] * 4
-        + [shape((8, width), F32)],
-        scratch_shapes=[VM((rows, width), BF)] * 4,
-        compiler_params=pltpu.CompilerParams(
-            dimension_semantics=("arbitrary",), vmem_limit_bytes=56 * 2**20
-        ),
-        cost_estimate=pl.CostEstimate(
-            flops=16 * total * width * width + 10 * total * slot * width,
-            bytes_accessed=24 * total * width,
-            transcendentals=0,
-        ),
-    )(lengths, tokens, cot, dm, hidden, act, q, k, v, ctx, prob, wq, wk, wv, wo, g1[None], g2[None])
 
 
 MESH_ID = pl.DeviceIdType.MESH
@@ -401,42 +415,61 @@
 
 
 def expert_kernel(
-    cap, tab, gates, m, cot, win, wback, dm_o, py_o, gin_o, gback_o, dg_o, *scratch
+    cap, tab, gates, m_in, cot_in, near_in, far_in, core_in, win_in, wback_in,
+    dm_o, py_o, gin_o, gback_o, dg_o, *scratch
 ):
-    sents, slot, width = m.shape
-    hidden = win.shape[1]
-    held_m = dict(zip(range(1, 8), scratch[0:7]))
-    held_c = dict(zip(range(1, 8), scratch[7:14]))
-    parts = dict(zip(range(8), scratch[14:22]))
-    cores = dict(zip((0, 2, 4, 6), scratch[22:26]))
-    sides = scratch[26:32]
-    xs, gs, dys, zs, dus, ys, dms, stage, dg_s, accb, acci, sends, recvs, local = scratch[32:]
+    sents, slot, width = m_in.shape
+    hidden = win_in.shape[1]
+    half = sents // 2
+    held_m = dict(zip(range(8), scratch[0:8]))
+    held_c = dict(zip(range(8), scratch[8:16]))
+    parts = dict(zip(range(8), scratch[16:24]))
+    cores = dict(zip((0, 2, 4, 6), scratch[24:28]))
+    sides = scratch[28:34]
+    win, wback = scratch[34:36]
+    xs, gs, dys, zs, dus, ys, dms, stage, dg_s, accb, acci, sends, recvs, local = scratch[36:]
     me = lax.axis_index("expert")
-    tile = min(512, hidden)
-    entries = 2 * cap + sents
+    tile = min(1024, hidden)
+    low, high = pl.ds(0, half), pl.ds(half, half)
+    loads = [
+        pltpu.make_async_copy(src, dst, local.at[2 + place])
+        for place, (src, dst) in enumerate(
+            [
+                (m_in, held_m[0]),
+                (cot_in, held_c[0]),
+                (win_in, win),
+                (wback_in, wback),
+                (core_in, held_c[1]),
+                (near_in, held_c[2].at[low]),
+                (far_in, held_c[4].at[high]),
+            ]
+        )
+    ]
+    for load in loads:
+        load.start()
 
     plane_barrier()
-    to_m = gather_copies(m, held_m, sends, recvs, 0)
-    to_c = gather_copies(cot, held_c, sends, recvs, 10)
+    to_m = gather_copies(m_in, held_m, sends, recvs, 0)
+    to_c = gather_copies(cot_in, held_c, sends, recvs, 10)
     back = return_copies(parts, cores, sides, sends, recvs, 20)
     gates_back = {
-        r: remote(dg_s.at[r], dg_o.at[r], sends, recvs, 30 + r, r) for r in range(1, 8)
+        r: remote(dg_s.at[r], dg_o.at[me], sends, recvs, 30 + r, r) for r in range(1, 8)
     }
-    for place in (0, 1, 2):
+    for place in (0, 1, 2, 3, 4):
         to_m[place].start()
-        to_c[place].start()
     for place in (3, 4):
-        to_m[place].start()
         to_c[place].start()
     accb[...] = jnp.zeros_like(accb)
     acci[...] = jnp.zeros_like(acci)
     place = lax.broadcasted_iota(jnp.int32, (slot, width), 0)
-    held_m[0], held_c[0] = m, cot
+    for load in loads[0:4]:
+        load.wait()
 
     def arrive(*indices):
         for index in indices:
             to_m[index].wait_recv()
-            to_c[index].wait_recv()
+            if index > 2:
+                to_c[index].wait_recv()
 
     def forward(*indices):
         for index in indices:
@@ -446,7 +479,10 @@
     def before(r):
         if r == 1:
             arrive(2)
+            loads[4].wait()
         if r == 2:
+            loads[5].wait()
+            loads[6].wait()
             arrive(0, 1)
             forward(5, 6)
             arrive(3)
@@ -465,16 +501,16 @@
         source = plane_peer(r)
 
         def fetch(j, carry):
-            index = tab[source, me * entries + j]
-            length = tab[source, me * entries + cap + j]
-            gate = gates[source, me * cap + j]
+            index = tab[source, 0, j]
+            length = tab[source, 0, cap + j]
+            gate = gates[source, 0, j]
             xs[j] = held_m[r][index]
             gt = jnp.where(place < length, held_c[r][index].astype(F32), 0.0)
             gs[j] = gt.astype(BF)
             dys[j] = (gt * gate).astype(BF)
             return carry
 
-        lax.fori_loop(0, cap, fetch, 0)
+        lax.fori_loop(0, cap, fetch, 0, unroll=2)
 
     def after(r):
         source = plane_peer(r)
@@ -482,27 +518,27 @@
             pltpu.make_async_copy(stage.at[r % 2], py_o.at[r - 2], local.at[r % 2]).wait()
 
         def give(i, carry):
-            index = tab[source, me * entries + 2 * cap + i]
+            index = tab[source, 0, 2 * cap + i]
             there = jnp.maximum(index, 0)
-            gate = gates[source, me * cap + there]
+            gate = gates[source, 0, there]
             hit = (index >= 0).astype(F32)
             parts[r][i] = (dms[there].astype(F32) * hit).astype(BF)
             stage[r % 2, i] = (ys[there].astype(F32) * (hit * gate)).astype(BF)
             return carry
 
-        lax.fori_loop(0, sents, give, 0)
+        lax.fori_loop(0, sents, give, 0, unroll=2)
         pltpu.make_async_copy(stage.at[r % 2], py_o.at[r], local.at[r % 2]).start()
 
         def dots(j, carry):
             product = ys[j].astype(F32) * gs[j].astype(F32)
             total = jnp.sum(jnp.sum(product, axis=0, keepdims=True), axis=1, keepdims=True)
             if r == 0:
-                dg_o[0, pl.ds(j, 1)] = jnp.broadcast_to(total, (1, 128))
+                dg_o[me, pl.ds(j, 1)] = jnp.broadcast_to(total, (1, 128))
             else:
                 dg_s[r, pl.ds(j, 1)] = jnp.broadcast_to(total, (1, 128))
             return carry
 
-        lax.fori_loop(0, cap, dots, 0)
+        lax.fori_loop(0, cap, dots, 0, unroll=4)
         if r > 0:
             gates_back[r].start()
         if r % 2 == 1:
@@ -553,30 +589,40 @@
         return carry
 
     lax.fori_loop(0, 8, chunk, 0)
-    gin_o[...] = acci[...].astype(BF)
-    gback_o[...] = accb[...].astype(BF)
+    win[...] = acci[...].astype(BF)
+    wback[...] = accb[...].astype(BF)
+    stores = [
+        pltpu.make_async_copy(win, gin_o, local.at[4]),
+        pltpu.make_async_copy(wback, gback_o, local.at[5]),
+    ]
+    for store in stores:
+        store.start()
     return_finish(parts, sides, back, dm_o)
+    for store in stores:
+        store.wait()
     for r in range(1, 8):
         gates_back[r].wait()
     for index in range(10):
         to_m[index].wait_send()
-        to_c[index].wait_send()
+        if index > 2:
+            to_c[index].wait_send()
     for r in (6, 7):
         pltpu.make_async_copy(stage.at[r % 2], py_o.at[r], local.at[r % 2]).wait()
 
 
-def expert_exchange(tab, gates, m, cot, win, wback, cap):
+def expert_exchange(tab, gates, m, cot, near, far, core, win, wback, cap):
     sents, slot, width = m.shape
     hidden = win.shape[1]
     vm = pl.BlockSpec(memory_space=VM)
     sm = pl.BlockSpec(memory_space=pltpu.SMEM)
+    anywhere = pl.BlockSpec(memory_space=pl.ANY)
     shape = jax.ShapeDtypeStruct
     cube = (sents, slot, width)
     rows = cap * slot
     return pl.pallas_call(
         functools.partial(expert_kernel, cap),
-        in_specs=[sm, sm, vm, vm, vm, vm],
-        out_specs=[vm, pl.BlockSpec(memory_space=pl.ANY), vm, vm, vm],
+        in_specs=[sm, sm] + [anywhere] * 7,
+        out_specs=[vm, anywhere, anywhere, anywhere, vm],
         out_shape=[
             shape(cube, BF),
             shape((8,) + cube, BF),
@@ -584,8 +630,9 @@
             shape((hidden, width), BF),
             shape((8, cap, 128), F32),
         ],
-        scratch_shapes=[VM(cube, BF)] * (14 + 8 + 4)
+        scratch_shapes=[VM(cube, BF)] * (16 + 8 + 4)
         + [VM((sents // 2, slot, width), BF)] * 6
+        + [VM((width, hidden), BF), VM((hidden, width), BF)]
         + [VM((cap, slot, width), BF)] * 3
         + [VM((rows, hidden), BF)] * 2
         + [VM((cap, slot, width), BF)] * 2
@@ -594,7 +641,7 @@
         + [
             pltpu.SemaphoreType.DMA((38,)),
             pltpu.SemaphoreType.DMA((38,)),
-            pltpu.SemaphoreType.DMA((2,)),
+            pltpu.SemaphoreType.DMA((9,)),
         ],
         compiler_params=pltpu.CompilerParams(
             collective_id=1, has_side_effects=True, vmem_limit_bytes=63 * 2**20
@@ -602,7 +649,7 @@
         cost_estimate=pl.CostEstimate(
             flops=12 * 8 * rows * width * hidden, bytes_accessed=40 * 2**20, transcendentals=0
         ),
-    )(tab, gates, m, cot, win, wback)
+    )(tab, gates, m, cot, near, far, core, win, wback)
 
 
 def line_peer(offset, depth):
@@ -724,7 +771,7 @@
 
 def backward_kernel(
     heads, depth, len_ref, x_ref, cot_ref, dm_ref, h_ref, act, q, k, v, ctx, p_ref,
-    wq, wk, wv, wo, g1, g2, small_in, py, gin, gback,
+    wq, wk, wv, wo, g1, g2, attn_sum, plan, tasks, lengths, dots, py, gin, gback,
     ig_o, out_o, fin_o, fin_0, fin_1, gin_o, gback_o, small_o, *scratch
 ):
     sents, slot, width = x_ref.shape
@@ -888,7 +935,10 @@
         )
     red_o, red_0, red_1 = reds
 
-    small[...] = small_in[...]
+    small[...] = jnp.zeros_like(small)
+    small[4:5] = attn_sum[...]
+    small[7:8, 0:sents] = lengths[...].astype(F32)
+    experts = plan.shape[0] // 3
     chunk_place = lax.broadcasted_iota(jnp.int32, (slot, width), 0)
 
     def masked(ref, c):
@@ -920,6 +970,19 @@
         return carry
 
     lax.fori_loop(0, sents // count, first, 0)
+    hit = plan[0:experts] > 0.5
+    place = plan[experts : 2 * experts]
+    gate = plan[2 * experts : 3 * experts]
+    taken = jnp.zeros(gate.shape, F32)
+    for j in range(dots.shape[1]):
+        taken = taken + jnp.where(place == float(j), dots[:, j, 0:sents], 0.0)
+    inner = jnp.sum(gate * taken, axis=0, keepdims=True)
+    dlogit = jnp.where(hit, gate * (taken - inner), 0.0)
+    hot = lax.broadcasted_iota(jnp.int32, (slot, sents), 0) == tasks[...]
+    small[8 : 8 + experts, 0:slot] = lax.dot_general(
+        dlogit, hot.astype(F32), (((1,), (1,)), ((), ())), precision=lax.Precision.HIGHEST,
+        preferred_element_type=F32,
+    )
     red_o.value[...] = mm(ctx[...], da_s[...], 0, 0)
     red_o.send_core()
     mask = block_diagonal(group, slot, head)
@@ -1071,10 +1134,11 @@
 
 def backward_exchange(
     depth, lengths, tokens, cot, dm, hidden, act, q, k, v, ctx, prob, wq, wk, wv, wo, g1, g2,
-    small, py, gin, gback, heads,
+    attn_sum, plan, tasks, dots, py, gin, gback, heads,
 ):
     sents, slot, width = tokens.shape
     total = sents * slot
+    small = jax.ShapeDtypeStruct((16, width), F32)
     vm = pl.BlockSpec(memory_space=VM)
     shape = jax.ShapeDtypeStruct
     cube = (sents, slot, width)
@@ -1097,7 +1161,7 @@
     return pl.pallas_call(
         functools.partial(backward_kernel, heads, depth),
         in_specs=[pl.BlockSpec(memory_space=pltpu.SMEM)]
-        + [vm] * 17
+        + [vm] * 21
         + [pl.BlockSpec(memory_space=pl.ANY), pl.BlockSpec(memory_space=pl.ANY)]
         + [pl.BlockSpec(memory_space=pl.ANY)],
         out_specs=[vm] * 8,
@@ -1127,7 +1191,7 @@
         ),
     )(
         lengths, tokens, cot, dm, hidden, act, q, k, v, ctx, prob, wq, wk, wv, wo,
-        g1[None], g2[None], small, py, gin, gback,
+        g1[None], g2[None], attn_sum, plan, tasks[None], lengths[None], dots, py, gin, gback,
     )
 
 
@@ -1151,9 +1215,11 @@
 ):
     sents, slot, width = tokens.shape
     heads = HEADS
+    head = width // heads
     experts = gate_table.shape[1]
     ntasks = routes.shape[0]
     capacity = max(1, 4 * sents // experts)
+    scale = 1.0 / jnp.sqrt(jnp.float32(head))
     task_hot = (tasks[:, None] == jnp.arange(ntasks)[None, :]).astype(jnp.int32)
     chosen = jnp.sum(task_hot[:, :, None] * routes[None, :, :], axis=1)
     flat = chosen.reshape(-1)
@@ -1168,12 +1234,31 @@
     collect = dispatch.T
     expert_hot = (chosen[:, :, None] == jnp.arange(experts)[None, None, :]).astype(jnp.float32)
     valid = (jnp.arange(slot)[None, :] < lengths[:, None]).astype(jnp.float32)
+    keymask = valid[:, None, None, :] > 0.5
     mask3 = valid[:, :, None]
-    act, query, keyed, valued, context, prob, hidden, mixed, attn_sum = attention_forward(
-        tokens, lengths, w_query, w_key, w_value, w_out,
-        ln1_gain, ln1_bias, ln2_gain, ln2_bias, heads,
-    )
-    hidden_res = hidden.reshape(sents, slot, width)
+    xfull = tokens.astype(jnp.float32)
+    normed1, inverse1 = normalize(xfull)
+    act = (normed1 * ln1_gain + ln1_bias).astype(jnp.bfloat16).reshape(-1, width)
+    query = project(act, w_query).astype(jnp.bfloat16).reshape(sents, slot, heads, head)
+    keyed = project(act, w_key).astype(jnp.bfloat16).reshape(sents, slot, heads, head)
+    valued = project(act, w_value).astype(jnp.bfloat16).reshape(sents, slot, heads, head)
+
+    def scores_of(qpart, kpart):
+        raw = (
+            jnp.einsum("sqhd,skhd->shqk", qpart, kpart, preferred_element_type=jnp.float32) * scale
+        )
+        return jnp.where(keymask, raw, -1000000000.0)
+
+    scores = scores_of(query, keyed)
+    peak = jnp.max(scores, axis=-1, keepdims=True)
+    logsum = peak + jnp.log(jnp.sum(jnp.exp(scores - peak), axis=-1, keepdims=True))
+    prob_low = jnp.exp(scores - logsum).astype(jnp.bfloat16)
+    context = jnp.einsum("shqk,skhd->sqhd", prob_low, valued, preferred_element_type=jnp.float32)
+    context = context.astype(jnp.bfloat16).reshape(-1, width)
+    attention_block = project(context, w_out).reshape(sents, slot, width)
+    hidden_res = xfull + attention_block
+    normed2, inverse2 = normalize(hidden_res)
+    mixed = (normed2 * ln2_gain + ln2_bias).astype(jnp.bfloat16)
     table_rows = jnp.dot(task_hot.astype(jnp.float32), gate_table, precision=lax.Precision.HIGHEST)
     picked = jnp.sum(expert_hot * table_rows[:, None, :], axis=-1)
     gate_values = jax.nn.softmax(picked, axis=-1)
@@ -1225,7 +1310,7 @@
     stats_local = jnp.stack(
         [
             jnp.sum(total * total),
-            jnp.sum(attn_sum),
+            jnp.sum(mask3 * attention_block * attention_block),
             jnp.sum(mask3 * expert_mixture * expert_mixture),
             jnp.sum(valid),
         ]
@@ -1239,11 +1324,34 @@
         sents, 2, slot, width
     )
     dmixed = jnp.sum(dmixed, axis=1)
-    input_grad, wq_grad, wk_grad, wv_grad, wout_grad, norms = attention_backward(
-        lengths, tokens, cotangent, dmixed, hidden, act, query, keyed, valued, context, prob,
-        w_query, w_key, w_value, w_out, ln1_gain, ln2_gain, heads,
-    )
-    gain1_grad, bias1_grad, gain2_grad, bias2_grad = norms[0], norms[1], norms[2], norms[3]
+    dres2, gain2_grad, bias2_grad = norm_backward(dmixed, normed2, inverse2, ln2_gain)
+    dhidden = grad_total + dres2
+    dattn = dhidden.astype(jnp.bfloat16).reshape(-1, width)
+    wout_grad = project(context.T, dattn)
+    dcontext = project(dattn, w_out.T).astype(jnp.bfloat16).reshape(sents, slot, heads, head)
+    again = jnp.exp(scores_of(query, keyed) - logsum)
+    dprob = jnp.einsum("sqhd,skhd->shqk", dcontext, valued, preferred_element_type=jnp.float32)
+    dscores = (again * (dprob - jnp.sum(dprob * again, axis=-1, keepdims=True))).astype(
+        jnp.bfloat16
+    )
+    dquery = (
+        jnp.einsum("shqk,skhd->sqhd", dscores, keyed, preferred_element_type=jnp.float32) * scale
+    )
+    dkeyed = (
+        jnp.einsum("shqk,sqhd->skhd", dscores, query, preferred_element_type=jnp.float32) * scale
+    )
+    dvalued = jnp.einsum("shqk,sqhd->skhd", prob_low, dcontext, preferred_element_type=jnp.float32)
+    dquery = dquery.astype(jnp.bfloat16).reshape(-1, width)
+    dkeyed = dkeyed.astype(jnp.bfloat16).reshape(-1, width)
+    dvalued = dvalued.astype(jnp.bfloat16).reshape(-1, width)
+    wq_grad = project(act.T, dquery)
+    wk_grad = project(act.T, dkeyed)
+    wv_grad = project(act.T, dvalued)
+    dact = project(dquery, w_query.T) + project(dkeyed, w_key.T) + project(dvalued, w_value.T)
+    dres1, gain1_grad, bias1_grad = norm_backward(
+        dact.reshape(sents, slot, width), normed1, inverse1, ln1_gain
+    )
+    input_grad = (dhidden + dres1).astype(jnp.bfloat16)
     members = (
         wq_grad,
         wk_grad,
@@ -1303,66 +1411,24 @@
     w_back,
     cotangent,
 ):
+    experts = gate_table.shape[1]
     sents, slot, width = tokens.shape
     heads = HEADS
-    experts = gate_table.shape[1]
-    ntasks = routes.shape[0]
     capacity = max(1, 4 * sents // experts)
-    task_hot = (tasks[:, None] == jnp.arange(ntasks)[None, :]).astype(jnp.int32)
-    chosen = jnp.sum(task_hot[:, :, None] * routes[None, :, :], axis=1)
-    flat = chosen.reshape(-1)
-    order = jnp.arange(2 * sents)
-    earlier = (flat[:, None] == flat[None, :]) & (order[None, :] < order[:, None])
-    rank = jnp.sum(earlier.astype(jnp.int32), axis=1)
-    slot_id = flat * capacity + rank
-    placed = rank < capacity
-    expert_hot = (chosen[:, :, None] == jnp.arange(experts)[None, None, :]).astype(jnp.float32)
-    valid = (jnp.arange(slot)[None, :] < lengths[:, None]).astype(jnp.float32)
-    act, query, keyed, valued, context, prob, hidden, mixed, attn_sum = attention_forward(
-        tokens, lengths, w_query, w_key, w_value, w_out,
-        ln1_gain, ln1_bias, ln2_gain, ln2_bias, heads,
-    )
-    table_rows = jnp.dot(task_hot.astype(jnp.float32), gate_table, precision=lax.Precision.HIGHEST)
-    picked = jnp.sum(expert_hot * table_rows[:, None, :], axis=-1)
-    gate_values = jax.nn.softmax(picked, axis=-1)
-    hits = (
-        (jnp.arange(experts * capacity)[:, None] == slot_id[None, :]) & placed[None, :]
-    ).astype(jnp.float32)
-    per_copy = jnp.stack(
-        [
-            (order // 2).astype(jnp.float32),
-            jnp.repeat(lengths, 2).astype(jnp.float32),
-            gate_values.reshape(-1),
-        ]
-    )
-    per_slot = jnp.sum(hits[None] * per_copy[:, None, :], axis=-1).reshape(3, experts, capacity)
-    taken = (flat[None, :] == jnp.arange(experts)[:, None]) & placed[None, :]
-    ranks = jnp.sum(
-        (taken * (rank + 1)[None, :]).reshape(experts, sents, 2), axis=-1
-    ).astype(jnp.float32)
-    sent_table = jnp.concatenate([per_slot[0], per_slot[1], ranks - 1.0, per_slot[2]], axis=1)
-    table = lax.all_gather(sent_table, "expert")
-    entries = 2 * capacity + sents
-    places = table[:, :, :entries].astype(jnp.int32).reshape(experts, -1)
-    gate_slots = table[:, :, entries:].reshape(experts, -1)
+    (
+        act, query, keyed, valued, context, prob, hidden, mixed, attn_sum, plan, places,
+        gate_slots, near, far, core,
+    ) = attention_forward(
+        tokens, lengths, w_query, w_key, w_value, w_out, ln1_gain, ln1_bias, ln2_gain, ln2_bias,
+        tasks, routes, gate_table, cotangent, heads, capacity,
+    )
     dmixed, parts_back, in_local, back_local, slot_dots = expert_exchange(
-        places, gate_slots, mixed, cotangent, w_in[0], w_back[0], capacity
-    )
-    me = lax.axis_index("expert")
-    dots_here = jnp.take(slot_dots[:, :, 0], me ^ jnp.arange(experts), axis=0).reshape(-1)
-    gate_dot = jnp.sum(hits * dots_here[:, None], axis=0).reshape(sents, 2)
-    dpicked = gate_values * (gate_dot - jnp.sum(gate_values * gate_dot, axis=-1, keepdims=True))
-    dlogits = jnp.sum(expert_hot * dpicked[:, :, None], axis=1)
-    table_grad = jnp.dot(task_hot.T.astype(jnp.float32), dlogits, precision=lax.Precision.HIGHEST)
-    row = lambda value: jnp.pad(value.reshape(-1), (0, width - value.size))[None]
-    empty = jnp.zeros((4, width), jnp.float32)
-    small = jnp.concatenate(
-        [empty, attn_sum, empty[:2], row(jnp.sum(valid)), row(table_grad), empty, empty[:3]]
+        places, gate_slots, mixed, cotangent, near, far, core, w_in[0], w_back[0], capacity
     )
     input_grad, output, sum_o, sum_0, sum_1, in_share, back_share, small = backward_exchange(
         depth, lengths, tokens, cotangent, dmixed, hidden, act, query, keyed, valued, context,
         prob, w_query, w_key, w_value, w_out, ln1_gain, ln2_gain,
-        small, parts_back, in_local, back_local, heads,
+        attn_sum, plan, tasks, slot_dots, parts_back, in_local, back_local, heads,
     )
     sides = jnp.concatenate([sum_0, sum_1], axis=1).astype(jnp.float32)
     wide = lambda place: sides[place * width : (place + 1) * width]
@@ -1371,7 +1437,7 @@
     return (
         output,
         input_grad,
-        small[8, : table_grad.size].reshape(table_grad.shape),
+        small[8 : 8 + experts, : gate_table.shape[0]].T,
         small[0],
         small[1],
         small[2],

time: 308 us -> 276 us (0.90)
  Pallas kernels: 268 us -> 255 us
  blocking collectives: 10.5 us -> 0 us
  other arithmetic: 10.5 us -> 6.06 us
  local copies, waits for them, and re-layouts: 16 us -> 12.4 us
    pallas_call x2, Pallas kernels: 159 us -> 147 us  [the longest x1 126 us: expert_exchange(): pl.pallas_call(functools.partial(expert_kernel, cap), in_specs=[sm, sm] +...]
    all_gather x1 -> x0, blocking collectives: 10.5 us -> none  [local_plane(): table = lax.all_gather(sent_table, 'expert')]
    unnamed x23 -> x18, local copies, waits for them, and re-layouts: 5.24 us -> 7.28 us
where the time goes in v4:
time: 276 us; the launch traced here: 275 us
  Pallas kernels  255 us (92%)
  local copies, waits for them, and re-layouts  12.4 us (4%)
  other arithmetic  6.06 us (2%)
    pallas_call x1, Pallas kernels, expert_exchange(): pl.pallas_call(functools.partial(expert_kernel, cap), in_specs=[sm, sm] +...  126 us
    pallas_call x1, Pallas kernels, backward_exchange(): pl.pallas_call(functools.partial(backward_kernel, heads, depth), in_specs...  108 us
    pallas_call x1, Pallas kernels, attention_forward(): pl.pallas_call(functools.partial(attention_forward_kernel, heads, cap), g...  21.2 us
    unnamed x18, local copies, waits for them, and re-layouts  7.28 us

profile of v4, /device:TPU:0, one launch (start us, length us, event | category | flops | bytes accessed | tf_op | source)
XLA Modules:
  0.0 275.0 jit_solution(6958466353907610914)
XLA Ops:
  0.6 1.4 copy.30.routes
  2.0 1.4 copy.31.gate_table
  3.4 21.2 %shard_map.263 = (bf16[1024,512]{1,0:T(8,128)(2,1)}, bf16[1024,512]{1,0:T(8,128)(2,1)}, bf16[1024,512]{1,0:T(8,128)(2,1)}, bf16[1024,512]{1,0:T(8,128)(2,1)}, bf...) custom-call(s32[16]{0:T(128)} %len_ref.3, ...), custom_call_target="tpu_custom_call" | custom-call | flops 2281701376 | bytes 8388608 | tf_op jit(solution)/shard_map/pallas_call | solution.py:231
  24.6 125.5 %shard_map.264 = (bf16[16,64,512]{2,1,0:T(8,128)(2,1)}, bf16[8,16,64,512]{3,2,1,0:T(8,128)(2,1)}, bf16[512,2048]{1,0:T(8,128)(2,1)}, bf16[2048,512]{1,0:T(8,128)(2,1)}, f32[8,8,128]{2,1,0:T(8,128)}) custom-call(s32[8,8,128]{2,1,0:T(8,128)} %get-tuple-element.42.tab, f32[8,8,128]{2,1,0:T(8,128)} %get-tuple-element.43.gates, ...), custom_call_target="tpu_custom_call" | custom-call | flops 51539607552 | bytes 41943040 | tf_op jit(solution)/shard_map/pallas_call | solution.py:622
  150.1 108.5 %shard_map.265 = (bf16[16,64,512]{2,1,0:T(8,128)(2,1)}, bf16[16,64,512]{2,1,0:T(8,128)(2,1)}, bf16[512,512]{1,0:T(8,128)(2,1)}, bf16[1536,256]{1,0:T(8,128)(2,1)...) custom-call(s32[16]{0:T(128)} %len_ref.3, ...), custom_call_target="tpu_custom_call" | custom-call | flops 4294967296 | bytes 41943040 | tf_op jit(solution)/shard_map/pallas_call | solution.py:1161
  258.6 0.0 copy-start.4
  258.6 0.0 copy-start.5
  258.6 1.0 slice_reduce_fusion
  259.6 0.6 fusion.3
  260.8 2.5 fusion
  263.4 1.3 slice_bitcast_fusion
  264.6 1.5 fusion.2
  266.1 2.1 convert_element_type.7
  268.2 0.0 copy-done.4
  268.3 0.0 copy-done.5
  268.3 0.4 maximum_convert_fusion
  268.7 0.0 copy-start.3
  268.7 1.7 fusion.1
  270.4 0.0 copy-start.2
  270.4 0.1 copy-done.3
  270.5 0.0 copy-start.1
  270.5 1.0 copy.36
  271.5 0.6 copy-done.2
  272.0 0.0 copy-start
  272.1 1.0 copy.37
  273.0 0.0 copy-done.1
  273.0 1.0 copy.38
  274.0 0.0 copy-done
  274.0 1.0 copy.39
Async XLA Ops:
  258.6 9.6 %copy-start.4 = (bf16[1536,256]{1,0:T(8,128)(2,1)S(1)}, bf16[1536,256]{1,0:T(8,128)(2,1)}, u32[]{:S(2)}) copy-start(bf16[1536,256]{1,0:T(8,128)(2,1)} %get-tuple-element.65) | copy-start | bytes 2359300
  258.6 9.6 %copy-start.5 = (bf16[1536,256]{1,0:T(8,128)(2,1)S(1)}, bf16[1536,256]{1,0:T(8,128)(2,1)}, u32[]{:S(2)}) copy-start(bf16[1536,256]{1,0:T(8,128)(2,1)} %get-tuple-element.66) | copy-start | bytes 2359300
  268.7 1.8 copy-start.3
  270.4 1.6 copy-start.2
  270.5 2.5 copy-start.1
  272.0 1.9 copy-start

commit v5 on v4

--- a/solution.py
+++ b/solution.py
@@ -85,21 +85,24 @@
 
 def route_tables(cap, tasks, lengths, routes, gate_table):
     sents = tasks.shape[1]
-    ntasks, experts = gate_table.shape
+    experts, ntasks = gate_table.shape
     iota = lambda rows, cols, axis: lax.broadcasted_iota(jnp.int32, (rows, cols), axis)
     hot = (iota(ntasks, sents, 0) == tasks).astype(F32)
-    first = jnp.sum(hot * routes[:, 0:1].astype(F32), axis=0, keepdims=True)
-    second = jnp.sum(hot * routes[:, 1:2].astype(F32), axis=0, keepdims=True)
+    exact = functools.partial(
+        lax.dot_general,
+        dimension_numbers=(((1,), (0,)), ((), ())),
+        precision=lax.Precision.HIGHEST,
+        preferred_element_type=F32,
+    )
+    chosen = exact(routes.astype(F32), hot)
+    first, second = chosen[0:1], chosen[1:2]
     expert = iota(experts, sents, 0).astype(F32)
     is_first, is_second = expert == first, expert == second
     hit = jnp.logical_or(is_first, is_second)
     before = (iota(sents, sents, 0) < iota(sents, sents, 1)).astype(BF)
     rank = mm(hit.astype(F32).astype(BF), before)
     place = jnp.where(hit, jnp.where(rank < cap, rank, -1.0), -1.0)
-    logits = lax.dot_general(
-        gate_table, hot, (((0,), (0,)), ((), ())), precision=lax.Precision.HIGHEST,
-        preferred_element_type=F32,
-    )
+    logits = exact(gate_table, hot)
     one = jnp.sum(jnp.where(is_first, logits, 0.0), axis=0, keepdims=True)
     two = jnp.sum(jnp.where(is_second, logits, 0.0), axis=0, keepdims=True)
     peak = jnp.maximum(one, two)
@@ -125,9 +128,9 @@
 
 def attention_forward_kernel(
     heads, cap, len_ref, x_ref, wq, wk, wv, wo, g1, b1, g2, b2, tasks, lengths, routes,
-    gate_table, cot,
+    gate_table, cot_in,
     act_o, q_o, k_o, v_o, ctx_o, p_o, h_o, m_o, st_o, plan_o, tab_o, gates_o, near_o, far_o,
-    core_o, tab_s, gates_s, sends, recvs, local,
+    core_o, cot, tab_s, gates_s, sends, recvs, local,
 ):
     count, slot, width = x_ref.shape
     head = width // heads
@@ -136,7 +139,7 @@
     step = pl.program_id(0)
     scale = head ** -0.5
     mask = block_diagonal(group, slot, head)
-    experts = gate_table.shape[1]
+    experts = gate_table.shape[0]
     me = lax.axis_index("expert")
     half = cot.shape[0] // 2
     copies = [
@@ -157,7 +160,10 @@
 
     @pl.when(step == 0)
     def _():
+        load = pltpu.make_async_copy(cot_in, cot, local.at[2])
+        load.start()
         plane_barrier()
+        load.wait()
         for copy in copies[0:3]:
             copy.start()
         table, gates, hit, place, gate = route_tables(
@@ -215,7 +221,7 @@
     tokens, lengths, wq, wk, wv, wo, g1, b1, g2, b2, tasks, routes, gate_table, cot, heads, cap
 ):
     sents, slot, width = tokens.shape
-    experts = gate_table.shape[1]
+    experts = gate_table.shape[0]
     count = 4 if sents % 4 == 0 else 1
     rows = count * slot
     head = width // heads
@@ -253,11 +259,12 @@
             shape(tokens.shape, BF),
         ],
         scratch_shapes=[
+            VM(cot.shape, BF),
             VM((experts, 8, 128), jnp.int32),
             VM((experts, 8, 128), F32),
             pltpu.SemaphoreType.DMA((17,)),
             pltpu.SemaphoreType.DMA((17,)),
-            pltpu.SemaphoreType.DMA((2,)),
+            pltpu.SemaphoreType.DMA((3,)),
         ],
         compiler_params=pltpu.CompilerParams(
             dimension_semantics=("arbitrary",), vmem_limit_bytes=56 * 2**20,
@@ -321,16 +328,29 @@
     )
 
 
-def plane_barrier():
+def line_peer(offset, depth):
+    return lax.rem(lax.axis_index("dp") + offset, depth)
+
+
+def along(src, dst, sends, recvs, index, offset, depth):
+    return pltpu.make_async_remote_copy(
+        src_ref=src,
+        dst_ref=dst,
+        send_sem=sends.at[index],
+        recv_sem=recvs.at[index],
+        device_id=(line_peer(offset, depth), lax.axis_index("expert")),
+        device_id_type=MESH_ID,
+    )
+
+
+def plane_barrier(depth=1):
     barrier = pltpu.get_barrier_semaphore()
-    for relation in range(1, 8):
-        pl.semaphore_signal(
-            barrier,
-            inc=1,
-            device_id=(lax.axis_index("dp"), plane_peer(relation)),
-            device_id_type=MESH_ID,
-        )
-    pl.semaphore_wait(barrier, 7)
+    targets = [(lax.axis_index("dp"), plane_peer(relation)) for relation in range(1, 8)]
+    for offset in range(1, depth):
+        targets.append((line_peer(offset, depth), lax.axis_index("expert")))
+    for target in targets:
+        pl.semaphore_signal(barrier, inc=1, device_id=target, device_id_type=MESH_ID)
+    pl.semaphore_wait(barrier, len(targets))
 
 
 def gather_copies(own, held, sends, recvs, base):
@@ -384,8 +404,8 @@
     lax.fori_loop(0, count, one, 0)
 
 
-def return_finish(parts, sides, back, out):
-    half = out.shape[0] // 2
+def return_finish(parts, sides, back):
+    half = parts[0].shape[0] // 2
     back[4].wait_recv()
     add_into(parts[0], 0, sides[0], half)
     back[5].wait_recv()
@@ -400,12 +420,6 @@
     add_into(parts[0], 0, sides[4], half)
     back[9].wait_recv()
     add_into(parts[0], half, sides[5], half)
-
-    def one(i, carry):
-        out[i] = parts[0][i]
-        return carry
-
-    lax.fori_loop(0, out.shape[0], one, 0)
     for copy in back:
         copy.wait_send()
 
@@ -415,8 +429,8 @@
 
 
 def expert_kernel(
-    cap, tab, gates, m_in, cot_in, near_in, far_in, core_in, win_in, wback_in,
-    dm_o, py_o, gin_o, gback_o, dg_o, *scratch
+    cap, depth, tab, gates, m_in, cot_in, near_in, far_in, core_in, win_in, wback_in,
+    dm_o, py_o, cy_o, gin_o, gback_o, dg_o, *scratch
 ):
     sents, slot, width = m_in.shape
     hidden = win_in.shape[1]
@@ -427,7 +441,8 @@
     cores = dict(zip((0, 2, 4, 6), scratch[24:28]))
     sides = scratch[28:34]
     win, wback = scratch[34:36]
-    xs, gs, dys, zs, dus, ys, dms, stage, dg_s, accb, acci, sends, recvs, local = scratch[36:]
+    xs, gs, dys, zs, dus, ys, dms, stage, dg_s, accb, acci = scratch[36:47]
+    line_in, line_back, sends, recvs, local = scratch[47:]
     me = lax.axis_index("expert")
     tile = min(1024, hidden)
     low, high = pl.ds(0, half), pl.ds(half, half)
@@ -448,13 +463,32 @@
     for load in loads:
         load.start()
 
-    plane_barrier()
-    to_m = gather_copies(m_in, held_m, sends, recvs, 0)
-    to_c = gather_copies(cot_in, held_c, sends, recvs, 10)
+    z = lax.axis_index("dp")
+    plane_barrier(depth)
+    to_m = gather_copies(held_m[0], held_m, sends, recvs, 0)
+    to_c = gather_copies(held_c[0], held_c, sends, recvs, 10)
     back = return_copies(parts, cores, sides, sends, recvs, 20)
     gates_back = {
         r: remote(dg_s.at[r], dg_o.at[me], sends, recvs, 30 + r, r) for r in range(1, 8)
     }
+    outputs_back = {
+        r: remote(stage.at[1], cy_o.at[r // 2], sends, recvs, 38 + r // 2, CORE)
+        for r in (1, 3, 5, 7)
+    }
+
+    def line_first(right, array):
+        offset = 1 if right else depth - 1
+        s = depth - 1 if right else 0
+        source, into = ((win, line_in), (wback, line_back))[array]
+        share = source.shape[0] // depth
+        here = pl.ds(s * share, share)
+        index = 42 + 2 * int(right) + array
+        return here, along(
+            source.at[here], into.at[int(right)], sends, recvs, index, offset, depth
+        )
+
+    for load in loads[0:2]:
+        load.wait()
     for place in (0, 1, 2, 3, 4):
         to_m[place].start()
     for place in (3, 4):
@@ -462,7 +496,7 @@
     accb[...] = jnp.zeros_like(accb)
     acci[...] = jnp.zeros_like(acci)
     place = lax.broadcasted_iota(jnp.int32, (slot, width), 0)
-    for load in loads[0:4]:
+    for load in loads[2:4]:
         load.wait()
 
     def arrive(*indices):
@@ -514,8 +548,10 @@
 
     def after(r):
         source = plane_peer(r)
-        if r >= 2:
-            pltpu.make_async_copy(stage.at[r % 2], py_o.at[r - 2], local.at[r % 2]).wait()
+        if r >= 2 and r % 2 == 0:
+            pltpu.make_async_copy(stage.at[0], py_o.at[r // 2 - 1], local.at[0]).wait()
+        if r >= 2 and r % 2 == 1:
+            outputs_back[r - 2].wait_send()
 
         def give(i, carry):
             index = tab[source, 0, 2 * cap + i]
@@ -527,7 +563,10 @@
             return carry
 
         lax.fori_loop(0, sents, give, 0, unroll=2)
-        pltpu.make_async_copy(stage.at[r % 2], py_o.at[r], local.at[r % 2]).start()
+        if r % 2 == 0:
+            pltpu.make_async_copy(stage.at[0], py_o.at[r // 2], local.at[0]).start()
+        else:
+            outputs_back[r].start()
 
         def dots(j, carry):
             product = ys[j].astype(F32) * gs[j].astype(F32)
@@ -591,26 +630,56 @@
     lax.fori_loop(0, 8, chunk, 0)
     win[...] = acci[...].astype(BF)
     wback[...] = accb[...].astype(BF)
+    for right in (True, False):
+
+        @pl.when(z == (0 if right else depth - 1))
+        def _():
+            for array in (0, 1):
+                line_first(right, array)[1].start()
+
+    return_finish(parts, sides, back)
+    kept = pltpu.make_async_copy(parts[0], dm_o, local.at[2])
+    kept.start()
+    for right in (True, False):
+
+        @pl.when(z == (1 if right else depth - 2))
+        def _():
+            for array in (0, 1):
+                here, copy = line_first(right, array)
+                copy.wait_recv()
+                source, into = ((win, line_in), (wback, line_back))[array]
+                total = source[here, :].astype(F32) + into[int(right)].astype(F32)
+                source[here, :] = total.astype(BF)
+
     stores = [
         pltpu.make_async_copy(win, gin_o, local.at[4]),
         pltpu.make_async_copy(wback, gback_o, local.at[5]),
     ]
     for store in stores:
         store.start()
-    return_finish(parts, sides, back, dm_o)
     for store in stores:
         store.wait()
+    kept.wait()
+    for right in (True, False):
+
+        @pl.when(z == (0 if right else depth - 1))
+        def _():
+            for array in (0, 1):
+                line_first(right, array)[1].wait_send()
+
+    for r in (1, 3, 5, 7):
+        outputs_back[r].wait_recv()
+    outputs_back[7].wait_send()
+    pltpu.make_async_copy(stage.at[0], py_o.at[3], local.at[0]).wait()
     for r in range(1, 8):
         gates_back[r].wait()
     for index in range(10):
         to_m[index].wait_send()
         if index > 2:
             to_c[index].wait_send()
-    for r in (6, 7):
-        pltpu.make_async_copy(stage.at[r % 2], py_o.at[r], local.at[r % 2]).wait()
-
-
-def expert_exchange(tab, gates, m, cot, near, far, core, win, wback, cap):
+
+
+def expert_exchange(tab, gates, m, cot, near, far, core, win, wback, cap, depth):
     sents, slot, width = m.shape
     hidden = win.shape[1]
     vm = pl.BlockSpec(memory_space=VM)
@@ -620,12 +689,13 @@
     cube = (sents, slot, width)
     rows = cap * slot
     return pl.pallas_call(
-        functools.partial(expert_kernel, cap),
+        functools.partial(expert_kernel, cap, depth),
         in_specs=[sm, sm] + [anywhere] * 7,
-        out_specs=[vm, anywhere, anywhere, anywhere, vm],
+        out_specs=[anywhere] * 5 + [vm],
         out_shape=[
             shape(cube, BF),
-            shape((8,) + cube, BF),
+            shape((4,) + cube, BF),
+            shape((4,) + cube, BF),
             shape((width, hidden), BF),
             shape((hidden, width), BF),
             shape((8, cap, 128), F32),
@@ -638,9 +708,10 @@
         + [VM((cap, slot, width), BF)] * 2
         + [VM((2,) + cube, BF), VM((8, cap, 128), F32)]
         + [VM((hidden, width), F32), VM((width, hidden), F32)]
+        + [VM((2, width // depth, hidden), BF), VM((2, hidden // depth, width), BF)]
         + [
-            pltpu.SemaphoreType.DMA((38,)),
-            pltpu.SemaphoreType.DMA((38,)),
+            pltpu.SemaphoreType.DMA((46,)),
+            pltpu.SemaphoreType.DMA((46,)),
             pltpu.SemaphoreType.DMA((9,)),
         ],
         compiler_params=pltpu.CompilerParams(
@@ -650,21 +721,6 @@
             flops=12 * 8 * rows * width * hidden, bytes_accessed=40 * 2**20, transcendentals=0
         ),
     )(tab, gates, m, cot, near, far, core, win, wback)
-
-
-def line_peer(offset, depth):
-    return lax.rem(lax.axis_index("dp") + offset, depth)
-
-
-def along(src, dst, sends, recvs, index, offset, depth):
-    return pltpu.make_async_remote_copy(
-        src_ref=src,
-        dst_ref=dst,
-        send_sem=sends.at[index],
-        recv_sem=recvs.at[index],
-        device_id=(line_peer(offset, depth), lax.axis_index("expert")),
-        device_id_type=MESH_ID,
-    )
 
 
 class Reduction:
@@ -769,66 +825,120 @@
         self.back_core.wait()
 
 
+class SmallSum:
+    @staticmethod
+    def semaphores(depth):
+        return 4 + depth
+
+    def __init__(self, depth, value, core_r, plane, line, sems, base):
+        sends, recvs = sems
+        self.value, self.core_r, self.plane, self.line = value, core_r, plane, line
+        self.spot = lax.axis_index("expert") // 2
+        self.z = lax.axis_index("dp")
+        self.to_core = remote(value, core_r, sends, recvs, base, CORE)
+        spot = plane.at[self.spot]
+        self.to_plane = [
+            remote(spot, spot, sends, recvs, base + 1 + place, relation)
+            for place, relation in enumerate((2, 4, 6))
+        ]
+        spot = line.at[self.z]
+        self.to_line = [
+            along(spot, spot, sends, recvs, base + 3 + offset, offset, depth)
+            for offset in range(1, depth)
+        ]
+
+    def send_core(self):
+        self.to_core.start()
+
+    def send_plane(self):
+        self.to_core.wait()
+        self.plane[self.spot] = self.value[...] + self.core_r[...]
+        for copy in self.to_plane:
+            copy.start()
+
+    def send_line(self):
+        for copy in self.to_plane:
+            copy.wait()
+        total = self.plane[0]
+        for place in range(1, 4):
+            total = total + self.plane[place]
+        self.line[self.z] = total
+        for copy in self.to_line:
+            copy.start()
+
+    def finish(self, out):
+        for copy in self.to_line:
+            copy.wait()
+        total = self.line[0]
+        for place in range(1, self.line.shape[0]):
+            total = total + self.line[place]
+        out[...] = total
+
+
 def backward_kernel(
-    heads, depth, len_ref, x_ref, cot_ref, dm_ref, h_ref, act, q, k, v, ctx, p_ref,
-    wq, wk, wv, wo, g1, g2, attn_sum, plan, tasks, lengths, dots, py, gin, gback,
-    ig_o, out_o, fin_o, fin_0, fin_1, gin_o, gback_o, small_o, *scratch
+    heads, depth, len_ref, g1, g2, attn_sum, plan, tasks, lengths, dots,
+    x_in, cot_in, dm_in, h_in, act_in, q_in, k_in, v_in, ctx_in, p_in,
+    wq_in, wk_in, wv_in, wo_in, py, cy, gin, gback,
+    ig_o, out_o, gq_o, gk_o, gv_o, go_o, gin_o, gback_o, small_o, *scratch
 ):
+    inputs = (
+        x_in, cot_in, dm_in, h_in, act_in, q_in, k_in, v_in, ctx_in, p_in,
+        wq_in, wk_in, wv_in, wo_in, gin, gback,
+    )
+    held = scratch[0:16]
+    (
+        x_ref, cot_ref, dm_ref, h_ref, act, q, k, v, ctx, p_ref, wq, wk, wv, wo, gin_s, gback_s,
+    ) = held
+    parts = dict(zip((0, 2, 4, 6), scratch[16:20]))
+    cores = dict(zip((0, 2, 4, 6), scratch[20:24]))
+    sides = scratch[24:30]
+    dh_s, da_s, dctx_s, dq_s, dk_s, dv_s = scratch[30:36]
+    red = scratch[36:57]
+    line_in, line_back, extra_in, extra_back = scratch[57:61]
+    small, small_core, small_plane, small_line = scratch[61:65]
+    sends, recvs, local = scratch[65:]
+    sems = (sends, recvs)
     sents, slot, width = x_ref.shape
-    total_rows = sents * slot
     head = width // heads
     group = max(1, min(heads, 256 // head))
     span = group * head
     scale = head ** -0.5
     count = 4 if sents % 4 == 0 else 1
     rows_per = count * slot
+    half = sents // 2
     z = lax.axis_index("dp")
-    parts = {0: scratch[0], 2: scratch[1], 4: scratch[2], 6: scratch[3]}
-    cores = dict(zip((0, 2, 4, 6), scratch[4:8]))
-    sides = scratch[8:14]
-    dh_s, da_s, dctx_s, dq_s, dk_s, dv_s = scratch[14:20]
-    red = scratch[20:38]
-    line_in, line_back, extra_in, extra_back = scratch[38:42]
-    small, small_core, small_plane, small_line = scratch[42:46]
-    gin_s, gback_s = scratch[46:48]
-    sends, recvs, local = scratch[48:]
-    sems = (sends, recvs)
-    grad_loads = [
-        pltpu.make_async_copy(gin, gin_s, local.at[4]),
-        pltpu.make_async_copy(gback, gback_s, local.at[5]),
-    ]
-    for load in grad_loads:
-        load.start()
 
     loads = {
-        r: pltpu.make_async_copy(py.at[r], parts[r], local.at[r // 2]) for r in (0, 2, 4, 6)
+        id(ref): pltpu.make_async_copy(source, ref, local.at[place])
+        for place, (source, ref) in enumerate(zip(inputs, held))
     }
-    for r in (6, 2, 4, 0):
-        loads[r].start()
-    barrier = pltpu.get_barrier_semaphore()
-    for relation in range(1, 8):
-        pl.semaphore_signal(
-            barrier, inc=1, device_id=(z, plane_peer(relation)), device_id_type=MESH_ID
+    for place, r in enumerate((0, 2, 4, 6)):
+        loads[id(parts[r])] = pltpu.make_async_copy(
+            py.at[r // 2], parts[r], local.at[16 + place]
         )
-    for offset in range(1, depth):
-        pl.semaphore_signal(
-            barrier,
-            inc=1,
-            device_id=(line_peer(offset, depth), lax.axis_index("expert")),
-            device_id_type=MESH_ID,
+        loads[id(cores[r])] = pltpu.make_async_copy(
+            cy.at[r // 2], cores[r], local.at[20 + place]
         )
-    pl.semaphore_wait(barrier, 6 + depth)
-
-    all_parts = dict(parts)
-    for r in (1, 3, 5, 7):
-        all_parts[r] = py.at[r]
+
+    def begin(*refs):
+        for ref in refs:
+            loads[id(ref)].start()
+
+    def ready(*refs):
+        for ref in refs:
+            loads[id(ref)].wait()
+
+    begin(gin_s, gback_s, h_ref, dm_ref, cot_ref, wo, parts[6], cores[6], ctx)
+    begin(parts[2], cores[2], parts[4], cores[4], q, k, v, p_ref, act, parts[0], cores[0])
+    begin(wq, wk, wv, x_ref)
+    plane_barrier(depth)
+
+    all_parts = {r: parts[r - r % 2] for r in range(8)}
     back = return_copies(all_parts, cores, sides, sends, recvs, 0)
-    for r in (7, 3, 5, 1):
-        back[r // 2].start()
 
     base = 10
-    in_rows = gin.shape[0] // depth
-    back_rows = gback.shape[0] // depth
+    in_rows = gin_s.shape[0] // depth
+    back_rows = gback_s.shape[0] // depth
 
     def line_piece(s, array, right, last):
         offset = 1 if right else depth - 1
@@ -868,7 +978,7 @@
         for right in (True, False):
             every = pieces(right)
             edge = 0 if right else depth - 1
-            opening = range(0, 1 + ahead) if t == 0 else range(t + ahead, t + ahead + 1)
+            opening = range(2, 3 + ahead) if t == 0 else range(t + ahead + 2, t + ahead + 3)
 
             @pl.when(z == edge)
             def _():
@@ -877,14 +987,17 @@
                         start_piece(*every[number], right)
 
             for number, (s, array) in enumerate(every):
-                hops = t - number
                 away = s if right else depth - 1 - s
-                if 0 < hops < away:
+                for hops in range(1, away):
+                    given = hops == 1 and number < 2
+                    if t != (0 if given else number + hops - 1):
+                        continue
 
                     @pl.when(z == (hops if right else depth - 1 - hops))
                     def _():
-                        line_piece(s, array, right, False).wait_recv()
-                        add_piece(s, array)
+                        if not given:
+                            line_piece(s, array, right, False).wait_recv()
+                            add_piece(s, array)
                         start_piece(s, array, right)
 
     def line_end():
@@ -909,31 +1022,26 @@
 
         for s in range(depth):
             for array in (0, 1):
-
-                @pl.when(z < s)
+                first_right = 1 if s == depth - 1 else 0
+                first_left = depth - 2 if s == 0 else depth - 1
+
+                @pl.when(jnp.logical_and(z < s, z >= first_right))
                 def _():
                     line_piece(s, array, True, False).wait_send()
 
-                @pl.when(z > s)
+                @pl.when(jnp.logical_and(z > s, z <= first_left))
                 def _():
                     line_piece(s, array, False, False).wait_send()
 
-    for load in grad_loads:
-        load.wait()
-    line_service(0)
-
     base_red = base + 4 * depth
     per = Reduction.semaphores(depth)
-    reds = []
-    for place, final in enumerate((fin_o, fin_0, fin_1)):
-        value, wide, core_r, plane_r, line_s, line_r = red[6 * place : 6 * place + 6]
-        reds.append(
-            Reduction(
-                depth, value, wide, core_r, plane_r, line_s, line_r, final, sems,
-                base_red + place * per,
-            )
-        )
-    red_o, red_0, red_1 = reds
+    red_o, red_0, red_1 = [
+        Reduction(depth, *red[7 * place : 7 * place + 7], sems, base_red + place * per)
+        for place in range(3)
+    ]
+    sums = SmallSum(
+        depth, small, small_core, small_plane, small_line, sems, base_red + 3 * per
+    )
 
     small[...] = jnp.zeros_like(small)
     small[4:5] = attn_sum[...]
@@ -969,22 +1077,6 @@
         dctx_s[rows, :] = mm(dattn, wo[...], 1, 1).astype(BF)
         return carry
 
-    lax.fori_loop(0, sents // count, first, 0)
-    hit = plan[0:experts] > 0.5
-    place = plan[experts : 2 * experts]
-    gate = plan[2 * experts : 3 * experts]
-    taken = jnp.zeros(gate.shape, F32)
-    for j in range(dots.shape[1]):
-        taken = taken + jnp.where(place == float(j), dots[:, j, 0:sents], 0.0)
-    inner = jnp.sum(gate * taken, axis=0, keepdims=True)
-    dlogit = jnp.where(hit, gate * (taken - inner), 0.0)
-    hot = lax.broadcasted_iota(jnp.int32, (slot, sents), 0) == tasks[...]
-    small[8 : 8 + experts, 0:slot] = lax.dot_general(
-        dlogit, hot.astype(F32), (((1,), (1,)), ((), ())), precision=lax.Precision.HIGHEST,
-        preferred_element_type=F32,
-    )
-    red_o.value[...] = mm(ctx[...], da_s[...], 0, 0)
-    red_o.send_core()
     mask = block_diagonal(group, slot, head)
 
     def pull(part, into):
@@ -1006,24 +1098,9 @@
         into.value[2 * width : 3 * width, :] = mm(act[...], dv_s[:, cols], 0, 0)
         into.send_core()
 
-    def returned(r, starts):
-        loads[r].wait()
-        back[r // 2].wait_recv()
+    def returned(r):
+        ready(parts[r], cores[r])
         add_into(parts[r], 0, cores[r], sents)
-        for index in starts:
-            back[index].start()
-
-    pull(0, red_0)
-    red_o.send_plane()
-    line_service(1)
-    returned(6, (5, 7))
-    pull(1, red_1)
-    red_0.send_plane()
-    red_o.send_line()
-    line_service(2)
-    returned(2, ())
-    returned(4, ())
-    returned(0, ())
 
     def last(c, carry):
         rows = pl.ds(pl.multiple_of(c * rows_per, rows_per), rows_per)
@@ -1039,38 +1116,6 @@
         ig_o[pl.ds(c * count, count)] = dx.astype(BF).reshape(count, slot, width)
         return carry
 
-    lax.fori_loop(0, sents // count, last, 0)
-    red_1.send_plane()
-    back[4].start()
-    back[6].start()
-    red_o.send_back_line()
-    red_0.send_line()
-    line_service(3)
-    red_o.send_back_plane()
-    red_0.send_back_line()
-    red_1.send_line()
-    half = sents // 2
-    back[5].wait_recv()
-    add_into(parts[4], 0, sides[1], half)
-    back[7].wait_recv()
-    add_into(parts[2], half, sides[3], half)
-    line_service(4)
-    red_o.send_back_core()
-    red_0.send_back_plane()
-    red_1.send_back_line()
-    back[8].start()
-    back[9].start()
-    red_1.send_back_plane()
-    red_0.send_back_core()
-    back[4].wait_recv()
-    add_into(parts[0], 0, sides[0], half)
-    back[6].wait_recv()
-    add_into(parts[0], half, sides[2], half)
-    line_service(5)
-    red_1.send_back_core()
-    back[8].wait_recv()
-    back[9].wait_recv()
-
     def outcome(low, side):
         def one(i, carry):
             at = low + i
@@ -1085,61 +1130,105 @@
 
         lax.fori_loop(0, half, one, 0)
 
+    def gate_gradient():
+        hit = plan[0:experts] > 0.5
+        place = plan[experts : 2 * experts]
+        gate = plan[2 * experts : 3 * experts]
+        taken = jnp.zeros(gate.shape, F32)
+        for j in range(dots.shape[1]):
+            taken = taken + jnp.where(place == float(j), dots[:, j, 0:sents], 0.0)
+        inner = jnp.sum(gate * taken, axis=0, keepdims=True)
+        dlogit = jnp.where(hit, gate * (taken - inner), 0.0)
+        hot = lax.broadcasted_iota(jnp.int32, (slot, sents), 0) == tasks[...]
+        small[8 : 8 + experts, 0:slot] = lax.dot_general(
+            dlogit, hot.astype(F32), (((1,), (1,)), ((), ())),
+            precision=lax.Precision.HIGHEST, preferred_element_type=F32,
+        )
+
+    ready(gin_s, gback_s)
+    line_service(0)
+    returned(6)
+    back[5].start()
+    back[7].start()
+    ready(h_ref, dm_ref, cot_ref, wo)
+    lax.fori_loop(0, sents // count, first, 0)
+    ready(ctx)
+    red_o.value[...] = mm(ctx[...], da_s[...], 0, 0)
+    red_o.send_core()
+    returned(2)
+    returned(4)
+    ready(q, k, v, p_ref, act)
+    pull(0, red_0)
+    red_o.send_plane()
+    back[4].start()
+    back[6].start()
+    line_service(1)
+    back[5].wait_recv()
+    add_into(parts[4], 0, sides[1], half)
+    back[7].wait_recv()
+    add_into(parts[2], half, sides[3], half)
+    pull(1, red_1)
+    red_0.send_plane()
+    back[8].start()
+    back[9].start()
+    red_o.send_line()
+    line_service(2)
+    ready(wq, wk, wv, x_ref)
+    lax.fori_loop(0, sents // count, last, 0)
+    red_1.send_plane()
+    red_o.send_back_line()
+    gate_gradient()
+    returned(0)
+    red_0.send_line()
+    line_service(3)
+    back[4].wait_recv()
+    add_into(parts[0], 0, sides[0], half)
+    back[6].wait_recv()
+    add_into(parts[0], half, sides[2], half)
+    red_o.send_back_plane()
+    red_0.send_back_line()
+    red_1.send_line()
+    back[8].wait_recv()
     outcome(0, sides[4])
+    back[9].wait_recv()
     outcome(half, sides[5])
-
-    base_small = base_red + 3 * per
-    me = lax.axis_index("expert")
-    to_core = remote(small, small_core, sends, recvs, base_small, CORE)
-    to_core.start()
-    to_core.wait()
-    spot = me // 2
-    small_plane[spot] = small[...] + small_core[...]
-    to_plane = [
-        remote(
-            small_plane.at[spot], small_plane.at[spot], sends, recvs, base_small + 1 + place,
-            relation,
-        )
-        for place, relation in enumerate((2, 4, 6))
-    ]
-    for copy in to_plane:
-        copy.start()
-    for copy in to_plane:
-        copy.wait()
-    total = small_plane[0]
-    for place in range(1, 4):
-        total = total + small_plane[place]
-    small_line[z] = total
-    to_line = [
-        along(
-            small_line.at[z], small_line.at[z], sends, recvs, base_small + 3 + offset, offset,
-            depth,
-        )
-        for offset in range(1, depth)
-    ]
-    for copy in to_line:
-        copy.start()
-    for copy in to_line:
-        copy.wait()
-    total = small_line[0]
-    for place in range(1, depth):
-        total = total + small_line[place]
-    small_o[...] = total
-    for one in reds:
-        one.finish()
+    sums.send_core()
+    red_o.send_back_core()
+    red_0.send_back_plane()
+    red_1.send_back_line()
+    sums.send_plane()
+    red_1.send_back_plane()
+    red_0.send_back_core()
+    sums.send_line()
+    red_1.send_back_core()
+    red_o.finish()
+    go_o[...] = red_o.final[...]
+    red_0.finish()
+
+    def share(red, low):
+        for place, ref in enumerate((gq_o, gk_o, gv_o)):
+            ref[:, low : low + red.final.shape[1]] = red.final[
+                place * width : (place + 1) * width, :
+            ]
+
+    share(red_0, 0)
+    sums.finish(small_o)
+    red_1.finish()
+    share(red_1, span)
     line_end()
-    for copy in back:
+    for copy in back[4:]:
         copy.wait_send()
 
 
 def backward_exchange(
     depth, lengths, tokens, cot, dm, hidden, act, q, k, v, ctx, prob, wq, wk, wv, wo, g1, g2,
-    attn_sum, plan, tasks, dots, py, gin, gback, heads,
+    attn_sum, plan, tasks, dots, py, cy, gin, gback, heads,
 ):
     sents, slot, width = tokens.shape
     total = sents * slot
     small = jax.ShapeDtypeStruct((16, width), F32)
     vm = pl.BlockSpec(memory_space=VM)
+    anywhere = pl.BlockSpec(memory_space=pl.ANY)
     shape = jax.ShapeDtypeStruct
     cube = (sents, slot, width)
     head = width // heads
@@ -1154,21 +1243,23 @@
             VM((3, rows // 8, cols), BF),
             VM((rows // 8, cols), BF),
             VM((depth - 1, rows // 8 // depth, cols), BF),
+            VM((rows, cols), BF),
         ]
     in_share = (gin.shape[0] // depth, gin.shape[1])
     back_share = (gback.shape[0] // depth, gback.shape[1])
-    semaphores = 10 + 4 * depth + 3 * Reduction.semaphores(depth) + 4 + depth
+    semaphores = 10 + 4 * depth + 3 * Reduction.semaphores(depth) + SmallSum.semaphores(depth)
+    large = (
+        tokens, cot, dm, hidden, act, q, k, v, ctx, prob, wq, wk, wv, wo, py, cy, gin, gback,
+    )
     return pl.pallas_call(
         functools.partial(backward_kernel, heads, depth),
-        in_specs=[pl.BlockSpec(memory_space=pltpu.SMEM)]
-        + [vm] * 21
-        + [pl.BlockSpec(memory_space=pl.ANY), pl.BlockSpec(memory_space=pl.ANY)]
-        + [pl.BlockSpec(memory_space=pl.ANY)],
-        out_specs=[vm] * 8,
+        in_specs=[pl.BlockSpec(memory_space=pltpu.SMEM)] + [vm] * 7 + [anywhere] * len(large),
+        out_specs=[vm] * 9,
         out_shape=[shape(cube, BF), shape(cube, BF)]
-        + [shape(piece, BF) for piece in pieces]
+        + [shape((width, width), BF)] * 4
         + [shape(in_share, F32), shape(back_share, F32), shape(small.shape, F32)],
-        scratch_shapes=[VM(cube, BF)] * 8
+        scratch_shapes=[VM(ref.shape, ref.dtype) for ref in large[:14] + large[16:]]
+        + [VM(cube, BF)] * 8
         + [VM((sents // 2, slot, width), BF)] * 6
         + [VM((total, width), F32)]
         + [VM((total, width), BF)] * 5
@@ -1177,11 +1268,10 @@
         + [VM(in_share, BF), VM(back_share, BF)]
         + [VM(small.shape, F32)] * 2
         + [VM((4,) + small.shape, F32), VM((depth,) + small.shape, F32)]
-        + [VM(gin.shape, BF), VM(gback.shape, BF)]
         + [
             pltpu.SemaphoreType.DMA((semaphores,)),
             pltpu.SemaphoreType.DMA((semaphores,)),
-            pltpu.SemaphoreType.DMA((6,)),
+            pltpu.SemaphoreType.DMA((24,)),
         ],
         compiler_params=pltpu.CompilerParams(
             collective_id=2, has_side_effects=True, vmem_limit_bytes=63 * 2**20
@@ -1190,9 +1280,84 @@
             flops=16 * total * width * width, bytes_accessed=40 * 2**20, transcendentals=0
         ),
     )(
-        lengths, tokens, cot, dm, hidden, act, q, k, v, ctx, prob, wq, wk, wv, wo,
-        g1[None], g2[None], attn_sum, plan, tasks[None], lengths[None], dots, py, gin, gback,
-    )
+        lengths, g1[None], g2[None], attn_sum, plan, tasks[None], lengths[None], dots, *large
+    )
+
+
+def outputs_kernel(
+    out_in, ig_in, gin_in, gback_in, q_in, k_in, v_in, o_in, small,
+    out_o, ig_o, gin_o, gback_o, q_o, k_o, v_o, o_o, l1g, l1b, l2g, l2b, table_o, rms_o,
+    low, wide, cubes, share_in, share_back, sems,
+):
+    fetches = [
+        pltpu.make_async_copy(src, low.at[place], sems.at[place])
+        for place, src in enumerate((q_in, k_in, v_in, o_in))
+    ]
+    stores = [
+        pltpu.make_async_copy(wide.at[place], dst, sems.at[4 + place])
+        for place, dst in enumerate((q_o, k_o, v_o, o_o))
+    ]
+    moves = [
+        (pltpu.make_async_copy(src, held, sems.at[8 + place]),
+         pltpu.make_async_copy(held, dst, sems.at[12 + place]))
+        for place, (src, held, dst) in enumerate(
+            [
+                (out_in, cubes.at[0], out_o),
+                (ig_in, cubes.at[1], ig_o),
+                (gin_in, share_in, gin_o),
+                (gback_in, share_back, gback_o),
+            ]
+        )
+    ]
+    for fetch in fetches:
+        fetch.start()
+    for enter, _ in moves:
+        enter.start()
+    width = small.shape[1]
+    for row, ref in enumerate((l1g, l1b, l2g, l2b)):
+        ref[...] = small[row : row + 1]
+    table_o[...] = small[8 : 8 + table_o.shape[0], 0 : table_o.shape[1]]
+    sums = jnp.sum(small[4:8], axis=1, keepdims=True)
+    ratio = jnp.sqrt(sums / (sums[3:4] * width))
+    lane = lax.broadcasted_iota(jnp.int32, (1, 3), 1)
+    pair = jnp.where(lane == 1, ratio[0:1], ratio[2:3])
+    rms_o[...] = jnp.where(lane == 0, ratio[1:2], pair)
+    for place in range(4):
+        fetches[place].wait()
+        wide[place] = low[place].astype(F32)
+        stores[place].start()
+    for enter, leave in moves:
+        enter.wait()
+        leave.start()
+    for store in stores:
+        store.wait()
+    for _, leave in moves:
+        leave.wait()
+
+
+def place_outputs(out, ig, gin, gback, q, k, v, o, small, experts, ntasks):
+    width = small.shape[1]
+    vm = pl.BlockSpec(memory_space=VM)
+    anywhere = pl.BlockSpec(memory_space=pl.ANY)
+    shape = jax.ShapeDtypeStruct
+    return pl.pallas_call(
+        outputs_kernel,
+        in_specs=[anywhere] * 8 + [vm],
+        out_specs=[anywhere] * 8 + [vm] * 6,
+        out_shape=[shape(a.shape, a.dtype) for a in (out, ig, gin, gback)]
+        + [shape(q.shape, F32)] * 4
+        + [shape((1, width), F32)] * 4
+        + [shape((experts, ntasks), F32), shape((1, 3), F32)],
+        scratch_shapes=[
+            VM((4,) + q.shape, BF),
+            VM((4,) + q.shape, F32),
+            VM((2,) + out.shape, BF),
+            VM(gin.shape, F32),
+            VM(gback.shape, F32),
+            pltpu.SemaphoreType.DMA((16,)),
+        ],
+        compiler_params=pltpu.CompilerParams(vmem_limit_bytes=60 * 2**20),
+    )(out, ig, gin, gback, q, k, v, o, small)
 
 
 def local(
@@ -1420,35 +1585,40 @@
         gate_slots, near, far, core,
     ) = attention_forward(
         tokens, lengths, w_query, w_key, w_value, w_out, ln1_gain, ln1_bias, ln2_gain, ln2_bias,
-        tasks, routes, gate_table, cotangent, heads, capacity,
-    )
-    dmixed, parts_back, in_local, back_local, slot_dots = expert_exchange(
-        places, gate_slots, mixed, cotangent, near, far, core, w_in[0], w_back[0], capacity
-    )
-    input_grad, output, sum_o, sum_0, sum_1, in_share, back_share, small = backward_exchange(
-        depth, lengths, tokens, cotangent, dmixed, hidden, act, query, keyed, valued, context,
-        prob, w_query, w_key, w_value, w_out, ln1_gain, ln2_gain,
-        attn_sum, plan, tasks, slot_dots, parts_back, in_local, back_local, heads,
-    )
-    sides = jnp.concatenate([sum_0, sum_1], axis=1).astype(jnp.float32)
-    wide = lambda place: sides[place * width : (place + 1) * width]
-    sums = jnp.sum(small[4:8], axis=1)
-    rms = jnp.sqrt(jnp.stack([sums[1], sums[0], sums[2]]) / (sums[3] * width))
+        tasks, routes.T, gate_table.T, cotangent, heads, capacity,
+    )
+    dmixed, parts_back, cores_back, in_local, back_local, slot_dots = expert_exchange(
+        places, gate_slots, mixed, cotangent, near, far, core, w_in[0], w_back[0], capacity, depth
+    )
+    input_grad, output, sum_q, sum_k, sum_v, sum_o, in_share, back_share, small = (
+        backward_exchange(
+            depth, lengths, tokens, cotangent, dmixed, hidden, act, query, keyed, valued,
+            context, prob, w_query, w_key, w_value, w_out, ln1_gain, ln2_gain, attn_sum, plan,
+            tasks, slot_dots, parts_back, cores_back, in_local, back_local, heads,
+        )
+    )
+    (
+        output, input_grad, in_share, back_share, grad_q, grad_k, grad_v, grad_o,
+        gain1, bias1, gain2, bias2, table_grad, rms,
+    ) = place_outputs(
+        output, input_grad, in_share, back_share, sum_q, sum_k, sum_v, sum_o, small,
+        experts, gate_table.shape[0],
+    )
     return (
         output,
         input_grad,
-        small[8 : 8 + experts, : gate_table.shape[0]].T,
-        small[0],
-        small[1],
-        small[2],
-        small[3],
-        wide(0),
-        wide(1),
-        wide(2),
-        sum_o.astype(jnp.float32),
+        table_grad.T,
+        gain1.reshape(-1),
+        bias1.reshape(-1),
+        gain2.reshape(-1),
+        bias2.reshape(-1),
+        grad_q,
+        grad_k,
+        grad_v,
+        grad_o,
         in_share[None],
         back_share[None],
-        rms,
+        rms.reshape(-1),
     )
 
 
@@ -1489,5 +1659,6 @@
     )
     plane = dict(mesh.shape)["expert"]
     depth = dict(mesh.shape)["dp"]
-    body = functools.partial(local_plane, depth) if plane == 2 * 2 * 2 else local
+    cube = plane == 2 * 2 * 2 and depth > 2
+    body = functools.partial(local_plane, depth) if cube else local
     return jax.shard_map(body, mesh=mesh, in_specs=in_specs, out_specs=out_specs, check_vma=False)

time: 276 us -> 235 us (0.85)
  Pallas kernels: 255 us -> 234 us
  local copies, waits for them, and re-layouts: 12.4 us -> 0 us
  other arithmetic: 6.06 us -> 0 us
    pallas_call x1, Pallas kernels: 108 us -> 77.1 us  [backward_exchange(): pl.pallas_call(functools.partial(backward_kernel, heads, depth), in_specs...]
    pallas_call x1 -> x2, Pallas kernels: 126 us -> 136 us  [the longest x1 128 us: expert_exchange(): pl.pallas_call(functools.partial(expert_kernel, cap, depth), in_specs=[sm...]
    unnamed x18 -> x0, local copies, waits for them, and re-layouts: 7.28 us -> none
    slice x3 -> x0, local copies, waits for them, and re-layouts: 3.79 us -> none  [the longest x1 1.73 us: local_plane(): wide = lambda place: sides[place * width:(place + 1) * width]]
where the time goes in v5:
time: 235 us
  Pallas kernels  234 us (100%)
    pallas_call x1, Pallas kernels, expert_exchange(): pl.pallas_call(functools.partial(expert_kernel, cap, depth), in_specs=[sm...  128 us
    pallas_call x1, Pallas kernels, backward_exchange(): pl.pallas_call(functools.partial(backward_kernel, heads, depth), in_specs...  77.1 us
    pallas_call x1, Pallas kernels, attention_forward(): pl.pallas_call(functools.partial(attention_forward_kernel, heads, cap), g...  21.5 us
    pallas_call x1, Pallas kernels, place_outputs(): pl.pallas_call(outputs_kernel, in_specs=[anywhere] * 8 + [vm], out_specs=...  7.15 us

profile of v5, /device:TPU:0, one launch (start us, length us, event | category | flops | bytes accessed | tf_op | source)
XLA Modules:
  0.0 235.0 jit_solution(17798985690348161018)
XLA Ops:
  0.6 21.5 %shard_map.263 = (bf16[1024,512]{1,0:T(8,128)(2,1)}, bf16[1024,512]{1,0:T(8,128)(2,1)}, bf16[1024,512]{1,0:T(8,128)(2,1)}, bf16[1024,512]{1,0:T(8,128)(2,1)}, bf...) custom-call(s32[16]{0:T(128)} %len_ref.3, ...), custom_call_target="tpu_custom_call" | custom-call | flops 2281701376 | bytes 8388608 | tf_op jit(solution)/shard_map/pallas_call | solution.py:237
  22.1 128.5 %shard_map.264 = (bf16[16,64,512]{2,1,0:T(8,128)(2,1)}, bf16[4,16,64,512]{3,2,1,0:T(8,128)(2,1)}, bf16[4,16,64,512]{3,2,1,0:T(8,128)(2,1)}, bf16[512,2048]{1,0:T...) custom-call(s32[8,8,128]{2,1,0:T(8,128)} %get-tuple-element.60.tab, f32[8,8,128]{2,1,0:T(8,128)} %get-tuple-element.61.gates, ...), custom_call_target="tpu_custom_call" | custom-call | flops 51539607552 | bytes 41943040 | tf_op jit(solution)/shard_map/pallas_call | solution.py:691
  150.6 77.1 %shard_map.265 = (bf16[16,64,512]{2,1,0:T(8,128)(2,1)}, bf16[16,64,512]{2,1,0:T(8,128)(2,1)}, bf16[512,512]{1,0:T(8,128)(2,1)}, bf16[512,512]{1,0:T(8,128)(2,1)}...) custom-call(s32[16]{0:T(128)} %len_ref.3, ...), custom_call_target="tpu_custom_call" | custom-call | flops 4294967296 | bytes 41943040 | tf_op jit(solution)/shard_map/pallas_call | solution.py:1254
  227.7 7.1 %shard_map.266 = (bf16[16,64,512]{2,1,0:T(8,128)(2,1)}, bf16[16,64,512]{2,1,0:T(8,128)(2,1)}, f32[128,2048]{1,0:T(8,128)}, f32[512,512]{1,0:T(8,128)}, f32[512,5...) custom-call(bf16[16,64,512]{2,1,0:T(8,128)(2,1)} %get-tuple-element., ...), custom_call_target="tpu_custom_call" | custom-call | tf_op jit(solution)/shard_map/pallas_call | solution.py:1343

commit v6 on v5

--- a/solution.py
+++ b/solution.py
@@ -397,11 +397,10 @@
 
 def add_into(target, start, other, count):
     def one(i, carry):
-        total = target[start + i].astype(F32) + other[i].astype(F32)
-        target[start + i] = total.astype(BF)
+        target[start + i] = target[start + i] + other[i]
         return carry
 
-    lax.fori_loop(0, count, one, 0)
+    lax.fori_loop(0, count, one, 0, unroll=8)
 
 
 def return_finish(parts, sides, back):
@@ -428,6 +427,15 @@
 GELU_B = 0.044715
 
 
+def expert_steps():
+    waves = (((0, 1), (0,)), ((2, 3, 4, 5), (2,)), ((6, 7), ()))
+    steps = []
+    for taken, closed in waves:
+        steps += [("F", r) for r in taken] + [("B", r) for r in taken]
+        steps += [("U", r) for r in closed] + [("V", r) for r in closed]
+    return steps
+
+
 def expert_kernel(
     cap, depth, tab, gates, m_in, cot_in, near_in, far_in, core_in, win_in, wback_in,
     dm_o, py_o, cy_o, gin_o, gback_o, dg_o, *scratch
@@ -437,14 +445,20 @@
     half = sents // 2
     held_m = dict(zip(range(8), scratch[0:8]))
     held_c = dict(zip(range(8), scratch[8:16]))
-    parts = dict(zip(range(8), scratch[16:24]))
-    cores = dict(zip((0, 2, 4, 6), scratch[24:28]))
-    sides = scratch[28:34]
-    win, wback = scratch[34:36]
-    xs, gs, dys, zs, dus, ys, dms, stage, dg_s, accb, acci = scratch[36:47]
-    line_in, line_back, sends, recvs, local = scratch[47:]
+    sides = scratch[16:22]
+    win, wback = scratch[22:24]
+    first_part, xs, dys, zs, dus, ys, dms, stage, dg_s, accb, acci = scratch[24:35]
+    line_in, line_back, sends, recvs, local, free = scratch[35:]
+    parts = {
+        0: first_part, 1: held_c[1], 2: held_m[0], 3: held_c[3],
+        4: held_c[0], 5: held_c[5], 6: held_c[6], 7: held_c[7],
+    }
+    cores = {0: held_m[1], 2: held_m[3], 4: held_m[5], 6: held_m[7]}
+    sets = {r: r - 2 if r in (4, 5) else r % 2 for r in range(8)}
     me = lax.axis_index("expert")
-    tile = min(1024, hidden)
+    z = lax.axis_index("dp")
+    tile = min(512, hidden)
+    rows = cap * slot
     low, high = pl.ds(0, half), pl.ds(half, half)
     loads = [
         pltpu.make_async_copy(src, dst, local.at[2 + place])
@@ -462,8 +476,6 @@
     ]
     for load in loads:
         load.start()
-
-    z = lax.axis_index("dp")
     plane_barrier(depth)
     to_m = gather_copies(held_m[0], held_m, sends, recvs, 0)
     to_c = gather_copies(held_c[0], held_c, sends, recvs, 10)
@@ -472,8 +484,10 @@
         r: remote(dg_s.at[r], dg_o.at[me], sends, recvs, 30 + r, r) for r in range(1, 8)
     }
     outputs_back = {
-        r: remote(stage.at[1], cy_o.at[r // 2], sends, recvs, 38 + r // 2, CORE)
-        for r in (1, 3, 5, 7)
+        r: remote(stage, cy_o.at[r // 2], sends, recvs, 38 + r // 2, CORE) for r in (1, 3, 5, 7)
+    }
+    outputs_here = {
+        r: pltpu.make_async_copy(stage, py_o.at[r // 2], local.at[0]) for r in (0, 2, 4, 6)
     }
 
     def line_first(right, array):
@@ -483,93 +497,112 @@
         share = source.shape[0] // depth
         here = pl.ds(s * share, share)
         index = 42 + 2 * int(right) + array
-        return here, along(
-            source.at[here], into.at[int(right)], sends, recvs, index, offset, depth
-        )
+        return here, along(source.at[here], into, sends, recvs, index, offset, depth)
+
+    def line_open(array):
+        for right in (True, False):
+
+            @pl.when(z == (0 if right else depth - 1))
+            def _():
+                line_first(right, array)[1].start()
 
     for load in loads[0:2]:
         load.wait()
-    for place in (0, 1, 2, 3, 4):
-        to_m[place].start()
-    for place in (3, 4):
-        to_c[place].start()
+    for index in (0, 1, 2, 3, 4):
+        to_m[index].start()
+    for index in (3, 4):
+        to_c[index].start()
     accb[...] = jnp.zeros_like(accb)
     acci[...] = jnp.zeros_like(acci)
     place = lax.broadcasted_iota(jnp.int32, (slot, width), 0)
     for load in loads[2:4]:
         load.wait()
 
-    def arrive(*indices):
-        for index in indices:
-            to_m[index].wait_recv()
-            if index > 2:
-                to_c[index].wait_recv()
-
-    def forward(*indices):
-        for index in indices:
-            to_m[index].start()
-            to_c[index].start()
-
-    def before(r):
+    def before_forward(r):
         if r == 1:
-            arrive(2)
+            to_m[2].wait_recv()
+        if r == 2:
+            to_m[0].wait_recv()
+            to_m[5].start()
+            to_m[1].wait_recv()
+            to_m[6].start()
+            for load in loads[5:7]:
+                load.wait()
+            to_c[5].start()
+            to_c[6].start()
+            to_m[3].wait_recv()
+            to_m[7].start()
+            to_m[4].wait_recv()
+            to_m[8].start()
+        if r == 3:
+            to_m[7].wait_recv()
+        if r == 5:
+            to_m[8].wait_recv()
+        if r == 6:
+            to_m[5].wait_recv()
+            to_m[6].wait_recv()
+            to_m[9].start()
+        if r == 7:
+            to_m[9].wait_recv()
+        source = plane_peer(r)
+
+        def fetch(j, carry):
+            xs[sets[r], j] = held_m[r][tab[source, 0, j]]
+            return carry
+
+        lax.fori_loop(0, cap, fetch, 0, unroll=True)
+        if r % 2 == 1:
+            pl.semaphore_signal(
+                free.at[r // 2], inc=1, device_id=(z, plane_peer(CORE)), device_id_type=MESH_ID
+            )
+
+    def after_forward(r):
+        source = plane_peer(r)
+        if r > 0 and r % 2 == 1:
+            outputs_here[r - 1].wait()
+        if r > 0 and r % 2 == 0:
+            outputs_back[r - 1].wait_send()
+
+        def give(i, carry):
+            index = tab[source, 0, 2 * cap + i]
+            there = jnp.maximum(index, 0)
+            gate = jnp.where(index >= 0, gates[source, 0, there], 0.0)
+            stage[i] = (ys[sets[r], there].astype(F32) * gate).astype(BF)
+            return carry
+
+        lax.fori_loop(0, sents, give, 0, unroll=8)
+        if r % 2 == 0:
+            outputs_here[r].start()
+        else:
+            outputs_back[r].start()
+
+    def before_backward(r):
+        if r == 1:
             loads[4].wait()
         if r == 2:
-            loads[5].wait()
-            loads[6].wait()
-            arrive(0, 1)
-            forward(5, 6)
-            arrive(3)
-            forward(7)
-            arrive(4)
-            forward(8)
+            to_c[3].wait_recv()
+            to_c[7].start()
+            to_c[4].wait_recv()
+            to_c[8].start()
         if r == 3:
-            arrive(7)
+            to_c[7].wait_recv()
         if r == 5:
-            arrive(8)
+            to_c[8].wait_recv()
         if r == 6:
-            arrive(5, 6)
-            forward(9)
+            to_c[5].wait_recv()
+            to_c[6].wait_recv()
+            to_c[9].start()
         if r == 7:
-            arrive(9)
+            to_c[9].wait_recv()
         source = plane_peer(r)
 
         def fetch(j, carry):
             index = tab[source, 0, j]
             length = tab[source, 0, cap + j]
             gate = gates[source, 0, j]
-            xs[j] = held_m[r][index]
             gt = jnp.where(place < length, held_c[r][index].astype(F32), 0.0)
-            gs[j] = gt.astype(BF)
-            dys[j] = (gt * gate).astype(BF)
-            return carry
-
-        lax.fori_loop(0, cap, fetch, 0, unroll=2)
-
-    def after(r):
-        source = plane_peer(r)
-        if r >= 2 and r % 2 == 0:
-            pltpu.make_async_copy(stage.at[0], py_o.at[r // 2 - 1], local.at[0]).wait()
-        if r >= 2 and r % 2 == 1:
-            outputs_back[r - 2].wait_send()
-
-        def give(i, carry):
-            index = tab[source, 0, 2 * cap + i]
-            there = jnp.maximum(index, 0)
-            gate = gates[source, 0, there]
-            hit = (index >= 0).astype(F32)
-            parts[r][i] = (dms[there].astype(F32) * hit).astype(BF)
-            stage[r % 2, i] = (ys[there].astype(F32) * (hit * gate)).astype(BF)
-            return carry
-
-        lax.fori_loop(0, sents, give, 0, unroll=2)
-        if r % 2 == 0:
-            pltpu.make_async_copy(stage.at[0], py_o.at[r // 2], local.at[0]).start()
-        else:
-            outputs_back[r].start()
-
-        def dots(j, carry):
-            product = ys[j].astype(F32) * gs[j].astype(F32)
+            dys[sets[r], j] = (gt * gate).astype(BF)
+            product = ys[sets[r], j].astype(F32) * gt
             total = jnp.sum(jnp.sum(product, axis=0, keepdims=True), axis=1, keepdims=True)
             if r == 0:
                 dg_o[me, pl.ds(j, 1)] = jnp.broadcast_to(total, (1, 128))
@@ -577,66 +610,136 @@
                 dg_s[r, pl.ds(j, 1)] = jnp.broadcast_to(total, (1, 128))
             return carry
 
-        lax.fori_loop(0, cap, dots, 0, unroll=4)
+        lax.fori_loop(0, cap, fetch, 0, unroll=True)
         if r > 0:
             gates_back[r].start()
+
+    def after_backward(r):
+        source = plane_peer(r)
+        if r == 2:
+            for copy in to_m[0:5]:
+                copy.wait_send()
+        if r == 4:
+            for copy in to_c[3:5]:
+                copy.wait_send()
+        if r == 6:
+            to_c[9].wait_send()
+
+        def give(i, carry):
+            index = tab[source, 0, 2 * cap + i]
+            kept = dms[jnp.maximum(index, 0)]
+            parts[r][i] = jnp.where(index >= 0, kept, jnp.zeros_like(kept))
+            return carry
+
+        lax.fori_loop(0, sents, give, 0, unroll=8)
         if r % 2 == 1:
+            pl.semaphore_wait(free.at[r // 2], 1)
             back[r // 2].start()
         if r == 4:
-            back[1].wait_recv()
-            add_into(parts[2], 0, cores[2], sents)
+            join(2)
             back[4].start()
-        if r == 6:
-            back[2].wait_recv()
-            add_into(parts[4], 0, cores[4], sents)
+
+    def join(r):
+        back[r // 2].wait_recv()
+        add_into(parts[r], 0, cores[r], sents)
+
+    def after_back_grad(r):
+        if r == 2:
+            join(4)
             back[6].start()
-        if r == 7:
-            back[3].wait_recv()
-            add_into(parts[6], 0, cores[6], sents)
-            back[5].start()
-            back[7].start()
-            back[0].wait_recv()
-            add_into(parts[0], 0, cores[0], sents)
-
-    def chunk(t, carry):
-        for r in range(8):
-            pl.when(t == r)(functools.partial(before, r))
-        x = xs[...].reshape(cap * slot, width)
-        dy = dys[...].reshape(cap * slot, width)
-
-        def inner(f, carry):
-            cols = pl.ds(pl.multiple_of(f * tile, tile), tile)
+
+    def after_in_grad(r):
+        if r == 2:
+            join(0)
+
+    tiles = [slice(f * tile, (f + 1) * tile) for f in range(hidden // tile)]
+
+    def forward(spot):
+        x = xs[spot].reshape(rows, width)
+        here = pl.ds(pl.multiple_of(spot * rows, rows), rows)
+        for cols in tiles:
             u = mm(x, win[:, cols])
             square = u * u
             th = jnp.tanh(u * (GELU_A + GELU_A * GELU_B * square))
             cdf = 0.5 + 0.5 * th
             slope = cdf + (0.5 * u) * (1.0 - th * th) * (GELU_A + 3 * GELU_A * GELU_B * square)
-            z = (u * cdf).astype(BF)
-            zs[:, cols] = z
+            zs[here, cols] = (u * cdf).astype(BF)
+            dus[here, cols] = slope.astype(BF)
+        ys[spot] = mm(zs[here, :], wback[...]).astype(BF).reshape(cap, slot, width)
+
+    def backward(spot):
+        dy = dys[spot].reshape(rows, width)
+        here = pl.ds(pl.multiple_of(spot * rows, rows), rows)
+        for cols in tiles:
             dz = mm(dy, wback[cols, :], 1, 1)
-            du = (dz * slope).astype(BF)
-            dus[:, cols] = du
-            accb[cols, :] += mm(z, dy, 0, 0)
-            acci[:, cols] += mm(x, du, 0, 0)
-            return carry
-
-        lax.fori_loop(0, hidden // tile, inner, 0)
-        ys[...] = mm(zs[...], wback[...]).astype(BF).reshape(cap, slot, width)
-        dms[...] = mm(dus[...], win[...], 1, 1).astype(BF).reshape(cap, slot, width)
-        for r in range(8):
-            pl.when(t == r)(functools.partial(after, r))
+            dus[here, cols] = (dz * dus[here, cols].astype(F32)).astype(BF)
+        dms[...] = mm(dus[here, :], win[...], 1, 1).astype(BF).reshape(cap, slot, width)
+
+    def back_grad(count):
+        dy = dys[0:count].reshape(count * rows, width)
+        for cols in tiles:
+            yield cols, mm(zs[0 : count * rows, cols], dy, 0, 0)
+
+    def in_grad(count):
+        x = xs[0:count].reshape(count * rows, width)
+        for cols in tiles:
+            yield cols, mm(x, dus[0 : count * rows, cols], 0, 0)
+
+    def back_pair(spot):
+        for cols, total in back_grad(2):
+            accb[cols, :] += total
+
+    def in_pair(spot):
+        for cols, total in in_grad(2):
+            acci[:, cols] += total
+
+    steps = expert_steps()
+    actions = {
+        "F": (before_forward, forward, after_forward),
+        "B": (before_backward, backward, after_backward),
+        "U": (None, back_pair, after_back_grad),
+        "V": (None, in_pair, after_in_grad),
+    }
+
+    def spot_of(t, kind):
+        spot = jnp.int32(0)
+        for number, (other, r) in enumerate(steps):
+            if other == kind and sets[r]:
+                spot = spot + jnp.where(t == number, sets[r], 0)
+        return spot
+
+    def step(t, carry):
+        for kind, (pre, work, post) in actions.items():
+            mine = [number for number, (other, _) in enumerate(steps) if other == kind]
+            spans = [n for n in mine if n - 1 not in mine]
+            ends = [n for n in mine if n + 1 not in mine]
+            inside = functools.reduce(
+                jnp.logical_or,
+                [jnp.logical_and(t >= a, t <= b) for a, b in zip(spans, ends)],
+            )
+
+            @pl.when(inside)
+            def _():
+                if pre is not None:
+                    for number in mine:
+                        pl.when(t == number)(functools.partial(pre, steps[number][1]))
+                work(spot_of(t, kind))
+                for number in mine:
+                    pl.when(t == number)(functools.partial(post, steps[number][1]))
+
         return carry
 
-    lax.fori_loop(0, 8, chunk, 0)
-    win[...] = acci[...].astype(BF)
-    wback[...] = accb[...].astype(BF)
-    for right in (True, False):
-
-        @pl.when(z == (0 if right else depth - 1))
-        def _():
-            for array in (0, 1):
-                line_first(right, array)[1].start()
-
+    lax.fori_loop(0, len(steps), step, 0)
+    for cols, total in back_grad(4):
+        wback[cols, :] = (accb[cols, :] + total).astype(BF)
+        if cols.start == 0:
+            join(6)
+            back[5].start()
+            back[7].start()
+    line_open(1)
+    for cols, total in in_grad(4):
+        win[:, cols] = (acci[:, cols] + total).astype(BF)
+    line_open(0)
     return_finish(parts, sides, back)
     kept = pltpu.make_async_copy(parts[0], dm_o, local.at[2])
     kept.start()
@@ -644,11 +747,11 @@
 
         @pl.when(z == (1 if right else depth - 2))
         def _():
-            for array in (0, 1):
+            for array in (1, 0):
                 here, copy = line_first(right, array)
                 copy.wait_recv()
                 source, into = ((win, line_in), (wback, line_back))[array]
-                total = source[here, :].astype(F32) + into[int(right)].astype(F32)
+                total = source[here, :].astype(F32) + into[...].astype(F32)
                 source[here, :] = total.astype(BF)
 
     stores = [
@@ -670,13 +773,12 @@
     for r in (1, 3, 5, 7):
         outputs_back[r].wait_recv()
     outputs_back[7].wait_send()
-    pltpu.make_async_copy(stage.at[0], py_o.at[3], local.at[0]).wait()
     for r in range(1, 8):
         gates_back[r].wait()
-    for index in range(10):
+    for index in range(5, 10):
         to_m[index].wait_send()
-        if index > 2:
-            to_c[index].wait_send()
+    for index in range(5, 9):
+        to_c[index].wait_send()
 
 
 def expert_exchange(tab, gates, m, cot, near, far, core, win, wback, cap, depth):
@@ -687,6 +789,7 @@
     anywhere = pl.BlockSpec(memory_space=pl.ANY)
     shape = jax.ShapeDtypeStruct
     cube = (sents, slot, width)
+    taken = (cap, slot, width)
     rows = cap * slot
     return pl.pallas_call(
         functools.partial(expert_kernel, cap, depth),
@@ -700,19 +803,21 @@
             shape((hidden, width), BF),
             shape((8, cap, 128), F32),
         ],
-        scratch_shapes=[VM(cube, BF)] * (16 + 8 + 4)
+        scratch_shapes=[VM(cube, BF)] * 16
         + [VM((sents // 2, slot, width), BF)] * 6
         + [VM((width, hidden), BF), VM((hidden, width), BF)]
-        + [VM((cap, slot, width), BF)] * 3
-        + [VM((rows, hidden), BF)] * 2
-        + [VM((cap, slot, width), BF)] * 2
-        + [VM((2,) + cube, BF), VM((8, cap, 128), F32)]
+        + [VM(cube, BF)]
+        + [VM((4,) + taken, BF)] * 2
+        + [VM((4 * rows, hidden), BF)] * 2
+        + [VM((4,) + taken, BF), VM(taken, BF), VM(cube, BF)]
+        + [VM((8, cap, 128), F32)]
         + [VM((hidden, width), F32), VM((width, hidden), F32)]
-        + [VM((2, width // depth, hidden), BF), VM((2, hidden // depth, width), BF)]
+        + [VM((width // depth, hidden), BF), VM((hidden // depth, width), BF)]
         + [
             pltpu.SemaphoreType.DMA((46,)),
             pltpu.SemaphoreType.DMA((46,)),
             pltpu.SemaphoreType.DMA((9,)),
+            pltpu.SemaphoreType.REGULAR((4,)),
         ],
         compiler_params=pltpu.CompilerParams(
             collective_id=1, has_side_effects=True, vmem_limit_bytes=63 * 2**20
@@ -974,7 +1079,7 @@
         def _():
             line_piece(s, array, False, False).start()
 
-    def line_service(t, ahead=1):
+    def line_service(t, ahead=0):
         for right in (True, False):
             every = pieces(right)
             edge = 0 if right else depth - 1
@@ -1659,6 +1764,6 @@
     )
     plane = dict(mesh.shape)["expert"]
     depth = dict(mesh.shape)["dp"]
-    cube = plane == 2 * 2 * 2 and depth > 2
+    cube = plane == 2 * 2 * 2 and depth > 3
     body = functools.partial(local_plane, depth) if cube else local
     return jax.shard_map(body, mesh=mesh, in_specs=in_specs, out_specs=out_specs, check_vma=False)

time: 235 us -> 219 us (0.932)
  Pallas kernels: 234 us -> 218 us
    pallas_call x1, Pallas kernels: 128 us -> 112 us  [expert_exchange(): pl.pallas_call(functools.partial(expert_kernel, cap, depth), in_specs=[sm...]
where the time goes in v6:
time: 219 us
  Pallas kernels  218 us (100%)
    pallas_call x1, Pallas kernels, expert_exchange(): pl.pallas_call(functools.partial(expert_kernel, cap, depth), in_specs=[sm...  112 us
    pallas_call x1, Pallas kernels, backward_exchange(): pl.pallas_call(functools.partial(backward_kernel, heads, depth), in_specs...  77 us
    pallas_call x1, Pallas kernels, attention_forward(): pl.pallas_call(functools.partial(attention_forward_kernel, heads, cap), g...  21.5 us
    pallas_call x1, Pallas kernels, place_outputs(): pl.pallas_call(outputs_kernel, in_specs=[anywhere] * 8 + [vm], out_specs=...  7.15 us

profile of v6, /device:TPU:0, one launch (start us, length us, event | category | flops | bytes accessed | tf_op | source)
XLA Modules:
  0.0 218.7 jit_solution(3043268833004650393)
XLA Ops:
  0.6 21.5 %shard_map.263 = (bf16[1024,512]{1,0:T(8,128)(2,1)}, bf16[1024,512]{1,0:T(8,128)(2,1)}, bf16[1024,512]{1,0:T(8,128)(2,1)}, bf16[1024,512]{1,0:T(8,128)(2,1)}, bf...) custom-call(s32[16]{0:T(128)} %len_ref.3, ...), custom_call_target="tpu_custom_call" | custom-call | flops 2281701376 | bytes 8388608 | tf_op jit(solution)/shard_map/pallas_call | solution.py:237
  22.1 112.3 %shard_map.264 = (bf16[16,64,512]{2,1,0:T(8,128)(2,1)}, bf16[4,16,64,512]{3,2,1,0:T(8,128)(2,1)}, bf16[4,16,64,512]{3,2,1,0:T(8,128)(2,1)}, bf16[512,2048]{1,0:T...) custom-call(s32[8,8,128]{2,1,0:T(8,128)} %get-tuple-element.60.tab, f32[8,8,128]{2,1,0:T(8,128)} %get-tuple-element.61.gates, ...), custom_call_target="tpu_custom_call" | custom-call | flops 51539607552 | bytes 41943040 | tf_op jit(solution)/shard_map/pallas_call | solution.py:794
  134.4 77.0 %shard_map.265 = (bf16[16,64,512]{2,1,0:T(8,128)(2,1)}, bf16[16,64,512]{2,1,0:T(8,128)(2,1)}, bf16[512,512]{1,0:T(8,128)(2,1)}, bf16[512,512]{1,0:T(8,128)(2,1)}...) custom-call(s32[16]{0:T(128)} %len_ref.3, ...), custom_call_target="tpu_custom_call" | custom-call | flops 4294967296 | bytes 41943040 | tf_op jit(solution)/shard_map/pallas_call | solution.py:1359
  211.4 7.1 %shard_map.266 = (bf16[16,64,512]{2,1,0:T(8,128)(2,1)}, bf16[16,64,512]{2,1,0:T(8,128)(2,1)}, f32[128,2048]{1,0:T(8,128)}, f32[512,512]{1,0:T(8,128)}, f32[512,5...) custom-call(bf16[16,64,512]{2,1,0:T(8,128)(2,1)} %get-tuple-element., ...), custom_call_target="tpu_custom_call" | custom-call | tf_op jit(solution)/shard_map/pallas_call | solution.py:1448

commit v7 on v6

--- a/solution.py
+++ b/solution.py
@@ -127,7 +127,7 @@
 
 
 def attention_forward_kernel(
-    heads, cap, len_ref, x_ref, wq, wk, wv, wo, g1, b1, g2, b2, tasks, lengths, routes,
+    heads, cap, steps, len_ref, x_ref, wq, wk, wv, wo, g1, b1, g2, b2, tasks, lengths, routes,
     gate_table, cot_in,
     act_o, q_o, k_o, v_o, ctx_o, p_o, h_o, m_o, st_o, plan_o, tab_o, gates_o, near_o, far_o,
     core_o, cot, tab_s, gates_s, sends, recvs, local,
@@ -142,9 +142,10 @@
     experts = gate_table.shape[0]
     me = lax.axis_index("expert")
     half = cot.shape[0] // 2
+    early = near_o.shape[0]
     copies = [
-        remote(cot.at[pl.ds(0, half)], near_o, sends, recvs, 0, NEAR),
-        remote(cot.at[pl.ds(half, half)], far_o, sends, recvs, 1, FAR),
+        remote(cot.at[pl.ds(0, early)], near_o, sends, recvs, 0, NEAR),
+        remote(cot.at[pl.ds(half, early)], far_o, sends, recvs, 1, FAR),
         remote(cot, core_o, sends, recvs, 2, CORE),
     ]
     for relation in range(1, 8):
@@ -153,6 +154,7 @@
             remote(tab_s.at[there], tab_o.at[me], sends, recvs, 1 + 2 * relation, relation),
             remote(gates_s.at[there], gates_o.at[me], sends, recvs, 2 + 2 * relation, relation),
         ]
+    load = pltpu.make_async_copy(cot_in, cot, local.at[2])
     own = [
         pltpu.make_async_copy(tab_s.at[me], tab_o.at[me], local.at[0]),
         pltpu.make_async_copy(gates_s.at[me], gates_o.at[me], local.at[1]),
@@ -160,26 +162,25 @@
 
     @pl.when(step == 0)
     def _():
-        load = pltpu.make_async_copy(cot_in, cot, local.at[2])
         load.start()
-        plane_barrier()
-        load.wait()
-        for copy in copies[0:3]:
-            copy.start()
+        greet()
         table, gates, hit, place, gate = route_tables(
             cap, tasks[...], lengths[...], routes[...], gate_table[...]
         )
         for e in range(experts):
             tab_s[e] = jnp.broadcast_to(table[e : e + 1], (8, 128))
             gates_s[e] = jnp.broadcast_to(gates[e : e + 1], (8, 128))
-        for copy in copies[3:]:
-            copy.start()
-        for copy in own:
-            copy.start()
         plan_o[0:experts] = hit
         plan_o[experts : 2 * experts] = place
         plan_o[2 * experts : 3 * experts] = gate
         st_o[...] = jnp.zeros_like(st_o)
+
+    @pl.when(step == min(1, steps - 1))
+    def _():
+        await_greetings()
+        load.wait()
+        for copy in copies + own:
+            copy.start()
 
     x = x_ref[...].astype(F32).reshape(count * slot, width)
     normed, _ = normalize(x)
@@ -233,9 +234,9 @@
     anywhere = pl.BlockSpec(memory_space=pl.ANY)
     shape = jax.ShapeDtypeStruct
     total = sents * slot
-    half = (sents // 2, slot, width)
+    early = (sents // 4, slot, width)
     return pl.pallas_call(
-        functools.partial(attention_forward_kernel, heads, cap),
+        functools.partial(attention_forward_kernel, heads, cap, sents // count),
         grid=(sents // count,),
         in_specs=[pl.BlockSpec(memory_space=pltpu.SMEM), cube]
         + [whole(width, width)] * 4
@@ -254,8 +255,8 @@
             shape((3 * experts, sents), F32),
             shape((experts, 8, 128), jnp.int32),
             shape((experts, 8, 128), F32),
-            shape(half, BF),
-            shape(half, BF),
+            shape(early, BF),
+            shape(early, BF),
             shape(tokens.shape, BF),
         ],
         scratch_shapes=[
@@ -343,22 +344,26 @@
     )
 
 
-def plane_barrier(depth=1):
+def greet(depth=1):
     barrier = pltpu.get_barrier_semaphore()
     targets = [(lax.axis_index("dp"), plane_peer(relation)) for relation in range(1, 8)]
     for offset in range(1, depth):
         targets.append((line_peer(offset, depth), lax.axis_index("expert")))
     for target in targets:
         pl.semaphore_signal(barrier, inc=1, device_id=target, device_id_type=MESH_ID)
-    pl.semaphore_wait(barrier, len(targets))
-
-
-def gather_copies(own, held, sends, recvs, base):
+
+
+def await_greetings(depth=1):
+    pl.semaphore_wait(pltpu.get_barrier_semaphore(), 6 + depth)
+
+
+def gather_copies(own, held, sends, recvs, base, early=0):
     half = own.shape[0] // 2
     low, high = pl.ds(0, half), pl.ds(half, half)
+    near, far = pl.ds(early, half - early), pl.ds(half + early, half - early)
     plan = [
-        (own.at[low], held[2].at[low], NEAR),
-        (own.at[high], held[4].at[high], FAR),
+        (own.at[near], held[2].at[near], NEAR),
+        (own.at[far], held[4].at[far], FAR),
         (own, held[1], CORE),
         (own.at[high], held[2].at[high], NEAR),
         (own.at[low], held[4].at[low], FAR),
@@ -459,6 +464,7 @@
     z = lax.axis_index("dp")
     tile = min(512, hidden)
     rows = cap * slot
+    early = near_in.shape[0]
     low, high = pl.ds(0, half), pl.ds(half, half)
     loads = [
         pltpu.make_async_copy(src, dst, local.at[2 + place])
@@ -469,16 +475,16 @@
                 (win_in, win),
                 (wback_in, wback),
                 (core_in, held_c[1]),
-                (near_in, held_c[2].at[low]),
-                (far_in, held_c[4].at[high]),
+                (near_in, held_c[2].at[pl.ds(0, early)]),
+                (far_in, held_c[4].at[pl.ds(half, early)]),
             ]
         )
     ]
     for load in loads:
         load.start()
-    plane_barrier(depth)
+    greet(depth)
     to_m = gather_copies(held_m[0], held_m, sends, recvs, 0)
-    to_c = gather_copies(held_c[0], held_c, sends, recvs, 10)
+    to_c = gather_copies(held_c[0], held_c, sends, recvs, 10, early)
     back = return_copies(parts, cores, sides, sends, recvs, 20)
     gates_back = {
         r: remote(dg_s.at[r], dg_o.at[me], sends, recvs, 30 + r, r) for r in range(1, 8)
@@ -506,14 +512,15 @@
             def _():
                 line_first(right, array)[1].start()
 
+    accb[...] = jnp.zeros_like(accb)
+    acci[...] = jnp.zeros_like(acci)
     for load in loads[0:2]:
         load.wait()
+    await_greetings(depth)
     for index in (0, 1, 2, 3, 4):
         to_m[index].start()
-    for index in (3, 4):
+    for index in (0, 1, 3, 4):
         to_c[index].start()
-    accb[...] = jnp.zeros_like(accb)
-    acci[...] = jnp.zeros_like(acci)
     place = lax.broadcasted_iota(jnp.int32, (slot, width), 0)
     for load in loads[2:4]:
         load.wait()
@@ -526,16 +533,19 @@
             to_m[5].start()
             to_m[1].wait_recv()
             to_m[6].start()
-            for load in loads[5:7]:
-                load.wait()
-            to_c[5].start()
-            to_c[6].start()
             to_m[3].wait_recv()
             to_m[7].start()
             to_m[4].wait_recv()
             to_m[8].start()
         if r == 3:
             to_m[7].wait_recv()
+        if r == 4:
+            for load in loads[5:7]:
+                load.wait()
+            to_c[0].wait_recv()
+            to_c[5].start()
+            to_c[1].wait_recv()
+            to_c[6].start()
         if r == 5:
             to_m[8].wait_recv()
         if r == 6:
@@ -620,7 +630,7 @@
             for copy in to_m[0:5]:
                 copy.wait_send()
         if r == 4:
-            for copy in to_c[3:5]:
+            for copy in to_c[0:2] + to_c[3:5]:
                 copy.wait_send()
         if r == 6:
             to_c[9].wait_send()
@@ -1036,7 +1046,8 @@
     begin(gin_s, gback_s, h_ref, dm_ref, cot_ref, wo, parts[6], cores[6], ctx)
     begin(parts[2], cores[2], parts[4], cores[4], q, k, v, p_ref, act, parts[0], cores[0])
     begin(wq, wk, wv, x_ref)
-    plane_barrier(depth)
+    greet(depth)
+    await_greetings(depth)
 
     all_parts = {r: parts[r - r % 2] for r in range(8)}
     back = return_copies(all_parts, cores, sides, sends, recvs, 0)

time: 219 us -> 215 us (0.982)
  Pallas kernels: 218 us -> 214 us
    pallas_call x1, Pallas kernels: 21.5 us -> 17.6 us  [attention_forward(): pl.pallas_call(functools.partial(attention_forward_kernel, heads, cap, se...]
where the time goes in v7:
time: 215 us; the launch traced here: 214 us
  Pallas kernels  214 us (100%)
    pallas_call x1, Pallas kernels, expert_exchange(): pl.pallas_call(functools.partial(expert_kernel, cap, depth), in_specs=[sm...  112 us
    pallas_call x1, Pallas kernels, backward_exchange(): pl.pallas_call(functools.partial(backward_kernel, heads, depth), in_specs...  77 us
    pallas_call x1, Pallas kernels, attention_forward(): pl.pallas_call(functools.partial(attention_forward_kernel, heads, cap, se...  17.6 us
    pallas_call x1, Pallas kernels, place_outputs(): pl.pallas_call(outputs_kernel, in_specs=[anywhere] * 8 + [vm], out_specs=...  7.15 us

profile of v7, /device:TPU:0, one launch (start us, length us, event | category | flops | bytes accessed | tf_op | source)
XLA Modules:
  0.0 214.4 jit_solution(3459928820605222029)
XLA Ops:
  0.6 17.6 %shard_map.263 = (bf16[1024,512]{1,0:T(8,128)(2,1)}, bf16[1024,512]{1,0:T(8,128)(2,1)}, bf16[1024,512]{1,0:T(8,128)(2,1)}, bf16[1024,512]{1,0:T(8,128)(2,1)}, bf...) custom-call(s32[16]{0:T(128)} %len_ref.3, ...), custom_call_target="tpu_custom_call" | custom-call | flops 2281701376 | bytes 8388608 | tf_op jit(solution)/shard_map/pallas_call | solution.py:238
  18.3 111.8 %shard_map.264 = (bf16[16,64,512]{2,1,0:T(8,128)(2,1)}, bf16[4,16,64,512]{3,2,1,0:T(8,128)(2,1)}, bf16[4,16,64,512]{3,2,1,0:T(8,128)(2,1)}, bf16[512,2048]{1,0:T...) custom-call(s32[8,8,128]{2,1,0:T(8,128)} %get-tuple-element.60.tab, f32[8,8,128]{2,1,0:T(8,128)} %get-tuple-element.61.gates, ...), custom_call_target="tpu_custom_call" | custom-call | flops 51539607552 | bytes 41943040 | tf_op jit(solution)/shard_map/pallas_call | solution.py:804
  130.0 77.0 %shard_map.265 = (bf16[16,64,512]{2,1,0:T(8,128)(2,1)}, bf16[16,64,512]{2,1,0:T(8,128)(2,1)}, bf16[512,512]{1,0:T(8,128)(2,1)}, bf16[512,512]{1,0:T(8,128)(2,1)}...) custom-call(s32[16]{0:T(128)} %len_ref.3, ...), custom_call_target="tpu_custom_call" | custom-call | flops 4294967296 | bytes 41943040 | tf_op jit(solution)/shard_map/pallas_call | solution.py:1370
  207.0 7.1 %shard_map.266 = (bf16[16,64,512]{2,1,0:T(8,128)(2,1)}, bf16[16,64,512]{2,1,0:T(8,128)(2,1)}, f32[128,2048]{1,0:T(8,128)}, f32[512,512]{1,0:T(8,128)}, f32[512,5...) custom-call(bf16[16,64,512]{2,1,0:T(8,128)(2,1)} %get-tuple-element., ...), custom_call_target="tpu_custom_call" | custom-call | tf_op jit(solution)/shard_map/pallas_call | solution.py:1459

commit v8 on v7

--- a/solution.py
+++ b/solution.py
@@ -410,16 +410,16 @@
 
 def return_finish(parts, sides, back):
     half = parts[0].shape[0] // 2
-    back[4].wait_recv()
-    add_into(parts[0], 0, sides[0], half)
     back[5].wait_recv()
     add_into(parts[4], 0, sides[1], half)
     back[8].start()
-    back[6].wait_recv()
-    add_into(parts[0], half, sides[2], half)
     back[7].wait_recv()
     add_into(parts[2], half, sides[3], half)
     back[9].start()
+    back[4].wait_recv()
+    add_into(parts[0], 0, sides[0], half)
+    back[6].wait_recv()
+    add_into(parts[0], half, sides[2], half)
     back[8].wait_recv()
     add_into(parts[0], 0, sides[4], half)
     back[9].wait_recv()
@@ -750,28 +750,36 @@
     for cols, total in in_grad(4):
         win[:, cols] = (acci[:, cols] + total).astype(BF)
     line_open(0)
+    stores = [
+        pltpu.make_async_copy(win, gin_o, local.at[4]),
+        pltpu.make_async_copy(wback, gback_o, local.at[5]),
+    ]
+    for store in stores:
+        store.start()
     return_finish(parts, sides, back)
     kept = pltpu.make_async_copy(parts[0], dm_o, local.at[2])
     kept.start()
+    for store in stores:
+        store.wait()
     for right in (True, False):
 
         @pl.when(z == (1 if right else depth - 2))
         def _():
+            again = []
             for array in (1, 0):
                 here, copy = line_first(right, array)
                 copy.wait_recv()
                 source, into = ((win, line_in), (wback, line_back))[array]
                 total = source[here, :].astype(F32) + into[...].astype(F32)
                 source[here, :] = total.astype(BF)
-
-    stores = [
-        pltpu.make_async_copy(win, gin_o, local.at[4]),
-        pltpu.make_async_copy(wback, gback_o, local.at[5]),
-    ]
-    for store in stores:
-        store.start()
-    for store in stores:
-        store.wait()
+                output = (gin_o, gback_o)[array]
+                again.append(
+                    pltpu.make_async_copy(source.at[here], output.at[here], local.at[6 + array])
+                )
+                again[-1].start()
+            for store in again:
+                store.wait()
+
     kept.wait()
     for right in (True, False):
 
@@ -994,7 +1002,7 @@
     heads, depth, len_ref, g1, g2, attn_sum, plan, tasks, lengths, dots,
     x_in, cot_in, dm_in, h_in, act_in, q_in, k_in, v_in, ctx_in, p_in,
     wq_in, wk_in, wv_in, wo_in, py, cy, gin, gback,
-    ig_o, out_o, gq_o, gk_o, gv_o, go_o, gin_o, gback_o, small_o, *scratch
+    ig_out, out_out, gq_o, gk_o, gv_o, go_o, gin_o, gback_o, small_o, *scratch
 ):
     inputs = (
         x_in, cot_in, dm_in, h_in, act_in, q_in, k_in, v_in, ctx_in, p_in,
@@ -1011,7 +1019,7 @@
     red = scratch[36:57]
     line_in, line_back, extra_in, extra_back = scratch[57:61]
     small, small_core, small_plane, small_line = scratch[61:65]
-    sends, recvs, local = scratch[65:]
+    ig_o, out_o, sends, recvs, local = scratch[65:]
     sems = (sends, recvs)
     sents, slot, width = x_ref.shape
     head = width // heads
@@ -1276,21 +1284,26 @@
     ready(q, k, v, p_ref, act)
     pull(0, red_0)
     red_o.send_plane()
-    back[4].start()
-    back[6].start()
     line_service(1)
     back[5].wait_recv()
     add_into(parts[4], 0, sides[1], half)
+    back[8].start()
     back[7].wait_recv()
     add_into(parts[2], half, sides[3], half)
+    back[9].start()
     pull(1, red_1)
     red_0.send_plane()
-    back[8].start()
-    back[9].start()
+    back[4].start()
+    back[6].start()
     red_o.send_line()
     line_service(2)
     ready(wq, wk, wv, x_ref)
     lax.fori_loop(0, sents // count, last, 0)
+    leaving = [
+        pltpu.make_async_copy(ig_o, ig_out, local.at[24]),
+        pltpu.make_async_copy(out_o, out_out, local.at[25]),
+    ]
+    leaving[0].start()
     red_1.send_plane()
     red_o.send_back_line()
     gate_gradient()
@@ -1308,6 +1321,7 @@
     outcome(0, sides[4])
     back[9].wait_recv()
     outcome(half, sides[5])
+    leaving[1].start()
     sums.send_core()
     red_o.send_back_core()
     red_0.send_back_plane()
@@ -1317,21 +1331,26 @@
     red_0.send_back_core()
     sums.send_line()
     red_1.send_back_core()
+    def leave(source, output):
+        copy = pltpu.make_async_copy(source, output, local.at[26 + len(leaving)])
+        copy.start()
+        leaving.append(copy)
+
+    def share(red, low):
+        cols = pl.ds(low, red.final.shape[1])
+        for place, ref in enumerate((gq_o, gk_o, gv_o)):
+            leave(red.final.at[pl.ds(place * width, width)], ref.at[:, cols])
+
     red_o.finish()
-    go_o[...] = red_o.final[...]
+    leave(red_o.final, go_o)
     red_0.finish()
-
-    def share(red, low):
-        for place, ref in enumerate((gq_o, gk_o, gv_o)):
-            ref[:, low : low + red.final.shape[1]] = red.final[
-                place * width : (place + 1) * width, :
-            ]
-
     share(red_0, 0)
     sums.finish(small_o)
     red_1.finish()
     share(red_1, span)
     line_end()
+    for copy in leaving:
+        copy.wait()
     for copy in back[4:]:
         copy.wait_send()
 
@@ -1370,7 +1389,7 @@
     return pl.pallas_call(
         functools.partial(backward_kernel, heads, depth),
         in_specs=[pl.BlockSpec(memory_space=pltpu.SMEM)] + [vm] * 7 + [anywhere] * len(large),
-        out_specs=[vm] * 9,
+        out_specs=[anywhere] * 6 + [vm] * 3,
         out_shape=[shape(cube, BF), shape(cube, BF)]
         + [shape((width, width), BF)] * 4
         + [shape(in_share, F32), shape(back_share, F32), shape(small.shape, F32)],
@@ -1384,10 +1403,11 @@
         + [VM(in_share, BF), VM(back_share, BF)]
         + [VM(small.shape, F32)] * 2
         + [VM((4,) + small.shape, F32), VM((depth,) + small.shape, F32)]
+        + [VM(cube, BF)] * 2
         + [
             pltpu.SemaphoreType.DMA((semaphores,)),
             pltpu.SemaphoreType.DMA((semaphores,)),
-            pltpu.SemaphoreType.DMA((24,)),
+            pltpu.SemaphoreType.DMA((35,)),
         ],
         compiler_params=pltpu.CompilerParams(
             collective_id=2, has_side_effects=True, vmem_limit_bytes=63 * 2**20
@@ -1442,7 +1462,7 @@
         fetches[place].wait()
         wide[place] = low[place].astype(F32)
         stores[place].start()
-    for enter, leave in moves:
+        enter, leave = moves[place]
         enter.wait()
         leave.start()
     for store in stores:

time: 215 us -> 212 us (0.986)
  Pallas kernels: 214 us -> 211 us
where the time goes in v8:
time: 212 us
  Pallas kernels  211 us (100%)
    pallas_call x1, Pallas kernels, expert_exchange(): pl.pallas_call(functools.partial(expert_kernel, cap, depth), in_specs=[sm...  110 us
    pallas_call x1, Pallas kernels, backward_exchange(): pl.pallas_call(functools.partial(backward_kernel, heads, depth), in_specs...  76.5 us
    pallas_call x1, Pallas kernels, attention_forward(): pl.pallas_call(functools.partial(attention_forward_kernel, heads, cap, se...  17.6 us
    pallas_call x1, Pallas kernels, place_outputs(): pl.pallas_call(outputs_kernel, in_specs=[anywhere] * 8 + [vm], out_specs=...  6.63 us

profile of v8, /device:TPU:0, one launch (start us, length us, event | category | flops | bytes accessed | tf_op | source)
XLA Modules:
  0.0 212.0 jit_solution(6348974758755166938)
XLA Ops:
  0.6 17.6 %shard_map.263 = (bf16[1024,512]{1,0:T(8,128)(2,1)}, bf16[1024,512]{1,0:T(8,128)(2,1)}, bf16[1024,512]{1,0:T(8,128)(2,1)}, bf16[1024,512]{1,0:T(8,128)(2,1)}, bf...) custom-call(s32[16]{0:T(128)} %len_ref.3, ...), custom_call_target="tpu_custom_call" | custom-call | flops 2281701376 | bytes 8388608 | tf_op jit(solution)/shard_map/pallas_call | solution.py:238
  18.3 110.4 %shard_map.264 = (bf16[16,64,512]{2,1,0:T(8,128)(2,1)}, bf16[4,16,64,512]{3,2,1,0:T(8,128)(2,1)}, bf16[4,16,64,512]{3,2,1,0:T(8,128)(2,1)}, bf16[512,2048]{1,0:T...) custom-call(s32[8,8,128]{2,1,0:T(8,128)} %get-tuple-element.60.tab, f32[8,8,128]{2,1,0:T(8,128)} %get-tuple-element.61.gates, ...), custom_call_target="tpu_custom_call" | custom-call | flops 51539607552 | bytes 41943040 | tf_op jit(solution)/shard_map/pallas_call | solution.py:812
  128.7 76.5 %shard_map.265 = (bf16[16,64,512]{2,1,0:T(8,128)(2,1)}, bf16[16,64,512]{2,1,0:T(8,128)(2,1)}, bf16[512,512]{1,0:T(8,128)(2,1)}, bf16[512,512]{1,0:T(8,128)(2,1)}...) custom-call(s32[16]{0:T(128)} %len_ref.3, ...), custom_call_target="tpu_custom_call" | custom-call | flops 4294967296 | bytes 41943040 | tf_op jit(solution)/shard_map/pallas_call | solution.py:1389
  205.2 6.6 %shard_map.266 = (bf16[16,64,512]{2,1,0:T(8,128)(2,1)}, bf16[16,64,512]{2,1,0:T(8,128)(2,1)}, f32[128,2048]{1,0:T(8,128)}, f32[512,512]{1,0:T(8,128)}, f32[512,5...) custom-call(bf16[16,64,512]{2,1,0:T(8,128)(2,1)} %get-tuple-element., ...), custom_call_target="tpu_custom_call" | custom-call | tf_op jit(solution)/shard_map/pallas_call | solution.py:1479

commit v9 on v8

--- a/solution.py
+++ b/solution.py
@@ -408,23 +408,53 @@
     lax.fori_loop(0, count, one, 0, unroll=8)
 
 
-def return_finish(parts, sides, back):
+def split_copies(parts, sides, sends, recvs, base):
     half = parts[0].shape[0] // 2
-    back[5].wait_recv()
-    add_into(parts[4], 0, sides[1], half)
-    back[8].start()
-    back[7].wait_recv()
-    add_into(parts[2], half, sides[3], half)
-    back[9].start()
+    piece = half // 2
+    hops = []
+    for number, (source, first, side, relation) in enumerate(
+        [
+            (parts[6], 0, sides[1], NEAR),
+            (parts[6], half, sides[3], FAR),
+            (parts[4], 0, sides[4], FAR),
+            (parts[2], half, sides[5], NEAR),
+        ]
+    ):
+        hops.append(
+            [
+                remote(
+                    source.at[pl.ds(first + q * piece, piece)],
+                    side.at[pl.ds(q * piece, piece)],
+                    sends, recvs, base + 2 * number + q, relation,
+                )
+                for q in range(2)
+            ]
+        )
+    return hops
+
+
+def return_finish(parts, sides, back, hops):
+    half = parts[0].shape[0] // 2
+    piece = half // 2
+    for q in range(2):
+        here = pl.ds(q * piece, piece)
+        hops[0][q].wait_recv()
+        add_into(parts[4], q * piece, sides[1].at[here], piece)
+        hops[2][q].start()
+        hops[1][q].wait_recv()
+        add_into(parts[2], half + q * piece, sides[3].at[here], piece)
+        hops[3][q].start()
     back[4].wait_recv()
     add_into(parts[0], 0, sides[0], half)
     back[6].wait_recv()
     add_into(parts[0], half, sides[2], half)
-    back[8].wait_recv()
-    add_into(parts[0], 0, sides[4], half)
-    back[9].wait_recv()
-    add_into(parts[0], half, sides[5], half)
-    for copy in back:
+    for q in range(2):
+        here = pl.ds(q * piece, piece)
+        hops[2][q].wait_recv()
+        add_into(parts[0], q * piece, sides[4].at[here], piece)
+        hops[3][q].wait_recv()
+        add_into(parts[0], half + q * piece, sides[5].at[here], piece)
+    for copy in back[0:4] + [back[4], back[6]] + [copy for pair in hops for copy in pair]:
         copy.wait_send()
 
 
@@ -486,6 +516,7 @@
     to_m = gather_copies(held_m[0], held_m, sends, recvs, 0)
     to_c = gather_copies(held_c[0], held_c, sends, recvs, 10, early)
     back = return_copies(parts, cores, sides, sends, recvs, 20)
+    hops = split_copies(parts, sides, sends, recvs, 46)
     gates_back = {
         r: remote(dg_s.at[r], dg_o.at[me], sends, recvs, 30 + r, r) for r in range(1, 8)
     }
@@ -744,8 +775,9 @@
         wback[cols, :] = (accb[cols, :] + total).astype(BF)
         if cols.start == 0:
             join(6)
-            back[5].start()
-            back[7].start()
+            for q in range(2):
+                hops[0][q].start()
+                hops[1][q].start()
     line_open(1)
     for cols, total in in_grad(4):
         win[:, cols] = (acci[:, cols] + total).astype(BF)
@@ -756,7 +788,7 @@
     ]
     for store in stores:
         store.start()
-    return_finish(parts, sides, back)
+    return_finish(parts, sides, back, hops)
     kept = pltpu.make_async_copy(parts[0], dm_o, local.at[2])
     kept.start()
     for store in stores:
@@ -832,8 +864,8 @@
         + [VM((hidden, width), F32), VM((width, hidden), F32)]
         + [VM((width // depth, hidden), BF), VM((hidden // depth, width), BF)]
         + [
-            pltpu.SemaphoreType.DMA((46,)),
-            pltpu.SemaphoreType.DMA((46,)),
+            pltpu.SemaphoreType.DMA((54,)),
+            pltpu.SemaphoreType.DMA((54,)),
             pltpu.SemaphoreType.DMA((9,)),
             pltpu.SemaphoreType.REGULAR((4,)),
         ],

time: 212 us -> 213 us (level)
  no operation moved by 1% of the time
where the time goes in v9:
time: 213 us; the launch traced here: 212 us
  Pallas kernels  212 us (100%)
    pallas_call x1, Pallas kernels, expert_exchange(): pl.pallas_call(functools.partial(expert_kernel, cap, depth), in_specs=[sm...  110 us
    pallas_call x1, Pallas kernels, backward_exchange(): pl.pallas_call(functools.partial(backward_kernel, heads, depth), in_specs...  77.5 us
    pallas_call x1, Pallas kernels, attention_forward(): pl.pallas_call(functools.partial(attention_forward_kernel, heads, cap, se...  17.6 us
    pallas_call x1, Pallas kernels, place_outputs(): pl.pallas_call(outputs_kernel, in_specs=[anywhere] * 8 + [vm], out_specs=...  6.63 us

profile of v9, /device:TPU:0, one launch (start us, length us, event | category | flops | bytes accessed | tf_op | source)
XLA Modules:
  0.0 212.4 jit_solution(14197064062798103881)
XLA Ops:
  0.6 17.6 %shard_map.263 = (bf16[1024,512]{1,0:T(8,128)(2,1)}, bf16[1024,512]{1,0:T(8,128)(2,1)}, bf16[1024,512]{1,0:T(8,128)(2,1)}, bf16[1024,512]{1,0:T(8,128)(2,1)}, bf...) custom-call(s32[16]{0:T(128)} %len_ref.3, ...), custom_call_target="tpu_custom_call" | custom-call | flops 2281701376 | bytes 8388608 | tf_op jit(solution)/shard_map/pallas_call | solution.py:238
  18.3 109.8 %shard_map.264 = (bf16[16,64,512]{2,1,0:T(8,128)(2,1)}, bf16[4,16,64,512]{3,2,1,0:T(8,128)(2,1)}, bf16[4,16,64,512]{3,2,1,0:T(8,128)(2,1)}, bf16[512,2048]{1,0:T...) custom-call(s32[8,8,128]{2,1,0:T(8,128)} %get-tuple-element.60.tab, f32[8,8,128]{2,1,0:T(8,128)} %get-tuple-element.61.gates, ...), custom_call_target="tpu_custom_call" | custom-call | flops 51539607552 | bytes 41943040 | tf_op jit(solution)/shard_map/pallas_call | solution.py:844
  128.1 77.5 %shard_map.265 = (bf16[16,64,512]{2,1,0:T(8,128)(2,1)}, bf16[16,64,512]{2,1,0:T(8,128)(2,1)}, bf16[512,512]{1,0:T(8,128)(2,1)}, bf16[512,512]{1,0:T(8,128)(2,1)}...) custom-call(s32[16]{0:T(128)} %len_ref.3, ...), custom_call_target="tpu_custom_call" | custom-call | flops 4294967296 | bytes 41943040 | tf_op jit(solution)/shard_map/pallas_call | solution.py:1421
  205.6 6.6 %shard_map.266 = (bf16[16,64,512]{2,1,0:T(8,128)(2,1)}, bf16[16,64,512]{2,1,0:T(8,128)(2,1)}, f32[128,2048]{1,0:T(8,128)}, f32[512,512]{1,0:T(8,128)}, f32[512,5...) custom-call(bf16[16,64,512]{2,1,0:T(8,128)(2,1)} %get-tuple-element., ...), custom_call_target="tpu_custom_call" | custom-call | tf_op jit(solution)/shard_map/pallas_call | solution.py:1511
